TPU v7x, 32 devices: a whole 2x2x4 slice. The times are simulated.
32 devices in a mesh: rep: 8 (over z, x), shard: 4 (over y, core).
Axes of the slice: x: 2, y: 2, z: 4, core: 2. Of those that a mesh axis runs over, the one named last changes fastest.
Arguments:
- hidden_in: bfloat16 [32768, 768], P(('rep', 'shard')), may hold values from -6 to 6
- enc_states: bfloat16 [32768, 768], P(('rep', 'shard')), may hold values from -6 to 6
- dec_segments: int32 [32768], P(('rep', 'shard')), may hold values from 0 to 1, as said below
- enc_segments: int32 [32768], P(('rep', 'shard')), may hold values from 0 to 1, as said below
- out_grad: bfloat16 [32768, 768], P(('rep', 'shard')), may hold values from -6 to 6
- gains: bfloat16 [3, 768], P(None, 'shard'), may hold values from 0.5 to 1.5
- rel_table: bfloat16 [32, 12], P('shard'), may hold values from -4 to 4
- self_qkv: bfloat16 [768, 2304], P('shard'), may hold values from -0.109375 to 0.109375
- self_out: bfloat16 [768, 768], P('shard'), may hold values from -2.5 to 2.5
- cross_q: bfloat16 [768, 768], P('shard'), may hold values from -0.109375 to 0.109375
- cross_kv: bfloat16 [768, 1536], P('shard'), may hold values from -0.109375 to 0.109375
- cross_out: bfloat16 [768, 768], P('shard'), may hold values from -2.5 to 2.5
- ff_in: bfloat16 [768, 4096], P('shard'), may hold values from -0.21875 to 0.21875
- ff_out: bfloat16 [2048, 768], P('shard'), may hold values from -0.1875 to 0.1875
Outputs:
- layer_out: bfloat16 [32768, 768], P(('rep', 'shard'))
- in_grad: float32 [32768, 768], P(('rep', 'shard'))
- enc_grad: float32 [32768, 768], P(('rep', 'shard'))
- gains_grad: float32 [3, 768], P(None, 'shard')
- rel_table_grad: float32 [32, 12], P('shard')
- self_qkv_grad: float32 [768, 2304], P('shard')
- self_out_grad: float32 [768, 768], P('shard')
- cross_query_gradient: float32 [768, 768], P('shard')
- cross_kv_grad: float32 [768, 1536], P('shard')
- cross_out_grad: float32 [768, 768], P('shard')
- ff_in_grad: float32 [768, 4096], P('shard')
- ff_out_grad: float32 [2048, 768], P('shard')
Inputs may be any that keep to these rules, and one draw needn't show every extreme that they name: `dec_segments`: in every decoder sequence of 512 tokens the positions before a cut, drawn for each sequence from 128 to 384, have number 0 and the rest number 1. `enc_segments`: in every encoder sequence of 512 states the positions before a cut, drawn for each sequence from 128 to 384, have number 0 and the rest number 1.
All inputs are finite; a program needn't handle non-finite values.
Results may differ from a plain program's by a relative error of at most 0.025.
The roundings to bfloat16 on the way count: a program that leaves them out, or rounds other values in their place, can miss the bound.
Values may be sent and summed in bfloat16 or wider, within the bound.
No kernel may reach another device: no remote copies, remote signals or barrier semaphores. Data moves between devices by JAX's collectives and lax.ppermute only.
A program may use at most 320 MiB of HBM per device.

v0:
```python
from functools import partial
import math

import jax
import jax.numpy as jnp
import numpy as np
from jax import lax
from jax.sharding import PartitionSpec as P

HEADS = 12
HEAD_DIM = 64
FF = 2048
NUM_BUCKETS = 32
SEQ = 512
ENC_SEQ = 512


eps = 1e-06
masked_score = -1e30
bucket_edges = np.array(
    list(range(1, 16)) + [int(math.ceil(16.0 * 8.0 ** ((b - 16) / 16.0))) for b in range(16, 32)],
    dtype=np.int32,
)


def as_sent(array):
    return jax.tree.map(lambda a: a.astype(jnp.bfloat16) if a.dtype == jnp.float32 else a, array)


def bucket_table(length):
    rows = jnp.arange(length, dtype=jnp.int32)
    distance = jnp.maximum(rows[:, None] - rows[None, :], 0)
    total = jnp.zeros((length, length), jnp.int32)
    for edge_value in bucket_edges:
        total = total + (distance >= int(edge_value)).astype(jnp.int32)
    return total


def gather_forward(parts):
    return jax.tree.map(
        lambda part, own: part.astype(own.dtype),
        lax.all_gather(as_sent(parts), "shard", axis=0, tiled=True),
        parts,
    )


def gather_backward(parts):
    return jax.tree.map(
        lambda part, own: part.astype(own.dtype),
        lax.all_gather(as_sent(parts), "shard", axis=0, tiled=True),
        parts,
    )


def obtain(parts):
    return gather_backward(parts)


def reduce_end(parts):
    shares = (
        lax.psum_scatter(
            parts[0].astype(jnp.bfloat16), "shard", scatter_dimension=0, tiled=True
        ).astype(jnp.float32),
        lax.psum_scatter(
            parts[1].astype(jnp.bfloat16), "shard", scatter_dimension=0, tiled=True
        ).astype(jnp.float32),
        lax.psum_scatter(
            parts[2].astype(jnp.bfloat16), "shard", scatter_dimension=0, tiled=True
        ).astype(jnp.float32),
        lax.psum_scatter(
            parts[3].astype(jnp.bfloat16), "shard", scatter_dimension=0, tiled=True
        ).astype(jnp.float32),
        lax.psum_scatter(
            parts[4].astype(jnp.bfloat16), "shard", scatter_dimension=0, tiled=True
        ).astype(jnp.float32),
        lax.psum_scatter(
            parts[5].astype(jnp.bfloat16), "shard", scatter_dimension=0, tiled=True
        ).astype(jnp.float32),
        lax.psum_scatter(
            parts[6].astype(jnp.bfloat16), "shard", scatter_dimension=0, tiled=True
        ).astype(jnp.float32),
        lax.psum_scatter(
            parts[7].astype(jnp.bfloat16), "shard", scatter_dimension=0, tiled=True
        ).astype(jnp.float32),
        lax.psum_scatter(
            parts[8].astype(jnp.bfloat16), "shard", scatter_dimension=0, tiled=True
        ).astype(jnp.float32),
        lax.psum_scatter(
            parts[9].astype(jnp.bfloat16), "shard", scatter_dimension=0, tiled=True
        ).astype(jnp.float32),
        lax.psum_scatter(
            parts[10].astype(jnp.bfloat16), "shard", scatter_dimension=0, tiled=True
        ).astype(jnp.float32),
    )
    return lax.psum(
        (
            shares[0],
            shares[1],
            shares[2],
            shares[3],
            shares[4],
            shares[5],
            shares[6],
            shares[7],
            shares[8],
            shares[9],
            shares[10],
        ),
        "rep",
    )


def norm_forward(inputs, gain):
    factor = lax.rsqrt(jnp.mean(inputs * inputs, -1, keepdims=True) + eps)
    return (factor, inputs * factor * gain)


def norm_backward(inputs, factor, gain, grad_norm):
    weighted = grad_norm * gain
    grad_gain = jnp.sum(grad_norm * inputs * factor, 0)
    grad_input = factor * weighted - inputs * factor**3 * jnp.mean(
        weighted * inputs, -1, keepdims=True
    )
    return (grad_input, grad_gain)


def masked_scores(queries, key_rows, position_bias, visible):
    scores = jnp.einsum("bqhd,bkhd->bhqk", queries, key_rows, preferred_element_type=jnp.float32)
    if position_bias is not None:
        scores = scores + position_bias
    return jnp.where(visible[:, None], scores, masked_score)


def attend_forward(queries, key_rows, value_rows, position_bias, visible):
    scores = masked_scores(queries, key_rows, position_bias, visible)
    top = jnp.max(scores, -1, keepdims=True)
    expd = jnp.exp(scores - top)
    total = jnp.sum(expd, -1, keepdims=True)
    probs = (expd / total).astype(jnp.bfloat16)
    mixed = jnp.einsum("bhqk,bkhd->bqhd", probs, value_rows, preferred_element_type=jnp.float32)
    return (mixed, top + jnp.log(total))


def attend_backward(queries, key_rows, value_rows, position_bias, visible, log_total, grad_mixed):
    scores = masked_scores(queries, key_rows, position_bias, visible)
    probs = jnp.exp(scores - log_total)
    grad_values = jnp.einsum(
        "bhqk,bqhd->bkhd",
        probs.astype(jnp.bfloat16),
        grad_mixed,
        preferred_element_type=jnp.float32,
    )
    grad_probs = jnp.einsum(
        "bqhd,bkhd->bhqk", grad_mixed, value_rows, preferred_element_type=jnp.float32
    )
    score_gradient = (probs * (grad_probs - jnp.sum(probs * grad_probs, -1, keepdims=True))).astype(
        jnp.bfloat16
    )
    query_rows_gradient = jnp.einsum(
        "bhqk,bkhd->bqhd", score_gradient, key_rows, preferred_element_type=jnp.float32
    )
    grad_keys = jnp.einsum(
        "bhqk,bqhd->bkhd", score_gradient, queries, preferred_element_type=jnp.float32
    )
    return (score_gradient, query_rows_gradient, grad_keys, grad_values)


def local(
    hidden_in,
    enc_states,
    dec_segments,
    enc_segments,
    out_grad,
    gains,
    rel_table,
    self_qkv,
    self_out,
    cross_q,
    cross_kv,
    cross_out,
    ff_in,
    ff_out,
):
    tokens_here = hidden_in.shape[0]
    batch_rows = tokens_here // SEQ
    enc_here = enc_states.shape[0]
    inner_width = HEADS * HEAD_DIM
    dec_ids = dec_segments.reshape(batch_rows, SEQ)
    enc_ids = enc_segments.reshape(batch_rows, ENC_SEQ)
    positions = jnp.arange(SEQ, dtype=jnp.int32)
    causal = positions[:, None] >= positions[None, :]
    causal_segment_mask = causal[None] & (dec_ids[:, :, None] == dec_ids[:, None, :])
    cross_mask = dec_ids[:, :, None] == enc_ids[:, None, :]
    bucket_indicator = (
        bucket_table(SEQ)[None] == jnp.arange(NUM_BUCKETS, dtype=jnp.int32)[:, None, None]
    ).astype(jnp.bfloat16)
    self_attention_weights = gather_forward((gains[0], rel_table, self_qkv, self_out))
    cross_set = gather_forward((gains[1], cross_q, cross_kv, cross_out))
    ffn_set = gather_forward((gains[2], ff_in, ff_out))
    inputs = hidden_in.astype(jnp.float32)
    gain_one = self_attention_weights[0].astype(jnp.float32)
    position_bias = jnp.einsum(
        "pai,pm->mai",
        bucket_indicator,
        self_attention_weights[1],
        preferred_element_type=jnp.float32,
    )
    factor_one, normed_one = norm_forward(inputs, gain_one)
    normed_one = normed_one.astype(jnp.bfloat16)
    qkv = jnp.dot(normed_one, self_attention_weights[2], preferred_element_type=jnp.float32).astype(
        jnp.bfloat16
    )
    qkv = qkv.reshape(batch_rows, SEQ, 3, HEADS, HEAD_DIM)
    self_q = qkv[:, :, 0]
    self_k = qkv[:, :, 1]
    self_v = qkv[:, :, 2]
    mixed_one, lse_one = attend_forward(self_q, self_k, self_v, position_bias, causal_segment_mask)
    attn_one = mixed_one.astype(jnp.bfloat16).reshape(tokens_here, inner_width)
    first = inputs + jnp.dot(
        attn_one, self_attention_weights[3], preferred_element_type=jnp.float32
    )
    gain_two = cross_set[0].astype(jnp.float32)
    factor_two, normed_two = norm_forward(first, gain_two)
    normed_two = normed_two.astype(jnp.bfloat16)
    cross_heads = jnp.dot(normed_two, cross_set[1], preferred_element_type=jnp.float32).astype(
        jnp.bfloat16
    )
    cross_heads = cross_heads.reshape(batch_rows, SEQ, HEADS, HEAD_DIM)
    enc_kv = jnp.dot(enc_states, cross_set[2], preferred_element_type=jnp.float32).astype(
        jnp.bfloat16
    )
    enc_kv = enc_kv.reshape(batch_rows, ENC_SEQ, 2, HEADS, HEAD_DIM)
    enc_k = enc_kv[:, :, 0]
    enc_v = enc_kv[:, :, 1]
    mixed_two, lse_two = attend_forward(cross_heads, enc_k, enc_v, None, cross_mask)
    attn_two = mixed_two.astype(jnp.bfloat16).reshape(tokens_here, inner_width)
    second = first + jnp.dot(attn_two, cross_set[3], preferred_element_type=jnp.float32)
    gain_three = ffn_set[0].astype(jnp.float32)
    factor_three, normed_three = norm_forward(second, gain_three)
    normed_three = normed_three.astype(jnp.bfloat16)
    pre = jnp.dot(normed_three, ffn_set[1], preferred_element_type=jnp.float32)
    gate_part = pre[:, :FF]
    up_part = pre[:, FF:]
    activated, gelu_pull = jax.vjp(partial(jax.nn.gelu, approximate=True), gate_part)
    hidden_units = (activated * up_part).astype(jnp.bfloat16)
    result = second + jnp.dot(hidden_units, ffn_set[2], preferred_element_type=jnp.float32)
    layer_out = result.astype(jnp.bfloat16)
    ffn_back = obtain((gains[2], ff_in, ff_out))
    grad_out = out_grad.astype(jnp.float32)
    ff_out_part = jnp.dot(hidden_units.T, out_grad, preferred_element_type=jnp.float32)
    grad_hidden = jnp.dot(out_grad, ffn_back[2].T, preferred_element_type=jnp.float32).astype(
        jnp.bfloat16
    )
    grad_gate = gelu_pull(grad_hidden * up_part)[0]
    grad_up = grad_hidden * activated
    grad_pre = jnp.concatenate([grad_gate, grad_up], 1).astype(jnp.bfloat16)
    ff_in_part = jnp.dot(normed_three.T, grad_pre, preferred_element_type=jnp.float32)
    grad_norm_three = jnp.dot(grad_pre, ffn_back[1].T, preferred_element_type=jnp.float32)
    back_three, gain_three_part = norm_backward(
        second, factor_three, ffn_back[0].astype(jnp.float32), grad_norm_three
    )
    grad_second = grad_out + back_three
    cross_attention_backward = obtain((gains[1], cross_q, cross_kv, cross_out))
    out_two = grad_second.astype(jnp.bfloat16)
    cross_out_part = jnp.dot(attn_two.T, out_two, preferred_element_type=jnp.float32)
    grad_attn_two = jnp.dot(
        out_two, cross_attention_backward[3].T, preferred_element_type=jnp.float32
    ).astype(jnp.bfloat16)
    grad_attn_two = grad_attn_two.reshape(batch_rows, SEQ, HEADS, HEAD_DIM)
    unused_scores, grad_cq, grad_ck, grad_cv = attend_backward(
        cross_heads, enc_k, enc_v, None, cross_mask, lse_two, grad_attn_two
    )
    grad_cq = grad_cq.astype(jnp.bfloat16).reshape(tokens_here, inner_width)
    grad_ckv = (
        jnp.stack([grad_ck, grad_cv], axis=2)
        .astype(jnp.bfloat16)
        .reshape(enc_here, 2 * inner_width)
    )
    cross_q_part = jnp.dot(normed_two.T, grad_cq, preferred_element_type=jnp.float32)
    cross_kv_part = jnp.dot(enc_states.T, grad_ckv, preferred_element_type=jnp.float32)
    enc_grad = jnp.dot(grad_ckv, cross_attention_backward[2].T, preferred_element_type=jnp.float32)
    grad_norm_two = jnp.dot(
        grad_cq, cross_attention_backward[1].T, preferred_element_type=jnp.float32
    )
    back_two, gain_two_part = norm_backward(
        first, factor_two, cross_attention_backward[0].astype(jnp.float32), grad_norm_two
    )
    grad_first = grad_second + back_two
    self_back = obtain((gains[0], rel_table, self_qkv, self_out))
    out_one = grad_first.astype(jnp.bfloat16)
    self_out_part = jnp.dot(attn_one.T, out_one, preferred_element_type=jnp.float32)
    grad_attn_one = jnp.dot(out_one, self_back[3].T, preferred_element_type=jnp.float32).astype(
        jnp.bfloat16
    )
    grad_attn_one = grad_attn_one.reshape(batch_rows, SEQ, HEADS, HEAD_DIM)
    score_gradient, grad_q, grad_k, grad_v = attend_backward(
        self_q, self_k, self_v, position_bias, causal_segment_mask, lse_one, grad_attn_one
    )
    table_part = jnp.einsum(
        "wtiy,aiy->at", score_gradient, bucket_indicator, preferred_element_type=jnp.float32
    )
    grad_qkv = (
        jnp.stack([grad_q, grad_k, grad_v], axis=2)
        .astype(jnp.bfloat16)
        .reshape(tokens_here, 3 * inner_width)
    )
    self_qkv_part = jnp.dot(normed_one.T, grad_qkv, preferred_element_type=jnp.float32)
    grad_norm_one = jnp.dot(grad_qkv, self_back[2].T, preferred_element_type=jnp.float32)
    back_one, gain_one_part = norm_backward(
        inputs, factor_one, self_back[0].astype(jnp.float32), grad_norm_one
    )
    in_grad = grad_first + back_one
    totals = reduce_end(
        (
            gain_one_part,
            gain_two_part,
            gain_three_part,
            table_part,
            self_qkv_part,
            self_out_part,
            cross_q_part,
            cross_kv_part,
            cross_out_part,
            ff_in_part,
            ff_out_part,
        )
    )
    gains_grad = jnp.stack([totals[0], totals[1], totals[2]])
    rel_table_grad = totals[3]
    self_qkv_grad = totals[4]
    self_out_grad = totals[5]
    cross_query_gradient = totals[6]
    cross_kv_grad = totals[7]
    cross_out_grad = totals[8]
    ff_in_grad = totals[9]
    ff_out_grad = totals[10]
    return (
        layer_out,
        in_grad,
        enc_grad,
        gains_grad,
        rel_table_grad,
        self_qkv_grad,
        self_out_grad,
        cross_query_gradient,
        cross_kv_grad,
        cross_out_grad,
        ff_in_grad,
        ff_out_grad,
    )


def solution(mesh):
    in_specs = (
        P(("rep", "shard"), None),
        P(("rep", "shard"), None),
        P(("rep", "shard")),
        P(("rep", "shard")),
        P(("rep", "shard"), None),
        P(None, "shard"),
        P("shard", None),
        P("shard", None),
        P("shard", None),
        P("shard", None),
        P("shard", None),
        P("shard", None),
        P("shard", None),
        P("shard", None),
    )
    out_specs = (
        P(("rep", "shard"), None),
        P(("rep", "shard"), None),
        P(("rep", "shard"), None),
        P(None, "shard"),
        P("shard", None),
        P("shard", None),
        P("shard", None),
        P("shard", None),
        P("shard", None),
        P("shard", None),
        P("shard", None),
        P("shard", None),
    )
    return jax.shard_map(local, mesh=mesh, in_specs=in_specs, out_specs=out_specs, check_vma=False)
```

profile of v0, /device:TPU:0, one launch (start us, length us, event | category | flops | bytes accessed | tf_op | source)
XLA Modules:
  0.0 981.7 jit_solution(17233902450009571987)
XLA Ops:
  16.0 8.7 all-reduce.9
  25.5 5.4 all_gather.45
  33.7 2.6 copy.116
  36.3 9.9 %fusion.18 = f32[12,512,512]{2,0,1:T(8,128)} fusion(s32[512,512]{1,0:T(8,128)} %convert_add_fusion.1, bf16[32,12]{1,0:T(8,128)(2,1)S(1)} %all_gather.45), kind=kOutput, calls=%fused_computation.34 | convolution fusion | flops 209715200 | bytes 13632256 | tf_op jit(solution)/shard_map/pai,pm->mai/dot_general | solution.py:202
  46.2 18.0 %copy.105 = f32[12,512,512]{1,2,0:T(8,128)} copy(f32[12,512,512]{2,0,1:T(8,128)} %fusion.18) | data formatting | bytes 25165824 | tf_op jit(solution)/shard_map/pai,pm->mai/dot_general | solution.py:202
  65.8 5.6 convolution_convert_fusion.3
  71.4 4.6 copy.108
  76.1 6.2 reshape.259
  82.3 5.2 fusion.113
  87.5 7.9 convolution_convert_fusion.1
  95.4 6.7 copy.101
  102.1 8.8 reshape.257
  111.0 6.8 fusion.112
  117.8 14.6 %fusion.115 = (f32[2,12,512]{2,1,0:T(8,128)S(1)}, f32[2,12,512,512]{2,3,1,0:T(8,128)}) fusion(f32[12,512,512]{1,2,0:T(8,128)} %copy.105, bf16[2,512,1,12,64]{1,0,4,3,2:T(2,128)(2,1)S(1)} %get-tuple-element.82, bf16[2,512,1,12,64]{1,0,4,3,2:T(2,128)(2,1)} %get-tuple-element.81, pred[2,512,512]{1,2,0:T(8,128)(4,1)} %get-tuple-element.92), kind=kOutput, calls=%fused_computation.190 | convolution fusion | flops 824168448 | bytes 41467904 | tf_op jit(solution)/shard_map/bqhd,bkhd->bhqk/dot_general | solution.py:128
  132.4 11.7 %fusion.2 = f32[2,12,512]{2,1,0:T(8,128)S(1)} fusion(f32[2,12,512,512]{2,3,1,0:T(8,128)} %get-tuple-element.96, f32[2,12,512]{2,1,0:T(8,128)S(1)} %get-tuple-element.95), kind=kLoop, calls=%fused_computation.15 | loop fusion | flops 12570624 | bytes 25264128 | tf_op jit(solution)/shard_map/reduce_sum | solution.py:138
  144.2 10.7 %fusion.56 = bf16[2,512,12,64]{1,3,2,0:T(8,128)(2,1)S(1)} fusion(f32[2,12,512,512]{2,3,1,0:T(8,128)} %get-tuple-element.96, f32[2,12,512]{2,1,0:T(8,128)S(1)} %fusion.2, f32[2,12,512]{2,1,0:T(8,128)S(1)} %get-tuple-element.95, bf16[2,512,1,12,64]{1,0,4,3,2:T(2,128)(2,1)S(1)} %copy-done.18), kind=kOutput, calls=%fused_computation.110 | convolution fusion | flops 824967168 | bytes 28409856 | tf_op jit(solution)/shard_map/bhqk,bkhd->bqhd/dot_general | solution.py:140
  158.1 5.0 multiply_reduce_fusion.7
  163.7 5.0 convolution_convert_fusion.13
  168.7 2.7 copy.110
  171.4 3.8 reshape.260
  175.2 12.9 %select_reduce_fusion = (f32[2,12,512]{2,1,0:T(8,128)S(1)}, f32[2,12,512,512]{2,3,1,0:T(8,128)}) fusion(pred[2,512,512]{1,2,0:T(8,128)(4,1)} %get-tuple-element.91, bf16[2,512,1,12,64]{1,0,4,3,2:T(2,128)(2,1)S(1)} %copy-done.4, bf16[2,512,12,64]{1,0,3,2:T(2,128)(2,1)} %reshape.260), kind=kOutput, calls=%fused_computation.17 | convolution fusion | flops 817876992 | bytes 28884992 | tf_op jit(solution)/shard_map/bqhd,bkhd->bhqk/dot_general | solution.py:128
  188.1 10.9 %fusion.3 = f32[2,12,512]{2,1,0:T(8,128)S(1)} fusion(f32[2,12,512,512]{2,3,1,0:T(8,128)} %get-tuple-element.100, f32[2,12,512]{2,1,0:T(8,128)S(1)} %get-tuple-element.99, pred[2,512,512]{1,2,0:T(8,128)(4,1)S(1)} %copy-done.10), kind=kLoop, calls=%fused_computation.16 | loop fusion | flops 18862080 | bytes 25788416 | tf_op jit(solution)/shard_map/reduce_sum | solution.py:138
  199.0 11.5 %fusion.57 = bf16[2,512,12,64]{1,3,2,0:T(8,128)(2,1)S(1)} fusion(f32[2,12,512,512]{2,3,1,0:T(8,128)} %get-tuple-element.100, f32[2,12,512]{2,1,0:T(8,128)S(1)} %fusion.3, f32[2,12,512]{2,1,0:T(8,128)S(1)} %get-tuple-element.99, pred[2,512,512]{1,2,0:T(8,128)(4,1)S(1)} %copy-done.10, bf16[2,512,1,12,64]{1,0,4,3,2:T(2,128)(2,1)S(1)} %copy-done.20), kind=kOutput, calls=%fused_computation.111 | convolution fusion | flops 831258624 | bytes 28934144 | tf_op jit(solution)/shard_map/bhqk,bkhd->bqhd/dot_general | solution.py:140
  213.7 5.9 multiply_reduce_fusion.6
  219.6 13.5 %fusion.111 = f32[1024,4096]{1,0:T(8,128)} fusion(bf16[768,4096]{1,0:T(8,128)(2,1)} %all-gather.21.cloned.1.call-done, f32[1024,768]{0,1:T(8,128)} %get-tuple-element.102, f32[768]{0:T(1024)S(1)} %copy-done.31, f32[1024]{0:T(1024)S(1)} %get-tuple-element.90), kind=kOutput, calls=%fused_computation.186 | convolution fusion | flops 6444810240 | bytes 26221568 | tf_op jit(solution)/shard_map/dot_general | solution.py:241
  233.2 17.6 %fusion.26 = (bf16[1024,2048]{1,0:T(8,128)(2,1)}, bf16[1024,2048]{1,0:T(8,128)(2,1)}, bf16[1024,2048]{1,0:T(8,128)(2,1)}) fusion(f32[1024,4096]{1,0:T(8,128)} %fusion.111, bf16[1024,768]{1,0:T(8,128)(2,1)} %param.18, bf16[2048,768]{1,0:T(8,128)(2,1)} %all-gather.23.cloned.1.call-done), kind=kOutput, calls=%fused_computation.42 | convolution fusion | flops 3279945728 | bytes 34078720 | tf_op jit(solution)/shard_map/dot_general | solution.py:251
  250.7 10.7 %multiply_reduce_fusion.2 = (bf16[768]{0:T(1024)(128)(2,1)}, f32[1024]{0:T(1024)S(1)}, f32[1024,768]{0,1:T(8,128)S(1)}) fusion(f32[1024,768]{0,1:T(8,128)S(1)} %copy-done.12, f32[1024]{0:T(1024)S(1)} %get-tuple-element.90, f32[768]{0:T(1024)S(1)} %copy-done.31, bf16[768,4096]{1,0:T(8,128)(2,1)S(1)} %copy-done.21, bf16[1024,2048]{1,0:T(8,128)(2,1)} %get-tuple-element.78, ...), kind=kOutput, calls=%fused_computation.71 | convolution fusion | flops 6463944704 | bytes 20984320 | tf_op jit(solution)/shard_map/dot_general | solution.py:258
  263.9 2.5 convolution_convert_fusion.14
  266.5 4.8 convolution_convert_fusion.12
  271.3 2.7 copy.118
  274.1 3.9 reshape.262
  277.9 20.9 %multiply_reduce_fusion.1 = (f32[2,12,512]{2,1,0:T(8,128)S(1)}, f32[2,12,512,512]{2,3,1,0:T(8,128)}) fusion(f32[2,12,512,512]{2,3,1,0:T(8,128)} %get-tuple-element.100, f32[2,12,512]{2,1,0:T(8,128)S(1)} %log_add_fusion.1, pred[2,512,512]{1,2,0:T(8,128)(4,1)} %get-tuple-element.91, bf16[2,512,1,12,64]{1,0,4,3,2:T(2,128)(2,1)} %get-tuple-element.83, ...), kind=kOutput, calls=%fused_computation.8 | convolution fusion | flops 830459904 | bytes 54099968 | tf_op jit(solution)/shard_map/bqhd,bkhd->bhqk/dot_general | solution.py:153
  298.8 17.1 %multiply_convert_fusion.1 = bf16[2,12,512,512]{2,3,1,0:T(8,128)(2,1)S(1)} fusion(f32[2,12,512,512]{2,3,1,0:T(8,128)} %get-tuple-element.105, f32[2,12,512,512]{2,3,1,0:T(8,128)} %get-tuple-element.100, f32[2,12,512]{2,1,0:T(8,128)S(1)} %get-tuple-element.104, f32[2,12,512]{2,1,0:T(8,128)S(1)} %log_add_fusion.1, pred[2,512,512]{1,2,0:T(8,128)(4,1)} %get-tuple-element.91), kind=kLoop, calls=%fused_computation.7 | loop fusion | flops 31457280 | bytes 63537152 | tf_op jit(solution)/shard_map/convert_element_type | solution.py:156
  325.2 4.7 multiply_reduce_fusion.3
  334.9 8.6 fusion.52
  343.5 11.3 %fusion.53 = bf16[2,512,1,12,64]{1,4,3,0,2:T(8,128)(2,1)S(1)} fusion(f32[2,12,512,512]{2,3,1,0:T(8,128)} %get-tuple-element.100, f32[2,12,512]{2,1,0:T(8,128)S(1)} %log_add_fusion.1, pred[2,512,512]{1,2,0:T(8,128)(4,1)S(1)} %copy-done.11, bf16[2,512,12,64]{1,0,3,2:T(2,128)(2,1)S(1)} %copy-done.19), kind=kOutput, calls=%fused_computation.109 | convolution fusion | flops 824967168 | bytes 28884992 | tf_op jit(solution)/shard_map/bhqk,bqhd->bkhd/dot_general | solution.py:147
  355.1 3.3 copy.135
  360.9 3.8 fusion.37
  364.7 4.3 copy.155
  369.6 3.8 convolution_convert_fusion.11
  375.0 2.9 reshape.264
  377.9 8.1 convolution_convert_fusion.6
  386.1 17.5 %multiply_reduce_fusion = (f32[2,12,512]{2,1,0:T(8,128)S(1)}, f32[2,12,512,512]{2,3,1,0:T(8,128)}) fusion(f32[2,12,512,512]{2,3,1,0:T(8,128)} %get-tuple-element.96, f32[2,12,512]{2,1,0:T(8,128)S(1)} %log_add_fusion, bf16[2,512,1,12,64]{1,0,4,3,2:T(2,128)(2,1)} %get-tuple-element.80, bf16[2,512,12,64]{1,0,3,2:T(2,128)(2,1)S(1)} %reshape.264), kind=kOutput, calls=%fused_computation.5 | convolution fusion | flops 824168448 | bytes 53575680 | tf_op jit(solution)/shard_map/bqhd,bkhd->bhqk/dot_general | solution.py:153
  403.5 25.8 %convert_reduce_fusion = (bf16[12,512,512]{1,2,0:T(8,128)(2,1)}, bf16[2,12,512,512]{2,3,1,0:T(8,128)(2,1)}) fusion(f32[2,12,512,512]{2,3,1,0:T(8,128)} %get-tuple-element.108, f32[2,12,512]{2,1,0:T(8,128)S(1)} %get-tuple-element.107, f32[2,12,512,512]{2,3,1,0:T(8,128)} %get-tuple-element.96, f32[2,12,512]{2,1,0:T(8,128)S(1)} %log_add_fusion), kind=kLoop, calls=%fused_computation.3 | loop fusion | flops 34603008 | bytes 69304320 | tf_op jit(solution)/shard_map/wtiy,aiy->at/reduce_sum | solution.py:299
  429.3 9.7 fusion.51
  439.0 7.7 fusion.50
  446.7 11.8 %fusion.46 = bf16[2,512,1,12,64]{1,4,3,0,2:T(8,128)(2,1)} fusion(f32[2,12,512,512]{2,3,1,0:T(8,128)} %get-tuple-element.96, f32[2,12,512]{2,1,0:T(8,128)S(1)} %log_add_fusion, bf16[2,512,12,64]{1,0,3,2:T(2,128)(2,1)S(1)} %reshape.264), kind=kOutput, calls=%fused_computation.104 | convolution fusion | flops 818675712 | bytes 28360704 | tf_op jit(solution)/shard_map/bhqk,bqhd->bkhd/dot_general | solution.py:147
  458.5 5.0 pad_maximum_fusion.3
  463.5 9.4 copy.129
  473.0 4.0 copy.165
  479.1 5.5 convolution_convert_fusion.2
  485.3 13.8 %convolution_convert_fusion = bf16[768,4096]{1,0:T(8,128)(2,1)} fusion(bf16[1024,2048]{1,0:T(8,128)(2,1)} %get-tuple-element.78, bf16[1024,2048]{1,0:T(8,128)(2,1)} %get-tuple-element.77, f32[1024,768]{0,1:T(8,128)} %get-tuple-element.102, f32[768]{0:T(1024)S(1)} %copy-done.32, f32[1024]{0:T(1024)S(1)} %copy-done.34), kind=kOutput, calls=%fused_computation.52 | convolution fusion | flops 6464733184 | bytes 17832960 | tf_op jit(solution)/shard_map/dot_general | solution.py:257
  500.3 8.7 add_convert_fusion
  509.0 2.8 copy.140
  511.8 7.5 fusion.36
  519.3 2.5 fusion.33
  521.8 3.6 copy.141
  525.4 14.8 %copy.139 = bf16[12,512,512]{2,0,1:T(8,128)(2,1)} copy(bf16[12,512,512]{1,2,0:T(8,128)(2,1)} %get-tuple-element.75) | data formatting | bytes 12582912 | tf_op jit(solution)/shard_map/wtiy,aiy->at/reduce_sum | solution.py:299
  540.2 6.9 fusion.68
  547.2 12.6 %all-reduce.8 = (bf16[768]{0:T(1024)(128)(2,1)S(1)}, bf16[768]{0:T(1024)(128)(2,1)S(1)}, bf16[768]{0:T(1024)(128)(2,1)S(1)}, bf16[32,12]{1,0:T(8,128)(2,1)S(1)}) all-reduce(bf16[768]{0:T(1024)(128)(2,1)S(1)} %copy-done.47, bf16[768]{0:T(1024)(128)(2,1)S(1)} %copy-done.48, ...), channel_id=7, replica_groups=mesh['rep'=8,'shard'=4] {'shard'}, use_global_device_ids=true, to_apply=%region_19.20.clone | all-reduce | flops 2688 | bytes 10752
  559.9 6.9 fusion.116
  568.3 19.9 %reduce-scatter.18.cloned.1.call-done = bf16[192,4096]{1,0:T(8,128)(2,1)} async-done(((bf16[768,4096]{1,0:T(8,128)(2,1)}), bf16[192,4096]{1,0:T(8,128)(2,1)}) %reduce-scatter.18.cloned.1.call-update) | async-done | bytes 1572880 | tf_op jit(solution)/shard_map/reduce_scatter | solution.py:88
  588.2 383.3 %all-reduce.11 = (f32[1,192]{1,0:T(1,128)S(1)}, f32[1,192]{1,0:T(1,128)S(1)}, f32[1,192]{1,0:T(1,128)S(1)}, f32[8,12]{1,0:T(8,128)}, f32[192,2304]{1,0:T(8,128)}...) all-reduce(f32[1,192]{1,0:T(1,128)S(1)} %bitcast.158, ...), channel_id=1, replica_groups=mesh['rep'=8,'shard'=4] {'rep'}, use_global_device_ids=true, to_apply=%region_20.21 | all-reduce | flops 2359968 | bytes 14161152 | tf_op jit(solution)/shard_map/psum | solution.py:95
  971.4 2.9 copy.142
  (186 shorter events, 46.8 us)
Async XLA Ops:
  7.2 58.6 %copy-start = (bf16[1024,768]{1,0:T(8,128)(2,1)S(1)}, bf16[1024,768]{1,0:T(8,128)(2,1)}, u32[]{:S(2)}) copy-start(bf16[1024,768]{1,0:T(8,128)(2,1)} %param.15) | copy-start | bytes 4718596
  7.2 6.9 copy-start.49
  7.2 6.9 copy-start.43
  7.2 18.2 %copy-start.44 = (s32[1024]{0:T(1024)S(1)}, s32[1024]{0:T(1024)}, u32[]{:S(2)}) copy-start(s32[1024]{0:T(1024)} %param.16) | copy-start | bytes 12292
  7.2 18.2 %copy-start.45 = (s32[1024]{0:T(1024)S(1)}, s32[1024]{0:T(1024)}, u32[]{:S(2)}) copy-start(s32[1024]{0:T(1024)} %param.17) | copy-start | bytes 12292
  7.2 18.2 %copy-start.46 = (bf16[8,12]{1,0:T(8,128)(2,1)S(1)}, bf16[8,12]{1,0:T(8,128)(2,1)}, u32[]{:S(2)}) copy-start(bf16[8,12]{1,0:T(8,128)(2,1)} %param.20) | copy-start | bytes 580
  7.2 58.5 %all-gather.15.cloned.1.call-start = ((), (), s32[]{:S(2)}) async-start(), calls=%async_computation.9 | async-start | bytes 2949120 | tf_op jit(solution)/shard_map/all_gather | solution.py:42
  8.0 79.5 %all-gather.11.cloned.1.call-start = ((), (), s32[]{:S(2)}) async-start(), calls=%async_computation.7 | async-start | bytes 4423680 | tf_op jit(solution)/shard_map/all_gather | solution.py:42
  8.7 149.4 %all-gather.13.cloned.1.call-start = ((), (), s32[]{:S(2)}) async-start(), calls=%async_computation.8 | async-start | bytes 1474560 | tf_op jit(solution)/shard_map/all_gather | solution.py:42
  9.5 154.2 %all-gather.17.cloned.1.call-start = ((), (), s32[]{:S(2)}) async-start(), calls=%async_computation.10 | async-start | bytes 1474560 | tf_op jit(solution)/shard_map/all_gather | solution.py:42
  10.0 203.6 %all-gather.19.cloned.1.call-start = ((), (), s32[]{:S(2)}) async-start(), calls=%async_computation.11 | async-start | bytes 1474560 | tf_op jit(solution)/shard_map/all_gather | solution.py:42
  10.6 209.0 %all-gather.21.cloned.1.call-start = ((), (), s32[]{:S(2)}) async-start(), calls=%async_computation.12 | async-start | bytes 7864320 | tf_op jit(solution)/shard_map/all_gather | solution.py:42
  11.2 221.9 %all-gather.23.cloned.1.call-start = ((), (), s32[]{:S(2)}) async-start(), calls=%async_computation.13 | async-start | bytes 3932160 | tf_op jit(solution)/shard_map/all_gather | solution.py:42
  12.0 554.9 %reduce-scatter.16.cloned.1.call-start = ((), (), s32[]{:S(2)}) async-start(), calls=%async_computation.17 | async-start | bytes 1474560 | tf_op jit(solution)/shard_map/reduce_scatter | solution.py:85
  24.8 62.7 %copy-start.41 = (f32[768]{0:T(1024)}, f32[768]{0:T(1024)S(1)}, u32[]{:S(2)}) copy-start(f32[768]{0:T(1024)S(1)} %convert_element_type.551) | copy-start | bytes 9220
  32.6 55.0 %copy-start.7 = (bf16[1024,768]{0,1:T(8,128)(2,1)}, bf16[1024,768]{0,1:T(8,128)(2,1)S(1)}, u32[]{:S(2)}) copy-start(bf16[1024,768]{0,1:T(8,128)(2,1)S(1)} %copy.100) | copy-start | bytes 4718596
  33.7 53.9 %copy-start.38 = (f32[1024]{0:T(1024)}, f32[1024]{0:T(1024)S(1)}, u32[]{:S(2)}) copy-start(f32[1024]{0:T(1024)S(1)} %get-tuple-element.86) | copy-start | bytes 12292
  117.8 14.6 %copy-start.2 = (bf16[2,512,1,12,64]{1,0,4,3,2:T(2,128)(2,1)}, bf16[2,512,1,12,64]{1,0,4,3,2:T(2,128)(2,1)S(1)}, u32[]{:S(2)}) copy-start(bf16[2,512,1,12,64]{1,0,4,3,2:T(2,128)(2,1)S(1)} %get-tuple-element.82) | copy-start | bytes 4718596
  132.4 11.8 %copy-start.29 = (f32[2,12,512]{2,1,0:T(8,128)}, f32[2,12,512]{2,1,0:T(8,128)S(1)}, u32[]{:S(2)}) copy-start(f32[2,12,512]{2,1,0:T(8,128)S(1)} %get-tuple-element.95) | copy-start | bytes 147460
  132.4 11.8 %copy-start.18 = (bf16[2,512,1,12,64]{1,0,4,3,2:T(2,128)(2,1)S(1)}, bf16[2,512,1,12,64]{1,0,4,3,2:T(2,128)(2,1)}, u32[]{:S(2)}) copy-start(bf16[2,512,1,12,64]{1,0,4,3,2:T(2,128)(2,1)} %get-tuple-element.80) | copy-start | bytes 4718596
  144.1 10.8 %copy-start.35 = (f32[2,12,512]{2,1,0:T(8,128)}, f32[2,12,512]{2,1,0:T(8,128)S(1)}, u32[]{:S(2)}) copy-start(f32[2,12,512]{2,1,0:T(8,128)S(1)} %fusion.2) | copy-start | bytes 147460
  154.9 3.2 copy-start.8
  168.7 6.6 copy-start.4
  175.2 12.9 %copy-start.10 = (pred[2,512,512]{1,2,0:T(8,128)(4,1)S(1)}, pred[2,512,512]{1,2,0:T(8,128)(4,1)}, u32[]{:S(2)}) copy-start(pred[2,512,512]{1,2,0:T(8,128)(4,1)} %get-tuple-element.91) | copy-start | bytes 1572868
  188.1 10.9 %copy-start.20 = (bf16[2,512,1,12,64]{1,0,4,3,2:T(2,128)(2,1)S(1)}, bf16[2,512,1,12,64]{1,0,4,3,2:T(2,128)(2,1)}, u32[]{:S(2)}) copy-start(bf16[2,512,1,12,64]{1,0,4,3,2:T(2,128)(2,1)} %get-tuple-element.83) | copy-start | bytes 4718596
  213.7 5.9 copy-start.31
  219.5 41.9 %copy-start.33 = (f32[1024]{0:T(1024)}, f32[1024]{0:T(1024)S(1)}, u32[]{:S(2)}) copy-start(f32[1024]{0:T(1024)S(1)} %get-tuple-element.90) | copy-start | bytes 12292
  233.1 17.6 %copy-start.12 = (f32[1024,768]{0,1:T(8,128)S(1)}, f32[1024,768]{0,1:T(8,128)}, u32[]{:S(2)}) copy-start(f32[1024,768]{0,1:T(8,128)} %get-tuple-element.102) | copy-start | bytes 9437188
  233.1 17.6 %copy-start.21 = (bf16[768,4096]{1,0:T(8,128)(2,1)S(1)}, bf16[768,4096]{1,0:T(8,128)(2,1)}, u32[]{:S(2)}) copy-start(bf16[768,4096]{1,0:T(8,128)(2,1)} %all-gather.21.cloned.1.call-done) | copy-start | bytes 18874372
  250.7 10.7 %copy-start.22 = (bf16[1024,768]{0,1:T(8,128)(2,1)S(1)}, bf16[1024,768]{0,1:T(8,128)(2,1)}, u32[]{:S(2)}) copy-start(bf16[1024,768]{0,1:T(8,128)(2,1)} %copy.116) | copy-start | bytes 4718596
  261.4 2.5 copy-start.28
  262.3 1.7 copy-start.15
  266.5 300.4 %reduce-scatter.14.cloned.1.call-start = ((), (), s32[]{:S(2)}) async-start(), calls=%async_computation.16 | async-start | bytes 1474560 | tf_op jit(solution)/shard_map/reduce_scatter | solution.py:79
  316.0 4.5 copy-start.1
  320.4 2.0 copy-start.25
  325.0 5.0 copy-start.40
  325.0 241.9 %reduce-scatter.12.cloned.1.call-start = ((), (), s32[]{:S(2)}) async-start(), calls=%async_computation.15 | async-start | bytes 1474560 | tf_op jit(solution)/shard_map/reduce_scatter | solution.py:76
  325.2 4.7 copy-start.16
  325.2 4.7 copy-start.26
  329.9 2.4 copy-start.27
  330.7 1.7 copy-start.13
  332.3 2.5 copy-start.6
  334.8 232.1 %reduce-scatter.22.cloned.1.call-start = ((), (), s32[]{:S(2)}) async-start(), calls=%async_computation.20 | async-start | bytes 2949120
  334.9 8.6 copy-start.11
  334.9 8.6 copy-start.19
  359.3 1.6 copy-start.24
  364.7 4.8 copy-start.30
  364.7 4.8 copy-start.36
  369.1 199.2 %reduce-scatter.20.cloned.1.call-start = ((), (), s32[]{:S(2)}) async-start(), calls=%async_computation.19 | async-start | bytes 3932160 | tf_op jit(solution)/shard_map/reduce_scatter | solution.py:91
  386.0 182.2 %reduce-scatter.10.cloned.1.call-start = ((), (), s32[]{:S(2)}) async-start(), calls=%async_computation.14 | async-start | bytes 4423680 | tf_op jit(solution)/shard_map/reduce_scatter | solution.py:73
  403.5 25.8 %copy-start.5 = (bf16[2,512,1,12,64]{1,0,4,3,2:T(2,128)(2,1)S(1)}, bf16[2,512,1,12,64]{1,0,4,3,2:T(2,128)(2,1)}, u32[]{:S(2)}) copy-start(bf16[2,512,1,12,64]{1,0,4,3,2:T(2,128)(2,1)} %get-tuple-element.81) | copy-start | bytes 4718596
  429.3 9.7 copy-start.3
  473.0 6.1 copy-start.9
  473.0 6.1 copy-start.39
  473.0 6.1 copy-start.42
  476.9 2.2 copy-start.23
  484.6 0.7 copy-start.32
  484.6 0.7 copy-start.34
  484.6 103.6 %reduce-scatter.18.cloned.1.call-start = ((), (), s32[]{:S(2)}) async-start(), calls=%async_computation.18 | async-start | bytes 7864320 | tf_op jit(solution)/shard_map/reduce_scatter | solution.py:88
  511.8 7.5 copy-start.14
  511.8 7.5 copy-start.37
  525.4 14.8 %copy-start.17 = (s32[512,512]{1,0:T(8,128)S(1)}, s32[512,512]{1,0:T(8,128)}, u32[]{:S(2)}) copy-start(s32[512,512]{1,0:T(8,128)} %convert_add_fusion.1) | copy-start | bytes 3145732
  540.2 7.0 copy-start.47
  540.2 7.0 copy-start.48
Sparse Core Ops, SparseCore 0:
  9.6 26.8 all-gather.14
  38.1 30.9 all-gather.10
  70.7 17.4 all-gather.12
  89.6 17.4 all-gather.16
  108.5 17.4 all-gather.18
  127.4 46.3 all-gather.20
  175.4 28.5 all-gather.22
  266.6 25.9 reduce-scatter.15
  325.1 25.9 reduce-scatter.13
  354.0 25.6 reduce-scatter.11
  382.5 33.0 reduce-scatter.21
  418.0 37.9 reduce-scatter.19
  484.7 42.4 reduce-scatter.9
  529.6 58.5 reduce-scatter.17
where the time goes:
time: 987 us; the launch traced here: 982 us
  blocking collectives  410 us (42%)
  matrix products  302 us (31%)
  local copies, waits for them, and re-layouts  146 us (15%)
  other arithmetic  81.6 us (8%)
  waiting for transfers between devices  24.5 us (2%)
  between operations  16.8 us (2%)
    psum x1, blocking collectives, reduce_end(): lax.psum((shares[0], shares[1], shares[2], shares[3], shares[4], shares[5...  383 us
    unnamed x119, local copies, waits for them, and re-layouts  39.1 us
    dot_general x2, matrix products, attend_backward(): jnp.einsum('bqhd,bkhd->bhqk', grad_mixed, value_rows, preferred_element_t...  38.3 us
    dot_general x2, matrix products, masked_scores(): jnp.einsum('bqhd,bkhd->bhqk', queries, key_rows, preferred_element_type=j...  27.5 us
    reduce_sum x1, other arithmetic, local(): jnp.einsum('wtiy,aiy->at', score_gradient, bucket_indicator, preferred_el...  25.8 us
    dot_general x2, matrix products, attend_backward(): jnp.einsum('bhqk,bqhd->bkhd', probs.astype(jnp.bfloat16), grad_mixed, pre...  23.1 us
    reduce_sum x2, other arithmetic, attend_forward(): total = jnp.sum(expd, -1, keepdims=True)  22.6 us
    dot_general x2, matrix products, attend_forward(): jnp.einsum('bhqk,bkhd->bqhd', probs, value_rows, preferred_element_type=j...  22.2 us
  transfers between devices with their start and end apart: 14, of which 1 were waited for; matrix products, arithmetic and copies ran while one was open for 49% of the time, Pallas kernels for 0%

commit v1 on v0

v1 whole, which is shorter than its diff:
```python
from functools import partial
import math

import jax
import jax.numpy as jnp
import numpy as np
from jax import lax
from jax.experimental import pallas as pl
from jax.experimental.pallas import tpu as pltpu
from jax.sharding import PartitionSpec as P

HEADS = 12
HEAD_DIM = 64
FF = 2048
NUM_BUCKETS = 32
SEQ = 512
D = 768
INNER = HEADS * HEAD_DIM
PAIRS = HEADS // 2
LANES = 128
SPAN = SEQ + LANES
FF_BLOCK = 512
ROWS = 256

eps = 1e-06
masked_score = -1e30
bf16 = jnp.bfloat16
f32 = jnp.float32
VMEM_LIMIT = 56 * 1024 * 1024

bucket_edges = np.array(
    list(range(1, 16)) + [int(math.ceil(16.0 * 8.0 ** ((b - 16) / 16.0))) for b in range(16, 32)],
    dtype=np.int32,
)

SELF_RANGES = ((0, 128), (0, 256), (0, 384), (128, 512))
CROSS_RANGES = ((0, 384), (0, 512), (0, 512), (128, 512))


def dot_nn(a, b):
    return lax.dot_general(a, b, (((1,), (0,)), ((), ())), preferred_element_type=f32)


def dot_nt(a, b):
    return lax.dot_general(a, b, (((1,), (1,)), ((), ())), preferred_element_type=f32)


def dot_tn(a, b):
    return lax.dot_general(a, b, (((0,), (0,)), ((), ())), preferred_element_type=f32)


def half_masks():
    lane = lax.broadcasted_iota(jnp.int32, (1, LANES), 1)
    low = (lane < HEAD_DIM).astype(f32)
    return low.astype(bf16), (1.0 - low).astype(bf16)


def pieces(value):
    lane = lax.broadcasted_iota(jnp.int32, value.shape, 1) % HEAD_DIM
    high = value.astype(bf16).astype(f32)
    rest = value - high
    middle = rest.astype(bf16).astype(f32)
    last = rest - middle
    return jnp.where(
        lane == 2, high, jnp.where(lane == 3, middle, jnp.where(lane == 4, last, 0.0))
    )


def stacked(block, low, high):
    return jnp.concatenate([block * low, block * high], axis=0)


def toeplitz(row):
    wide = jnp.broadcast_to(row, (LANES, SPAN))
    return pltpu.roll(wide, 0, 1, stride=1, stride_axis=0)[:, :SEQ]


def attend_forward_kernel(ranges, biased, *refs):
    if biased:
        q_ref, k_ref, v_ref, qa_ref, ka_ref, g_ref, o_ref, l_ref, slab = refs

        @pl.when(pl.program_id(1) == 0)
        def _():
            slab[0:LANES] = toeplitz(g_ref[0, 0:1, :])
            slab[LANES : 2 * LANES] = toeplitz(g_ref[0, 1:2, :])
    else:
        q_ref, k_ref, v_ref, qa_ref, ka_ref, o_ref, l_ref = refs
    low, high = half_masks()
    keys = jnp.concatenate([k_ref[...], ka_ref[...]], axis=1)
    values = jnp.concatenate([v_ref[...], jnp.ones((SEQ, LANES), bf16)], axis=1)
    lane = lax.broadcasted_iota(jnp.int32, (LANES, LANES), 1)
    for block, (start, stop) in enumerate(ranges):
        rows = slice(block * LANES, (block + 1) * LANES)
        extra = qa_ref[rows, :]
        left = jnp.concatenate(
            [stacked(q_ref[rows, :], low, high), jnp.concatenate([extra, extra], axis=0)], axis=1
        )
        scores = dot_nt(left, keys[start:stop])
        if biased:
            scores = scores + slab[:, SEQ - (stop - start) :]
        top = jnp.max(scores, axis=1, keepdims=True)
        expd = jnp.exp(scores - top)
        mixed = dot_nn(expd.astype(bf16), values[start:stop])
        total = mixed[:, LANES:]
        mixed = mixed[:, :LANES] / total
        o_ref[rows, :] = jnp.where(lane < HEAD_DIM, mixed[:LANES], mixed[LANES:]).astype(bf16)
        negative = pieces(-(top + jnp.log(total)))
        l_ref[rows, :] = jnp.where(lane < HEAD_DIM, negative[:LANES], negative[LANES:]).astype(bf16)


def attend_forward(q, q_at, k, k_at, v, v_at, q_extra, k_extra, g, ranges):
    tokens = q.shape[0]
    sequences = tokens // SEQ
    biased = g is not None

    def block(at):
        return pl.BlockSpec((SEQ, LANES), lambda p, s: (s, at + p))

    shared = pl.BlockSpec((SEQ, LANES), lambda p, s: (s, 0))
    in_specs = [block(q_at), block(k_at), block(v_at), shared, shared]
    args = [q, k, v, q_extra, k_extra]
    scratch = []
    if biased:
        in_specs.append(pl.BlockSpec((1, 2, SPAN), lambda p, s: (p, 0, 0)))
        args.append(g)
        scratch.append(pltpu.VMEM((2 * LANES, SEQ), f32))
    seen = sum(stop - start for start, stop in ranges)
    return pl.pallas_call(
        partial(attend_forward_kernel, ranges, biased),
        grid=(PAIRS, sequences),
        in_specs=in_specs,
        out_specs=[block(0), block(0)],
        out_shape=[jax.ShapeDtypeStruct((tokens, INNER), bf16)] * 2,
        scratch_shapes=scratch,
        compiler_params=pltpu.CompilerParams(vmem_limit_bytes=VMEM_LIMIT),
        cost_estimate=pl.CostEstimate(
            flops=2 * 2 * PAIRS * sequences * seen * 256 * 256,
            bytes_accessed=tokens * INNER * 10,
            transcendentals=PAIRS * sequences * seen * 256,
        ),
    )(*args)


def attend_backward_kernel(ranges, biased, waits, *refs):
    refs = refs[waits:]
    if biased:
        (q_ref, k_ref, v_ref, qa_ref, ka_ref, l_ref, o_ref, d_ref, g_ref) = refs[:9]
        out_ref, rel_ref, dk, dv, slab, dslab = refs[9:]

        @pl.when(pl.program_id(1) == 0)
        def _():
            slab[:, 0:LANES] = toeplitz(g_ref[0, 0:1, :]).T
            slab[:, LANES : 2 * LANES] = toeplitz(g_ref[0, 1:2, :]).T
            dslab[...] = jnp.zeros_like(dslab)
    else:
        (q_ref, k_ref, v_ref, qa_ref, ka_ref, l_ref, o_ref, d_ref) = refs[:8]
        dq_ref, out_ref, dk, dv = refs[8:]
    low, high = half_masks()
    low_lane = lax.broadcasted_iota(jnp.int32, (LANES, LANES), 1) < HEAD_DIM
    low_row = lax.broadcasted_iota(jnp.int32, (LANES, LANES), 0) < HEAD_DIM
    keys = jnp.concatenate([k_ref[...], ka_ref[...]], axis=1)
    values = jnp.concatenate([v_ref[...], ka_ref[...]], axis=1)
    keys_t = k_ref[...].T
    dk[...] = jnp.zeros_like(dk)
    dv[...] = jnp.zeros_like(dv)
    for block, (start, stop) in enumerate(ranges):
        rows = slice(block * LANES, (block + 1) * LANES)
        seen = slice(start, stop)
        q2 = stacked(q_ref[rows, :], low, high)
        extra = qa_ref[rows, :]
        totals = l_ref[rows, :]
        q_right = jnp.concatenate(
            [q2, jnp.concatenate([extra + totals * low, extra + totals * high], axis=0)], axis=1
        )
        scores = dot_nt(keys[seen], q_right)
        if biased:
            scores = scores + slab[SEQ - (stop - start) :, :]
        probs = jnp.exp(scores)
        grad = d_ref[rows, :]
        d2 = stacked(grad, low, high)
        product = grad.astype(f32) * o_ref[rows, :].astype(f32)
        sum_low = jnp.sum(jnp.where(low_lane, product, 0.0), axis=1, keepdims=True)
        sum_high = jnp.sum(jnp.where(low_lane, 0.0, product), axis=1, keepdims=True)
        delta = pieces(
            -jnp.concatenate(
                [
                    jnp.broadcast_to(sum_low, (LANES, LANES)),
                    jnp.broadcast_to(sum_high, (LANES, LANES)),
                ],
                axis=0,
            )
        ).astype(bf16)
        lows = jnp.concatenate([delta[:LANES] * low, delta[LANES:] * high], axis=0)
        d_right = jnp.concatenate([d2, lows], axis=1)
        grad_scores = probs * dot_nt(values[seen], d_right)
        probs16 = probs.astype(bf16)
        scores16 = grad_scores.astype(bf16)
        dv[seen, :] += dot_nn(probs16, d2)
        dk[seen, :] += dot_nn(scores16, q2)
        dq = dot_nn(keys_t[:, seen], scores16)
        dq = jnp.where(low_row, dq[:, :LANES], dq[:, LANES:]).T.astype(bf16)
        if biased:
            out_ref[0, rows, :] = dq
            dslab[SEQ - (stop - start) :, :] += grad_scores
        else:
            dq_ref[rows, :] = dq
    first = 1 if biased else 0
    out_ref[first] = dk[...].astype(bf16)
    out_ref[first + 1] = dv[...].astype(bf16)
    if biased:

        @pl.when(pl.program_id(1) == pl.num_programs(1) - 1)
        def _():
            for head in range(2):
                square = dslab[:, head * LANES : (head + 1) * LANES].T
                wide = jnp.concatenate([square, jnp.zeros((LANES, LANES), f32)], axis=1)
                half = LANES // 2
                while half >= 1:
                    wide = wide[:half] + pltpu.roll(wide[half:], SPAN - half, 1)
                    half //= 2
                rel_ref[0, head : head + 1, :] = wide


def attend_backward(q, q_at, k, k_at, v, v_at, q_extra, k_extra, lows, mixed, grad, g, ranges, after=()):
    tokens = q.shape[0]
    sequences = tokens // SEQ
    biased = g is not None

    def block(at):
        return pl.BlockSpec((SEQ, LANES), lambda p, s: (s, at + p))

    shared = pl.BlockSpec((SEQ, LANES), lambda p, s: (s, 0))
    in_specs = [block(q_at), block(k_at), block(v_at), shared, shared, block(0), block(0), block(0)]
    args = [q, k, v, q_extra, k_extra, lows, mixed, grad]
    scratch = [pltpu.VMEM((SEQ, LANES), f32), pltpu.VMEM((SEQ, LANES), f32)]
    if biased:
        in_specs.append(pl.BlockSpec((1, 2, SPAN), lambda p, s: (p, 0, 0)))
        args.append(g)
        scratch += [pltpu.VMEM((SEQ, 2 * LANES), f32)] * 2
        out_specs = [
            pl.BlockSpec((3, SEQ, LANES), lambda p, s: (0, s, p)),
            pl.BlockSpec((1, 2, SPAN), lambda p, s: (p, 0, 0)),
        ]
        out_shape = [
            jax.ShapeDtypeStruct((3, tokens, INNER), bf16),
            jax.ShapeDtypeStruct((PAIRS, 2, SPAN), f32),
        ]
    else:
        out_specs = [block(0), pl.BlockSpec((2, SEQ, LANES), lambda p, s: (0, s, p))]
        out_shape = [
            jax.ShapeDtypeStruct((tokens, INNER), bf16),
            jax.ShapeDtypeStruct((2, tokens, INNER), bf16),
        ]
    seen = sum(stop - start for start, stop in ranges)
    return pl.pallas_call(
        partial(attend_backward_kernel, ranges, biased, len(after)),
        grid=(PAIRS, sequences),
        in_specs=[pl.BlockSpec(memory_space=pl.ANY)] * len(after) + in_specs,
        out_specs=out_specs,
        out_shape=out_shape,
        scratch_shapes=scratch,
        compiler_params=pltpu.CompilerParams(vmem_limit_bytes=VMEM_LIMIT),
        cost_estimate=pl.CostEstimate(
            flops=5 * 2 * PAIRS * sequences * seen * 256 * 256,
            bytes_accessed=tokens * INNER * 20,
            transcendentals=PAIRS * sequences * seen * 256,
        ),
    )(*after, *args)


def shares(core, value, keep_ref, send_ref, *at):
    rows, cols = value.shape
    parts = value.astype(bf16).reshape(2, 2, rows // 4, cols)
    for y in range(2):
        place = (y,) + at
        keep_ref[place] = jnp.where(core == 0, parts[y, 0], parts[y, 1])
        send_ref[place] = jnp.where(core == 0, parts[y, 1], parts[y, 0])


def feed_forward_kernel(
    core_ref, x_ref, gain_ref, dout_ref, wg_ref, wu_ref, wo_ref,
    layer_ref, gx_ref, gx16_ref, gain_grad_ref, gk_ref, gs_ref, ok_ref, os_ref,
    n3, n3t, acc, dn, hid, dgate, dup,
):
    step = pl.program_id(0)
    tokens = x_ref.shape[0]
    chunks = tokens // ROWS

    @pl.when(step == 0)
    def _():
        gain = gain_ref[...]
        for chunk in range(chunks):
            rows = slice(chunk * ROWS, (chunk + 1) * ROWS)
            x = x_ref[rows, :]
            factor = lax.rsqrt(jnp.mean(x * x, -1, keepdims=True) + eps)
            normed = (x * factor * gain).astype(bf16)
            n3[rows, :] = normed
            n3t[:, rows] = normed.T
            acc[rows, :] = jnp.zeros((ROWS, D), f32)
            dn[rows, :] = jnp.zeros((ROWS, D), f32)

    c = math.sqrt(2.0 / math.pi)
    for chunk in range(chunks):
        rows = slice(chunk * ROWS, (chunk + 1) * ROWS)
        normed = n3[rows, :]
        gate = dot_nn(normed, wg_ref[...])
        up = dot_nn(normed, wu_ref[...])
        dhidden = dot_nt(dout_ref[rows, :], wo_ref[...]).astype(bf16).astype(f32)
        square = gate * gate
        t = jnp.tanh(c * gate * (1.0 + 0.044715 * square))
        half = 0.5 * (1.0 + t)
        act = gate * half
        slope = half + (0.5 * c) * gate * (1.0 - t * t) * (1.0 + (3.0 * 0.044715) * square)
        hid[rows, :] = (act * up).astype(bf16)
        dgate[rows, :] = (dhidden * up * slope).astype(bf16)
        dup[rows, :] = (dhidden * act).astype(bf16)
        acc[rows, :] += dot_nn(hid[rows, :], wo_ref[...])
        dn[rows, :] += dot_nt(dgate[rows, :], wg_ref[...]) + dot_nt(dup[rows, :], wu_ref[...])
    core = core_ref[0]
    shares(core, dot_nn(n3t[...], dgate[...]), gk_ref, gs_ref, 0)
    shares(core, dot_nn(n3t[...], dup[...]), gk_ref, gs_ref, 1)
    out_grad = dot_tn(hid[...], dout_ref[...]).astype(bf16)

    @pl.when(step % 2 == core)
    def _():
        ok_ref[0] = out_grad

    @pl.when(step % 2 != core)
    def _():
        os_ref[0] = out_grad

    @pl.when(step == pl.num_programs(0) - 1)
    def _():
        gain = gain_ref[...]
        total = jnp.zeros((1, D), f32)
        for chunk in range(chunks):
            rows = slice(chunk * ROWS, (chunk + 1) * ROWS)
            x = x_ref[rows, :]
            layer_ref[rows, :] = (x + acc[rows, :]).astype(bf16)
            factor = lax.rsqrt(jnp.mean(x * x, -1, keepdims=True) + eps)
            d = dn[rows, :]
            weighted = d * gain
            total += jnp.sum(d * x * factor, axis=0, keepdims=True)
            back = factor * weighted - x * (
                factor * factor * factor * jnp.mean(weighted * x, -1, keepdims=True)
            )
            gx = dout_ref[rows, :].astype(f32) + back
            gx_ref[rows, :] = gx
            gx16_ref[rows, :] = gx.astype(bf16)
        gain_grad_ref[...] = total


def feed_forward(core, x, gain, dout, ff_in, ff_out):
    tokens = x.shape[0]
    steps = FF // FF_BLOCK
    whole = pl.BlockSpec((tokens, D), lambda f, c: (0, 0))
    row = pl.BlockSpec((1, D), lambda f, c: (0, 0))
    columns = pl.BlockSpec((D, FF_BLOCK), lambda f, c: (0, f))
    in_share = pl.BlockSpec((2, 2, D // 4, FF_BLOCK), lambda f, c: (0, 0, 0, f))
    out_share = pl.BlockSpec((1, FF_BLOCK, D), lambda f, c: (f // 2, 0, 0))
    in_type = jax.ShapeDtypeStruct((2, 2, D // 4, FF), bf16)
    out_type = jax.ShapeDtypeStruct((2, FF_BLOCK, D), bf16)
    return pl.pallas_call(
        feed_forward_kernel,
        grid_spec=pltpu.PrefetchScalarGridSpec(
            num_scalar_prefetch=1,
            grid=(steps,),
            in_specs=[
                whole,
                row,
                whole,
                columns,
                pl.BlockSpec((D, FF_BLOCK), lambda f, c: (0, steps + f)),
                pl.BlockSpec((FF_BLOCK, D), lambda f, c: (f, 0)),
            ],
            out_specs=[
                whole, whole, whole, row, in_share, in_share, out_share, out_share,
            ],
            scratch_shapes=[
                pltpu.VMEM((tokens, D), bf16),
                pltpu.VMEM((D, tokens), bf16),
                pltpu.VMEM((tokens, D), f32),
                pltpu.VMEM((tokens, D), f32),
                pltpu.VMEM((tokens, FF_BLOCK), bf16),
                pltpu.VMEM((tokens, FF_BLOCK), bf16),
                pltpu.VMEM((tokens, FF_BLOCK), bf16),
            ],
        ),
        out_shape=[
            jax.ShapeDtypeStruct((tokens, D), bf16),
            jax.ShapeDtypeStruct((tokens, D), f32),
            jax.ShapeDtypeStruct((tokens, D), bf16),
            jax.ShapeDtypeStruct((1, D), f32),
            in_type, in_type, out_type, out_type,
        ],
        compiler_params=pltpu.CompilerParams(vmem_limit_bytes=VMEM_LIMIT),
        cost_estimate=pl.CostEstimate(
            flops=18 * tokens * D * FF,
            bytes_accessed=tokens * D * 16 + 12 * D * FF,
            transcendentals=tokens * FF,
        ),
    )(core, x, gain, dout, ff_in, ff_in, ff_out)


def norm_back_kernel(normed, onward, waits, *refs):
    refs = refs[waits:]
    grad_ref, w_ref = refs[:2]
    total = None
    for part in range(grad_ref.shape[0]):
        term = dot_nt(grad_ref[part], w_ref[:, part * D : (part + 1) * D])
        total = term if total is None else total + term
    if not normed:
        refs[2][...] = total
        return
    x_ref, gain_ref, up_ref = refs[2:5]
    refs = refs[5:]
    if onward:
        next_ref, out_ref, gain_grad_ref, out16_ref, onward_ref = refs
    else:
        out_ref, gain_grad_ref = refs
    x = x_ref[...].astype(f32)
    factor = lax.rsqrt(jnp.mean(x * x, -1, keepdims=True) + eps)
    weighted = total * gain_ref[...]
    grad_gain = jnp.sum(total * x * factor, axis=0, keepdims=True)

    @pl.when(pl.program_id(0) == 0)
    def _():
        gain_grad_ref[...] = jnp.zeros_like(gain_grad_ref)

    gain_grad_ref[...] += grad_gain
    scale = factor * factor * factor * jnp.mean(weighted * x, -1, keepdims=True)
    out = up_ref[...] + factor * weighted - x * scale
    out_ref[...] = out
    if onward:
        out16 = out.astype(bf16)
        out16_ref[...] = out16
        onward_ref[...] = dot_nt(out16, next_ref[...]).astype(bf16)


def norm_back(grads, w, x=None, gain=None, upstream=None, w_next=None, after=()):
    if grads.ndim == 2:
        grads = grads[None]
    parts, tokens, _ = grads.shape
    block = pl.BlockSpec((ROWS, D), lambda i: (i, 0))
    row = pl.BlockSpec((1, D), lambda i: (0, 0))
    in_specs = [pl.BlockSpec(memory_space=pl.ANY)] * len(after)
    in_specs += [
        pl.BlockSpec((parts, ROWS, D), lambda i: (0, i, 0)),
        pl.BlockSpec((D, parts * D), lambda i: (0, 0)),
    ]
    args = [*after, grads, w]
    wide = jax.ShapeDtypeStruct((tokens, D), f32)
    half = jax.ShapeDtypeStruct((tokens, D), bf16)
    out_specs, out_shape = [block], [wide]
    if x is not None:
        in_specs += [block, row, block]
        args += [x, gain, upstream]
        out_specs.append(row)
        out_shape.append(jax.ShapeDtypeStruct((1, D), f32))
        if w_next is not None:
            in_specs.append(pl.BlockSpec((D, D), lambda i: (0, 0)))
            args.append(w_next)
            out_specs += [block, block]
            out_shape += [half, half]
    return pl.pallas_call(
        partial(norm_back_kernel, x is not None, w_next is not None, len(after)),
        grid=(tokens // ROWS,),
        in_specs=in_specs,
        out_specs=out_specs,
        out_shape=out_shape,
        compiler_params=pltpu.CompilerParams(vmem_limit_bytes=VMEM_LIMIT),
        cost_estimate=pl.CostEstimate(
            flops=2 * tokens * D * D * (parts + (w_next is not None)),
            bytes_accessed=tokens * D * (2 * parts + 12) + D * D * 2 * parts,
            transcendentals=0,
        ),
    )(*args)


def weight_grad_kernel(counts, waits, core_ref, *refs):
    refs = refs[waits:]
    lefts, rights = refs[0 : len(counts)], refs[len(counts) : 2 * len(counts)]
    keep_ref, send_ref, left_t = refs[2 * len(counts) :]
    step = pl.program_id(0)
    core = core_ref[0]
    at = 0
    for left, right, count in zip(lefts, rights, counts):

        @pl.when(step == at)
        def _():
            left_t[...] = left[...].T

        @pl.when((step >= at) & (step < at + count))
        def _():
            block = right[...] if len(right.shape) == 2 else right[0]
            shares(core, dot_nn(left_t[...], block), keep_ref, send_ref)

        at += count


def weight_grad(core, terms, after=()):
    tokens = terms[0][0].shape[0]
    counts = []
    rights = []
    at = 0
    for _, right in terms:
        count = right.shape[-1] * (right.shape[0] if right.ndim == 3 else 1) // ROWS
        blocks = right.shape[-1] // ROWS

        def place(j, c, at=at, count=count, blocks=blocks, deep=right.ndim == 3):
            j = jnp.clip(j - at, 0, count - 1)
            return (j // blocks, 0, j % blocks) if deep else (0, j)

        shape = (1, tokens, ROWS) if right.ndim == 3 else (tokens, ROWS)
        rights.append(pl.BlockSpec(shape, place))
        counts.append(count)
        at += count
    share = pl.BlockSpec((2, D // 4, ROWS), lambda j, c: (0, 0, j))
    out_type = jax.ShapeDtypeStruct((2, D // 4, at * ROWS), bf16)
    return pl.pallas_call(
        partial(weight_grad_kernel, counts, len(after)),
        grid_spec=pltpu.PrefetchScalarGridSpec(
            num_scalar_prefetch=1,
            grid=(at,),
            in_specs=[pl.BlockSpec(memory_space=pl.ANY)] * len(after)
            + [pl.BlockSpec((tokens, D), lambda j, c: (0, 0))] * len(terms)
            + rights,
            out_specs=[share, share],
            scratch_shapes=[pltpu.VMEM((D, tokens), bf16)],
        ),
        out_shape=[out_type, out_type],
        compiler_params=pltpu.CompilerParams(vmem_limit_bytes=VMEM_LIMIT),
        cost_estimate=pl.CostEstimate(
            flops=2 * tokens * D * ROWS * at,
            bytes_accessed=tokens * (D * len(terms) + ROWS * at) * 2 + D * ROWS * at * 2,
            transcendentals=0,
        ),
    )(core, *after, *[left for left, _ in terms], *[right for _, right in terms])


def exchange(array, axis, size, bit):
    return lax.ppermute(array, axis, [(i, i ^ bit) for i in range(size)])


def part_of(array, dim, index):
    half = array.shape[dim] // 2
    return lax.dynamic_slice_in_dim(array, index * half, half, dim)


class Chain:
    def __init__(self, keep, send, sizes, dim, order):
        self.shards, self.reps = sizes
        self.dim = dim
        self.shard = lax.axis_index("shard")
        self.rep = lax.axis_index("rep")
        self.bits = [1 << b for b in range(self.reps.bit_length() - 1)]
        steps = []
        for name in order:
            steps += [("shard", 2)] if name == "y" else [("rep", bit) for bit in self.bits]
        self.steps = steps
        self.keep = keep
        self.got = exchange(send, "shard", self.shards, 1)
        self.at = 0

    def own(self):
        return (self.keep.astype(f32) + self.got.astype(f32)).astype(bf16)

    def advance(self):
        own = self.own()
        axis, bit = self.steps[self.at]
        self.at += 1
        index = lax.axis_index(axis)
        mine = (index // bit) % 2
        dim = 0 if axis == "shard" else self.dim
        size = self.shards if axis == "shard" else self.reps
        self.keep = part_of(own, dim, mine)
        self.got = exchange(part_of(own, dim, 1 - mine), axis, size, bit)
        return self.got

    def finish(self, permutes):
        while self.at < len(self.steps):
            self.advance()
        own = self.own()
        if permutes:
            for bit in reversed(self.bits):
                got = exchange(own, "rep", self.reps, bit)
                mine = (self.rep // bit) % 2
                low = jnp.where(mine == 0, own, got)
                high = jnp.where(mine == 0, got, own)
                own = jnp.concatenate([low, high], axis=self.dim)
            return own[0].astype(f32)
        full = lax.all_gather(own[0], "rep", axis=0)
        width = len(self.bits)
        shape = own[0].shape
        dim = self.dim - 1
        full = full.reshape((2,) * width + shape)
        rest = [width + d for d in range(len(shape))]
        turned = list(reversed(range(width)))
        full = full.transpose(rest[:dim] + turned + rest[dim:])
        return full.reshape(shape[:dim] + (-1,) + shape[dim + 1 :]).astype(f32)


def bias_rows(table):
    lane = np.arange(SPAN)
    distance = np.where(lane < SEQ, SEQ - LANES - lane, 2 * SEQ - lane)
    bucket = np.zeros(SPAN, np.int64)
    for edge in bucket_edges:
        bucket += distance >= edge
    onehot = np.zeros((SPAN, NUM_BUCKETS), np.float32)
    valid = (distance >= 0) & (distance < SEQ)
    onehot[np.arange(SPAN)[valid], bucket[valid]] = 1.0
    return onehot, valid


def norm_forward(inputs, gain):
    factor = lax.rsqrt(jnp.mean(inputs * inputs, -1, keepdims=True) + eps)
    return factor, inputs * factor * gain


def local(
    sizes,
    hidden_in,
    enc_states,
    dec_segments,
    enc_segments,
    out_grad,
    gains,
    rel_table,
    self_qkv,
    self_out,
    cross_q,
    cross_kv,
    cross_out,
    ff_in,
    ff_out,
):
    shards, reps = sizes
    own_rows = D // shards
    own_buckets = NUM_BUCKETS // shards
    small = jnp.zeros((own_rows, LANES), bf16)
    small = small.at[:, 0:3].set(gains.T)
    small = small.at[0:own_buckets, 16 : 16 + HEADS].set(rel_table)
    self_set = lax.all_gather(
        jnp.concatenate([self_qkv, self_out, small], axis=1), "shard", axis=0, tiled=True
    )
    cross_set = lax.all_gather(
        jnp.concatenate([cross_kv, cross_q, cross_out], axis=1), "shard", axis=0, tiled=True
    )
    ff_in = lax.all_gather(ff_in, "shard", axis=0, tiled=True)
    ff_out = lax.all_gather(ff_out, "shard", axis=0, tiled=True)
    w_qkv = self_set[:, : 3 * INNER]
    w_self_out = self_set[:, 3 * INNER : 4 * INNER]
    w_kv = cross_set[:, : 2 * INNER]
    w_cq = cross_set[:, 2 * INNER : 3 * INNER]
    w_cross_out = cross_set[:, 3 * INNER :]
    gains = self_set[:, 4 * INNER : 4 * INNER + 3].T.astype(f32)
    table = self_set[:, 4 * INNER + 16 : 4 * INNER + 16 + HEADS]
    table = table.reshape(shards, own_rows, HEADS)[:, :own_buckets].reshape(NUM_BUCKETS, HEADS)

    lane = jnp.arange(LANES, dtype=jnp.int32)[None, :]
    dec_ids = dec_segments[:, None]
    enc_ids = enc_segments[:, None]
    ones = ((lane % HEAD_DIM >= 2) & (lane % HEAD_DIM <= 4)).astype(f32)

    def key_extra(ids):
        return jnp.where(lane < 2, jnp.where(lane != ids, masked_score, 0.0), ones).astype(bf16)

    q_extra = ((lane < 2) & (lane == dec_ids)).astype(bf16)
    self_extra = key_extra(dec_ids)
    cross_extra = key_extra(enc_ids)
    onehot, valid = bias_rows(table)
    g = jnp.einsum("ub,bh->hu", onehot.astype(bf16), table, preferred_element_type=f32)
    g = jnp.where(valid[None], g, masked_score).reshape(PAIRS, 2, SPAN)

    inputs = hidden_in.astype(f32)
    factor_one, normed_one = norm_forward(inputs, gains[0])
    normed_one = normed_one.astype(bf16)
    qkv = dot_nn(normed_one, w_qkv).astype(bf16)
    ckv = dot_nn(enc_states, w_kv).astype(bf16)
    attn_one, lows_one = attend_forward(
        qkv, 0, qkv, PAIRS, qkv, 2 * PAIRS, q_extra, self_extra, g, SELF_RANGES
    )
    first = inputs + dot_nn(attn_one, w_self_out)
    factor_two, normed_two = norm_forward(first, gains[1])
    normed_two = normed_two.astype(bf16)
    cq = dot_nn(normed_two, w_cq).astype(bf16)
    attn_two, lows_two = attend_forward(
        cq, 0, ckv, 0, ckv, PAIRS, q_extra, cross_extra, None, CROSS_RANGES
    )
    second = first + dot_nn(attn_two, w_cross_out)

    core = (lax.axis_index("shard") % 2).astype(jnp.int32).reshape(1)
    layer_out, grad_second, out_two, gain_three, in_keep, in_send, out_keep, out_send = feed_forward(
        core, second, gains[2:3], out_grad, ff_in, ff_out
    )
    ff_in_chain = Chain(in_keep, in_send, sizes, 3, "yr")
    ff_out_chain = Chain(out_keep, out_send, sizes, 1, "ry")
    grad_attn_two = dot_nt(out_two, w_cross_out).astype(bf16)
    grad_cq, grad_ckv = attend_backward(
        cq, 0, ckv, 0, ckv, PAIRS, q_extra, cross_extra, lows_two, attn_two, grad_attn_two,
        None, CROSS_RANGES, after=[ff_in_chain.got, ff_out_chain.got],
    )
    ff_in_chain.advance()
    ff_out_chain.advance()
    cross_keep, cross_send = weight_grad(
        core,
        [(enc_states, grad_ckv), (normed_two, grad_cq), (attn_two, out_two)],
        after=[ff_out_chain.got],
    )
    cross_chain = Chain(cross_keep, cross_send, sizes, 2, "yr")
    ff_out_chain.advance()
    grad_first, gain_two, out_one, grad_attn_one = norm_back(
        grad_cq, w_cq, first, gains[1:2], grad_second, w_self_out,
        after=[ff_in_chain.got, cross_keep],
    )
    ff_in_chain.advance()
    grad_qkv, rel_part = attend_backward(
        qkv, 0, qkv, PAIRS, qkv, 2 * PAIRS, q_extra, self_extra, lows_one, attn_one,
        grad_attn_one, g, SELF_RANGES, after=[cross_chain.got, ff_out_chain.got],
    )
    cross_chain.advance()
    ff_out_chain.advance()
    self_keep, self_send = weight_grad(
        core, [(normed_one, grad_qkv), (attn_one, out_one)],
        after=[ff_in_chain.got, ff_out_chain.got, cross_chain.got],
    )
    self_chain = Chain(self_keep, self_send, sizes, 2, "yr")
    ff_in_chain.advance()
    ff_out_chain.advance()
    cross_chain.advance()
    (enc_grad,) = norm_back(grad_ckv, w_kv, after=[self_keep])
    in_grad, gain_one = norm_back(
        grad_qkv, w_qkv, hidden_in, gains[0:1], grad_first, after=[self_chain.got, enc_grad]
    )
    self_chain.advance()
    ff_in_grad = ff_in_chain.finish(False)
    ff_in_grad = jnp.concatenate([ff_in_grad[0], ff_in_grad[1]], axis=1)
    ff_out_grad = ff_out_chain.finish(False)
    cross_grad = cross_chain.finish(True)
    self_grad = self_chain.finish(True)

    table_part = jnp.einsum(
        "hu,ub->bh",
        rel_part.reshape(HEADS, SPAN),
        onehot,
        precision=lax.Precision.HIGHEST,
        preferred_element_type=f32,
    )
    tiny = jnp.zeros((8, D), f32)
    tiny = tiny.at[0].set(gain_one[0]).at[1].set(gain_two[0]).at[2].set(gain_three[0])
    tiny = tiny.at[3, : NUM_BUCKETS * HEADS].set(table_part.reshape(-1))
    tiny = jnp.sum(lax.all_gather(tiny, ("rep", "shard"), axis=0), axis=0)
    shard = lax.axis_index("shard")
    gains_grad = lax.dynamic_slice_in_dim(tiny[:3], shard * own_rows, own_rows, 1)
    rel_table_grad = lax.dynamic_slice_in_dim(
        tiny[3, : NUM_BUCKETS * HEADS].reshape(NUM_BUCKETS, HEADS), shard * own_buckets, own_buckets, 0
    )
    return (
        layer_out,
        in_grad,
        enc_grad,
        gains_grad,
        rel_table_grad,
        self_grad[:, : 3 * INNER],
        self_grad[:, 3 * INNER :],
        cross_grad[:, 2 * INNER : 3 * INNER],
        cross_grad[:, : 2 * INNER],
        cross_grad[:, 3 * INNER :],
        ff_in_grad,
        ff_out_grad,
    )


def solution(mesh):
    tokens = P(("rep", "shard"), None)
    ids = P(("rep", "shard"))
    rows = P("shard", None)
    columns = P(None, "shard")
    in_specs = (tokens, tokens, ids, ids, tokens, columns) + (rows,) * 8
    out_specs = (tokens, tokens, tokens, columns) + (rows,) * 8
    sizes = (mesh.shape["shard"], mesh.shape["rep"])
    return jax.shard_map(
        partial(local, sizes), mesh=mesh, in_specs=in_specs, out_specs=out_specs, check_vma=False
    )
```

time: 987 us -> 598 us (0.61)
  blocking collectives: 410 us -> 80.4 us
  matrix products: 302 us -> 32.4 us
  Pallas kernels: 0 us -> 181 us
  waiting for transfers between devices: 24.5 us -> 165 us
  local copies, waits for them, and re-layouts: 146 us -> 45.3 us
  other arithmetic: 81.6 us -> 34.3 us
  starting transfers between devices: 1.35 us -> 34 us
    psum x1 -> x0, blocking collectives: 383 us -> none  [reduce_end(): lax.psum((shares[0], shares[1], shares[2], shares[3], shares[4], shares[5...]
    dot_general x35 -> x8, matrix products: 302 us -> 32.4 us  [the longest x5 27.2 us: dot_nn(): lax.dot_general(a, b, (((1,), (0,)), ((), ())), preferred_element_type=f32)]
    pallas_call x0 -> x10, Pallas kernels: none -> 181 us  [the longest x2 49.8 us: attend_backward(): pl.pallas_call(partial(attend_backward_kernel, ranges, biased, len(after)...]
    all_gather x7 -> x5, waiting for transfers between devices: 0.03 us -> 90.4 us  [the longest x1 34.3 us: local(): lax.all_gather(jnp.concatenate([self_qkv, self_out, small], axis=1), 'sha...]
    all_gather x1 -> x2, blocking collectives: 5.35 us -> 80.4 us  [the longest x1 46.3 us: local(): tiny = jnp.sum(lax.all_gather(tiny, ('rep', 'shard'), axis=0), axis=0)]
    ppermute x0 -> x26, waiting for transfers between devices: none -> 73.6 us  [exchange(): return lax.ppermute(array, axis, [(i, i ^ bit) for i in range(size)])]
    reduce_sum x3 -> x1, other arithmetic: 48.4 us -> 0.06 us  [local(): tiny = jnp.sum(lax.all_gather(tiny, ('rep', 'shard'), axis=0), axis=0)]
    ppermute x0 -> x26, starting transfers between devices: none -> 33.8 us  [exchange(): return lax.ppermute(array, axis, [(i, i ^ bit) for i in range(size)])]
  transfers between devices with their start and end apart: 14 -> 31, of which waited for: 1 -> 13; matrix products, arithmetic and copies ran while one was open for 49% -> 17% of each run, Pallas kernels for 0% -> 24%
where the time goes in v1:
time: 598 us; the launch traced here: 588 us
  Pallas kernels  181 us (30%)
  waiting for transfers between devices  165 us (28%)
  blocking collectives  80.4 us (13%)
  local copies, waits for them, and re-layouts  45.3 us (8%)
  other arithmetic  34.3 us (6%)
  starting transfers between devices  34 us (6%)
  matrix products  32.4 us (5%)
  between operations  15 us (3%)
    ppermute x26, waiting for transfers between devices, exchange(): return lax.ppermute(array, axis, [(i, i ^ bit) for i in range(size)])  73.6 us
    pallas_call x2, Pallas kernels, attend_backward(): pl.pallas_call(partial(attend_backward_kernel, ranges, biased, len(after)...  49.8 us
    all_gather x1, blocking collectives, local(): tiny = jnp.sum(lax.all_gather(tiny, ('rep', 'shard'), axis=0), axis=0)  46.3 us
    pallas_call x1, Pallas kernels, feed_forward(): pl.pallas_call(feed_forward_kernel, grid_spec=pltpu.PrefetchScalarGridSpe...  42.2 us
    all_gather x1, waiting for transfers between devices, local(): lax.all_gather(jnp.concatenate([self_qkv, self_out, small], axis=1), 'sha...  34.3 us
    all_gather x1, blocking collectives, finish(): full = lax.all_gather(own[0], 'rep', axis=0)  34.1 us
    pallas_call x2, Pallas kernels, attend_forward(): pl.pallas_call(partial(attend_forward_kernel, ranges, biased), grid=(PAIR...  34.1 us
    ppermute x26, starting transfers between devices, exchange(): return lax.ppermute(array, axis, [(i, i ^ bit) for i in range(size)])  33.8 us
  transfers between devices with their start and end apart: 31, of which 13 were waited for; matrix products, arithmetic and copies ran while one was open for 17% of the time, Pallas kernels for 24%

profile of v1, /device:TPU:0, one launch (start us, length us, event | category | flops | bytes accessed | tf_op | source)
XLA Modules:
  0.0 588.0 jit_solution(13019463702770332944)
XLA Ops:
  7.3 2.5 pad_maximum_fusion.2
  11.8 2.0 fusion.10
  13.9 1.8 scatter.21
  19.7 1.1 select_convert_fusion
  20.8 29.6 %all-gather.8.cloned.1.call-done = bf16[768,3072]{1,0:T(8,128)(2,1)} async-done(((bf16[192,3072]{1,0:T(8,128)(2,1)}), bf16[768,3072]{1,0:T(8,128)(2,1)}) %all-gather.8.cloned.1.call-update) | async-done | bytes 4718608 | tf_op jit(solution)/shard_map/all_gather | solution.py:646
  50.4 6.4 %fusion.refs_1_.refs_2_.refs_3_.refs_4_ = bf16[1024,1536]{1,0:T(8,128)(2,1)} fusion(bf16[1024,768]{1,0:T(8,128)(2,1)} %refs_1_.1, bf16[768,3072]{1,0:T(8,128)(2,1)} %all-gather.8.cloned.1.call-done), kind=kOutput, calls=%fused_computation.8 | convolution fusion | flops 2417491968 | bytes 7077888 | tf_op jit(solution)/shard_map/dot_general | solution.py:41
  56.8 34.3 %all-gather.6.cloned.1.call-done = bf16[768,3200]{1,0:T(8,128)(2,1)} async-done(((bf16[192,3200]{1,0:T(8,128)(2,1)}), bf16[768,3200]{1,0:T(8,128)(2,1)}) %all-gather.6.cloned.1.call-update) | async-done | bytes 4915216 | tf_op jit(solution)/shard_map/all_gather | solution.py:643
  95.2 8.0 %convolution_convert_fusion.refs_0_.refs_1_.refs_2_.refs_3_.refs_4_ = bf16[1024,2304]{1,0:T(8,128)(2,1)} fusion(bf16[1024,768]{1,0:T(8,128)(2,1)S(1)} %fusion.3.refs_3_, bf16[768,3200]{1,0:T(8,128)(2,1)} %all-gather.6.cloned.1.call-done), kind=kOutput, calls=%fused_computation.1 | convolution fusion | flops 3626237952 | bytes 9830400 | tf_op jit(solution)/shard_map/dot_general | solution.py:41
  103.2 18.3 %shard_map.256 = (bf16[1024,768]{1,0:T(8,128)(2,1)}, bf16[1024,768]{1,0:T(8,128)(2,1)}) custom-call(bf16[1024,2304]{1,0:T(8,128)(2,1)} %convolution_convert_fusion.refs_0_.refs_1_.refs_2_.refs_3_.refs_4_, bf16[1024,2304]{1,0:T(8,128)(2,1)} %convolution_convert_fusion.refs_0_.refs_1_.refs_2_.refs_3_.refs_4_, ...), custom_call_target="tpu_custom_call" | custom-call | flops 3623878656 | bytes 7864320 | tf_op jit(solution)/shard_map/pallas_call | solution.py:128
  121.5 3.2 multiply_reduce_fusion
  125.1 4.8 convolution_convert_fusion.3.refs_0_.refs_2_
  129.9 15.8 %shard_map.257 = (bf16[1024,768]{1,0:T(8,128)(2,1)}, bf16[1024,768]{1,0:T(8,128)(2,1)}) custom-call(bf16[1024,768]{1,0:T(8,128)(2,1)} %convolution_convert_fusion.3.refs_0_.refs_2_, bf16[1024,1536]{1,0:T(8,128)(2,1)} %fusion.refs_1_.refs_2_.refs_3_.refs_4_, bf16[1024,1536]{1,0:T(8,128)(2,1)} %fusion.refs_1_.refs_2_.refs_3_.refs_4_, ...), custom_call_target="tpu_custom_call" | custom-call | flops 5637144576 | bytes 7864320 | tf_op jit(solution)/shard_map/pallas_call | solution.py:128
  145.7 4.8 convolution_add_fusion.x_ref
  150.5 18.7 %all-gather.10.cloned.1.call-done.wg_ref.wu_ref = bf16[768,4096]{1,0:T(8,128)(2,1)} async-done(((bf16[192,4096]{1,0:T(8,128)(2,1)}), bf16[768,4096]{1,0:T(8,128)(2,1)}) %all-gather.10.cloned.1.call-update) | async-done | bytes 6291472 | tf_op jit(solution)/shard_map/all_gather | solution.py:649
  169.2 42.2 %shard_map.258 = (bf16[1024,768]{1,0:T(8,128)(2,1)}, f32[1024,768]{1,0:T(8,128)}, bf16[1024,768]{1,0:T(8,128)(2,1)}, f32[1,768]{1,0:T(1,128)}, bf16[2,2,192,2048...) custom-call(s32[1]{0:T(128)} %bitcast.core_ref, ...), custom_call_target="tpu_custom_call" | custom-call | flops 28991029248 | bytes 31457280 | tf_op jit(solution)/shard_map/pallas_call | solution.py:363
  211.9 3.1 collective-permute-done.3.refs_1_
  215.1 1.2 copy-done.13
  216.2 2.3 add_convert_fusion.3
  218.6 1.5 collective-permute-start.4
  220.1 4.3 convolution_convert_fusion.2.refs_9_
  224.4 13.9 %collective-permute-done.4.refs_0_ = bf16[2,256,768]{2,1,0:T(8,128)(2,1)S(1)} collective-permute-done((bf16[2,256,768]{2,1,0:T(8,128)(2,1)S(1)}, bf16[2,256,768]{2,1,0:T(8,128)(2,1)S(1)}, u32[]{:S(2)}, u32[]{:S(2)}) %collective-permute-start.4) | collective-permute-done | bytes 786464 | tf_op jit(solution)/shard_map/ppermute | solution.py:542
  239.2 1.5 collective-permute-start.5
  240.7 22.5 %shard_map.259 = (bf16[1024,768]{1,0:T(8,128)(2,1)}, bf16[2,1024,768]{2,1,0:T(8,128)(2,1)}) custom-call(bf16[2,2,192,2048]{3,2,1,0:T(8,128)(2,1)} %collective-permute-done.refs_0_, bf16[2,512,768]{2,1,0:T(8,128)(2,1)} %copy-done.13, bf16[1024,768]{1,0:T(8,128)(2,1)} %convolution_convert_fusion.3.refs_0_.refs_2_, ...), custom_call_target="tpu_custom_call" | custom-call | flops 14092861440 | bytes 15728640 | tf_op jit(solution)/shard_map/pallas_call | solution.py:255
  263.2 15.1 %shard_map.260 = (bf16[2,192,3072]{2,1,0:T(8,128)(2,1)}, bf16[2,192,3072]{2,1,0:T(8,128)(2,1)}) custom-call(s32[1]{0:T(128)} %bitcast.core_ref, bf16[2,256,768]{2,1,0:T(8,128)(2,1)} %copy-done.16, bf16[1024,768]{1,0:T(8,128)(2,1)} %refs_1_.1, bf16[1024,768]{1,0:T(8,128)(2,1)} %copy-done.12, bf16[1024,768]{1,0:T(8,128)(2,1)} %get-tuple-element.111.refs_8_.refs_3_, ...), custom_call_target="tpu_custom_call" | custom-call | flops 4831838208 | bytes 15728640 | tf_op jit(solution)/shard_map/pallas_call | solution.py:520
  279.5 2.5 collective-permute-start.6
  282.0 2.4 slice.198.refs_3_
  284.3 3.3 slice.199.refs_2_
  287.6 2.4 slice.196.refs_7_
  290.0 4.1 slice.193.refs_3_
  294.9 3.2 add_convert_fusion
  298.2 1.5 collective-permute-start.1
  303.2 34.1 %all_gather.40 = bf16[8,64,768]{2,1,0:T(8,128)(2,1)} all-gather(bf16[1,64,768]{2,1,0:T(8,128)(2,1)S(1)} %add_convert_fusion.19), channel_id=1, replica_groups=mesh['rep'=8,'shard'=4] {'rep'}, dimensions={0}, use_global_device_ids=true | all-gather | bytes 884736 | tf_op jit(solution)/shard_map/all_gather | solution.py:592
  338.7 9.2 %shard_map.261 = (f32[1024,768]{1,0:T(8,128)}, f32[1,768]{1,0:T(1,128)}, bf16[1024,768]{1,0:T(8,128)(2,1)}, bf16[1024,768]{1,0:T(8,128)(2,1)}) custom-call(bf16[1,2,192,2048]{3,2,1,0:T(8,128)(2,1)} %copy-done.7, bf16[2,192,3072]{2,1,0:T(8,128)(2,1)} %get-tuple-element.121.refs_1_, bf16[1,1024,768]{2,1,0:T(8,128)(2,1)} %bitcast.48, ...), custom_call_target="tpu_custom_call" | custom-call | flops 2415919104 | bytes 12189696 | tf_op jit(solution)/shard_map/pallas_call | solution.py:465
  347.9 12.2 %collective-permute-done.8.refs_2_ = bf16[1,192,3072]{2,1,0:T(8,128)(2,1)S(1)} collective-permute-done((bf16[1,192,3072]{2,1,0:T(8,128)(2,1)}, bf16[1,192,3072]{2,1,0:T(8,128)(2,1)S(1)}, u32[]{:S(2)}, u32[]{:S(2)}) %collective-permute-start.8) | collective-permute-done | bytes 1179680 | tf_op jit(solution)/shard_map/ppermute | solution.py:542
  361.1 1.6 collective-permute-start.17
  362.7 27.3 %shard_map.262 = (bf16[3,1024,768]{2,1,0:T(8,128)(2,1)}, f32[6,2,640]{2,1,0:T(2,128)}) custom-call(bf16[2,192,3072]{2,1,0:T(8,128)(2,1)} %copy-done.10, bf16[2,128,768]{2,1,0:T(8,128)(2,1)} %collective-permute-done.5.refs_1_, bf16[1024,2304]{1,0:T(8,128)(2,1)} %convolution_convert_fusion.refs_0_.refs_1_.refs_2_.refs_3_.refs_4_, ...), custom_call_target="tpu_custom_call" | custom-call | flops 9059696640 | bytes 15728640 | tf_op jit(solution)/shard_map/pallas_call | solution.py:255
  391.6 14.2 %shard_map.263 = (bf16[2,192,3072]{2,1,0:T(8,128)(2,1)}, bf16[2,192,3072]{2,1,0:T(8,128)(2,1)}) custom-call(s32[1]{0:T(128)} %bitcast.core_ref, bf16[1,2,192,1024]{3,2,1,0:T(8,128)(2,1)} %copy-done.17, bf16[2,64,768]{2,1,0:T(8,128)(2,1)} %copy-done.21, bf16[1,192,3072]{2,1,0:T(8,128)(2,1)} %copy-done.14, bf16[1024,768]{1,0:T(8,128)(2,1)} %copy-done.11, ...), custom_call_target="tpu_custom_call" | custom-call | flops 4831838208 | bytes 14155776 | tf_op jit(solution)/shard_map/pallas_call | solution.py:520
  408.0 1.6 collective-permute-start.23
  409.6 6.8 %collective-permute-done.19 = bf16[1,192,384]{2,1,0:T(8,128)(2,1)S(1)} collective-permute-done((bf16[1,192,384]{2,1,0:T(8,128)(2,1)S(1)}, bf16[1,192,384]{2,1,0:T(8,128)(2,1)S(1)}, u32[]{:S(2)}, u32[]{:S(2)}) %collective-permute-start.19) | collective-permute-done | bytes 147488 | tf_op jit(solution)/shard_map/ppermute | solution.py:542
  416.7 1.3 copy.70
  418.6 7.4 %collective-permute-done.20 = bf16[1,192,384]{2,1,0:T(8,128)(2,1)S(1)} collective-permute-done((bf16[1,192,384]{2,1,0:T(8,128)(2,1)S(1)}, bf16[1,192,384]{2,1,0:T(8,128)(2,1)S(1)}, u32[]{:S(2)}, u32[]{:S(2)}) %collective-permute-start.20) | collective-permute-done | bytes 147488 | tf_op jit(solution)/shard_map/ppermute | solution.py:542
  427.8 2.1 collective-permute-start.24
  429.9 7.2 %collective-permute-done.21 = bf16[1,192,768]{2,1,0:T(8,128)(2,1)S(1)} collective-permute-done((bf16[1,192,768]{2,1,0:T(8,128)(2,1)S(1)}, bf16[1,192,768]{2,1,0:T(8,128)(2,1)S(1)}, u32[]{:S(2)}, u32[]{:S(2)}) %collective-permute-start.21) | collective-permute-done | bytes 294944 | tf_op jit(solution)/shard_map/ppermute | solution.py:542
  441.9 1.2 collective-permute-start.10
  443.9 1.7 add_convert_fusion.16
  445.6 7.0 %shard_map.264.refs_1_ = f32[1024,768]{1,0:T(8,128)} custom-call(bf16[2,192,3072]{2,1,0:T(8,128)(2,1)} %get-tuple-element.129.refs_0_, bf16[2,1024,768]{2,1,0:T(8,128)(2,1)} %get-tuple-element.119.refs_4_.refs_1_, bf16[768,1536]{1,0:T(8,128)(2,1)} %slice.199.refs_2_), custom_call_target="tpu_custom_call" | custom-call | flops 2415919104 | bytes 14942208 | tf_op jit(solution)/shard_map/pallas_call | solution.py:465
  452.6 1.4 broadcast_select_fusion.1
  454.0 9.9 %collective-permute-done.10 = bf16[1,192,3072]{2,1,0:T(8,128)(2,1)S(1)} collective-permute-done((bf16[1,192,3072]{2,1,0:T(8,128)(2,1)}, bf16[1,192,3072]{2,1,0:T(8,128)(2,1)S(1)}, u32[]{:S(2)}, u32[]{:S(2)}) %collective-permute-start.10) | collective-permute-done | bytes 1179680 | tf_op jit(solution)/shard_map/ppermute | solution.py:542
  464.4 1.6 collective-permute-start.11
  468.5 8.8 %collective-permute-done.11 = bf16[1,192,1536]{2,1,0:T(8,128)(2,1)S(1)} collective-permute-done((bf16[1,192,1536]{2,1,0:T(8,128)(2,1)S(1)}, bf16[1,192,1536]{2,1,0:T(8,128)(2,1)S(1)}, u32[]{:S(2)}, u32[]{:S(2)}) %collective-permute-start.11) | collective-permute-done | bytes 589856 | tf_op jit(solution)/shard_map/ppermute | solution.py:542
  477.5 8.7 %collective-permute-start.12 = (bf16[1,192,768]{2,1,0:T(8,128)(2,1)S(1)}, bf16[1,192,768]{2,1,0:T(8,128)(2,1)S(1)}, u32[]{:S(2)}, u32[]{:S(2)}) collective-permute-start(bf16[1,192,768]{2,1,0:T(8,128)(2,1)S(1)} %constant_dynamic-slice_fusion.7), channel_id=1, source_target_pairs={{0,8},{4,12},{8,0},{12,4},{16,24},{20,28},{24,16},{28,20},{1,9},{5... | collective-permute-start | bytes 884744 | tf_op jit(solution)/shard_map/ppermute | solution.py:542
  486.1 7.8 %all-gather.14.cloned.1.call-done = bf16[8,2,192,256]{3,2,1,0:T(8,128)(2,1)} async-done(((bf16[1,2,192,256]{3,2,1,0:T(8,128)(2,1)}), bf16[8,2,192,256]{3,2,1,0:T(8,128)(2,1)}) %all-gather.14.cloned.1.call-update) | async-done | bytes 1572880 | tf_op jit(solution)/shard_map/all_gather | solution.py:592
  493.9 1.7 convert_bitcast_fusion
  496.4 4.7 collective-permute-start.13
  501.2 1.4 fusion.15
  502.6 1.2 copy.68
  503.8 1.3 squeeze.4
  505.1 2.6 copy.69
  507.7 2.4 squeeze.5
  511.2 3.3 pad_maximum_fusion
  514.5 4.2 collective-permute-done.14
  518.8 9.8 %shard_map.265 = (f32[1024,768]{1,0:T(8,128)}, f32[1,768]{1,0:T(1,128)}) custom-call(bf16[2,192,3072]{2,1,0:T(8,128)(2,1)} %copy-done.2, f32[1024,768]{1,0:T(8,128)} %shard_map.264.refs_1_, bf16[3,1024,768]{2,1,0:T(8,128)(2,1)} %get-tuple-element.126.refs_5_.refs_2_, bf16[768,2304]{1,0:T(8,128)(2,1)} %slice.193.refs_3_, bf16[1024,768]{1,0:T(8,128)(2,1)} %refs_4_.1, ...), custom_call_target="tpu_custom_call" | custom-call | flops 3623878656 | bytes 17694720 | tf_op jit(solution)/shard_map/pallas_call | solution.py:465
  530.6 46.3 %all_gather.38 = f32[32,8,768]{2,1,0:T(8,128)S(1)} all-gather(f32[1,8,768]{2,1,0:T(8,128)S(1)} %scatter.29), channel_id=1, replica_groups=mesh['rep'=8,'shard'=4] {'rep','shard'}, dimensions={0}, use_global_device_ids=true | all-gather | bytes 811008 | tf_op jit(solution)/shard_map/all_gather | solution.py:752
  578.8 1.3 slice.204
  (191 shorter events, 41.2 us)
Async XLA Ops:
  7.2 2.6 copy-start.29
  7.2 2.7 copy-start.32
  7.2 3.4 copy-start.30
  7.2 8.5 %copy-start.15 = (bf16[192,2304]{1,0:T(8,128)(2,1)S(1)}, bf16[192,2304]{1,0:T(8,128)(2,1)}, u32[]{:S(2)}) copy-start(bf16[192,2304]{1,0:T(8,128)(2,1)} %param.36) | copy-start | bytes 2654212
  7.2 8.5 %copy-start.20 = (bf16[192,768]{1,0:T(8,128)(2,1)S(1)}, bf16[192,768]{1,0:T(8,128)(2,1)}, u32[]{:S(2)}) copy-start(bf16[192,768]{1,0:T(8,128)(2,1)} %param.37) | copy-start | bytes 884740
  7.2 43.2 %all-gather.8.cloned.1.call-start = ((), (), s32[]{:S(2)}) async-start(), calls=%async_computation.1 | async-start | bytes 5898240 | tf_op jit(solution)/shard_map/all_gather | solution.py:646
  9.8 81.4 %all-gather.6.cloned.1.call-start = ((), (), s32[]{:S(2)}) async-start(), calls=%async_computation | async-start | bytes 6144000 | tf_op jit(solution)/shard_map/all_gather | solution.py:643
  16.9 1.5 copy-start
  16.9 133.6 %all-gather.12.cloned.1.call-start = ((), (), s32[]{:S(2)}) async-start(), calls=%async_computation.3 | async-start | bytes 3932160 | tf_op jit(solution)/shard_map/all_gather | solution.py:650
  17.6 1.1 copy-start.25
  17.7 2.0 copy-start.26
  17.7 151.5 %all-gather.10.cloned.1.call-start = ((), (), s32[]{:S(2)}) async-start(), calls=%async_computation.2 | async-start | bytes 7864320 | tf_op jit(solution)/shard_map/all_gather | solution.py:649
  18.2 475.6 %all-gather.14.cloned.1.call-start = ((), (), s32[]{:S(2)}) async-start(), calls=%async_computation.4 | async-start | bytes 1769472 | tf_op jit(solution)/shard_map/all_gather | solution.py:592
  20.8 72.5 %copy-start.23 = (bf16[640,32]{1,0:T(8,128)(2,1)S(1)}, bf16[640,32]{1,0:T(8,128)(2,1)}, u32[]{:S(2)}) copy-start(bf16[640,32]{1,0:T(8,128)(2,1)} %constant.372.clone) | copy-start | bytes 122884
  20.8 72.5 %copy-start.31 = (pred[640]{0:T(1024)(128)(4,1)S(1)}, pred[640]{0:T(1024)(128)(4,1)}, u32[]{:S(2)}) copy-start(pred[640]{0:T(1024)(128)(4,1)} %constant.379) | copy-start | bytes 1924
  95.2 8.0 %copy-start.11 = (bf16[1024,768]{1,0:T(8,128)(2,1)}, bf16[1024,768]{1,0:T(8,128)(2,1)S(1)}, u32[]{:S(2)}) copy-start(bf16[1024,768]{1,0:T(8,128)(2,1)S(1)} %fusion.3.refs_3_) | copy-start | bytes 4718596
  124.8 20.9 %copy-start.1 = (f32[1024,768]{1,0:T(8,128)}, f32[1024,768]{1,0:T(8,128)S(1)}, u32[]{:S(2)}) copy-start(f32[1024,768]{1,0:T(8,128)S(1)} %get-tuple-element.162.refs_4_) | copy-start | bytes 9437188
  125.1 4.8 copy-start.12
  211.4 3.7 collective-permute-start.3
  211.7 29.0 %collective-permute-start = (bf16[2,2,192,2048]{3,2,1,0:T(8,128)(2,1)}, bf16[2,2,192,2048]{3,2,1,0:T(8,128)(2,1)}, u32[]{:S(2)}, u32[]{:S(2)}) collective-permute-start(bf16[2,2,192,2048]{3,2,1,0:T(8,128)(2,1)} %get-tuple-element.114), channel_id=1, source_target_pairs={{0,1},{1,0},{2,3},{3,2},{4,5},{5,4},{6,7},{7,6},{8,9},{9,8},{10,11... | collective-permute-start | bytes 9437192 | tf_op jit(solution)/shard_map/ppermute | solution.py:542
  215.1 1.2 copy-start.13
  218.6 19.8 %collective-permute-start.4 = (bf16[2,256,768]{2,1,0:T(8,128)(2,1)S(1)}, bf16[2,256,768]{2,1,0:T(8,128)(2,1)S(1)}, u32[]{:S(2)}, u32[]{:S(2)}) collective-permute-start(bf16[2,256,768]{2,1,0:T(8,128)(2,1)S(1)} %constant_dynamic-slice_fusion.15), channel_id=1, source_target_pairs={{0,4},{4,0},{8,12},{12,8},{16,20},{20,16},{24,28},{28,24},{1,5},{5... | collective-permute-start | bytes 2359304 | tf_op jit(solution)/shard_map/ppermute | solution.py:542
  238.3 0.9 copy-start.16
  239.2 39.1 %collective-permute-start.5 = (bf16[2,128,768]{2,1,0:T(8,128)(2,1)S(1)}, bf16[2,128,768]{2,1,0:T(8,128)(2,1)}, u32[]{:S(2)}, u32[]{:S(2)}) collective-permute-start(bf16[2,128,768]{2,1,0:T(8,128)(2,1)S(1)} %constant_dynamic-slice_fusion.14), channel_id=1, source_target_pairs={{0,8},{4,12},{8,0},{12,4},{16,24},{20,28},{24,16},{28,20},{1,9},{5... | collective-permute-start | bytes 1179656 | tf_op jit(solution)/shard_map/ppermute | solution.py:542
  278.3 21.5 %collective-permute-start.7 = (bf16[2,192,3072]{2,1,0:T(8,128)(2,1)}, bf16[2,192,3072]{2,1,0:T(8,128)(2,1)S(1)}, u32[]{:S(2)}, u32[]{:S(2)}) collective-permute-start(bf16[2,192,3072]{2,1,0:T(8,128)(2,1)} %get-tuple-element.122), channel_id=1, source_target_pairs={{0,1},{1,0},{2,3},{3,2},{4,5},{5,4},{6,7},{7,6},{8,9},{9,8},{10,11... | collective-permute-start | bytes 7077896 | tf_op jit(solution)/shard_map/ppermute | solution.py:542
  279.5 14.7 %collective-permute-start.6 = (bf16[2,64,768]{2,1,0:T(8,128)(2,1)S(1)}, bf16[2,64,768]{2,1,0:T(8,128)(2,1)S(1)}, u32[]{:S(2)}, u32[]{:S(2)}) collective-permute-start(bf16[2,64,768]{2,1,0:T(8,128)(2,1)S(1)} %constant_dynamic-slice_fusion.13), channel_id=1, source_target_pairs={{0,16},{4,20},{8,24},{12,28},{16,0},{20,4},{24,8},{28,12},{1,17},{... | collective-permute-start | bytes 589832 | tf_op jit(solution)/shard_map/ppermute | solution.py:542
  290.0 4.8 copy-start.9
  294.2 0.7 copy-start.21
  294.2 5.5 collective-permute-start.25
  298.1 1.7 copy-start.6
  298.2 39.1 %collective-permute-start.1 = (bf16[1,2,192,2048]{3,2,1,0:T(8,128)(2,1)S(1)}, bf16[1,2,192,2048]{3,2,1,0:T(8,128)(2,1)S(1)}, u32[]{:S(2)}, u32[]{:S(2)}) collective-permute-start(bf16[1,2,192,2048]{3,2,1,0:T(8,128)(2,1)S(1)} %constant_dynamic-slice_fusion.17), channel_id=1, source_target_pairs={{0,2},{1,3},{2,0},{3,1},{4,6},{5,7},{6,4},{7,5},{8,10},{9,11},{10,... | collective-permute-start | bytes 4718600 | tf_op jit(solution)/shard_map/ppermute | solution.py:542
  299.8 1.5 copy-start.10
  302.4 57.7 %collective-permute-start.8 = (bf16[1,192,3072]{2,1,0:T(8,128)(2,1)}, bf16[1,192,3072]{2,1,0:T(8,128)(2,1)S(1)}, u32[]{:S(2)}, u32[]{:S(2)}) collective-permute-start(bf16[1,192,3072]{2,1,0:T(8,128)(2,1)} %constant_dynamic-slice_fusion.12), channel_id=1, source_target_pairs={{0,2},{1,3},{2,0},{3,1},{4,6},{5,7},{6,4},{7,5},{8,10},{9,11},{10,... | collective-permute-start | bytes 3538952 | tf_op jit(solution)/shard_map/ppermute | solution.py:542
  337.4 1.2 copy-start.7
  338.6 52.1 %collective-permute-start.2 = (bf16[1,2,192,1024]{3,2,1,0:T(8,128)(2,1)S(1)}, bf16[1,2,192,1024]{3,2,1,0:T(8,128)(2,1)S(1)}, u32[]{:S(2)}, u32[]{:S(2)}) collective-permute-start(bf16[1,2,192,1024]{3,2,1,0:T(8,128)(2,1)S(1)} %constant_dynamic-slice_fusion.16), channel_id=1, source_target_pairs={{0,4},{4,0},{8,12},{12,8},{16,20},{20,16},{24,28},{28,24},{1,5},{5... | collective-permute-start | bytes 2359304 | tf_op jit(solution)/shard_map/ppermute | solution.py:542
  360.1 1.0 copy-start.14
  361.1 28.9 %collective-permute-start.17 = (bf16[1,192,1536]{2,1,0:T(8,128)(2,1)S(1)}, bf16[1,192,1536]{2,1,0:T(8,128)(2,1)S(1)}, u32[]{:S(2)}, u32[]{:S(2)}) collective-permute-start(bf16[1,192,1536]{2,1,0:T(8,128)(2,1)S(1)} %constant_dynamic-slice_fusion.5), channel_id=1, source_target_pairs={{0,4},{4,0},{8,12},{12,8},{16,20},{20,16},{24,28},{28,24},{1,5},{5... | collective-permute-start | bytes 1769480 | tf_op jit(solution)/shard_map/ppermute | solution.py:542
  390.2 15.6 %collective-permute-start.18 = (bf16[1,192,768]{2,1,0:T(8,128)(2,1)S(1)}, bf16[1,192,768]{2,1,0:T(8,128)(2,1)S(1)}, u32[]{:S(2)}, u32[]{:S(2)}) collective-permute-start(bf16[1,192,768]{2,1,0:T(8,128)(2,1)S(1)} %constant_dynamic-slice_fusion.4), channel_id=1, source_target_pairs={{0,8},{4,12},{8,0},{12,4},{16,24},{20,28},{24,16},{28,20},{1,9},{5... | collective-permute-start | bytes 884744 | tf_op jit(solution)/shard_map/ppermute | solution.py:542
  390.7 0.9 copy-start.17
  405.8 1.1 copy-start.18
  405.8 32.9 %collective-permute-start.9 = (bf16[2,192,3072]{2,1,0:T(8,128)(2,1)}, bf16[2,192,3072]{2,1,0:T(8,128)(2,1)S(1)}, u32[]{:S(2)}, u32[]{:S(2)}) collective-permute-start(bf16[2,192,3072]{2,1,0:T(8,128)(2,1)} %get-tuple-element.128), channel_id=1, source_target_pairs={{0,1},{1,0},{2,3},{3,2},{4,5},{5,4},{6,7},{7,6},{8,9},{9,8},{10,11... | collective-permute-start | bytes 7077896 | tf_op jit(solution)/shard_map/ppermute | solution.py:542
  405.9 10.6 %copy-start.8 = (bf16[8,64,768]{2,1,0:T(8,128)(2,1)S(1)}, bf16[8,64,768]{2,1,0:T(8,128)(2,1)}, u32[]{:S(2)}) copy-start(bf16[8,64,768]{2,1,0:T(8,128)(2,1)} %all_gather.40) | copy-start | bytes 2359300
  406.0 10.5 %collective-permute-start.19 = (bf16[1,192,384]{2,1,0:T(8,128)(2,1)S(1)}, bf16[1,192,384]{2,1,0:T(8,128)(2,1)S(1)}, u32[]{:S(2)}, u32[]{:S(2)}) collective-permute-start(bf16[1,192,384]{2,1,0:T(8,128)(2,1)S(1)} %constant_dynamic-slice_fusion.3), channel_id=1, source_target_pairs={{0,16},{4,20},{8,24},{12,28},{16,0},{20,4},{24,8},{28,12},{1,17},{... | collective-permute-start | bytes 442376 | tf_op jit(solution)/shard_map/ppermute | solution.py:542
  408.0 18.6 %collective-permute-start.23 = (bf16[1,2,192,512]{3,2,1,0:T(8,128)(2,1)}, bf16[1,2,192,512]{3,2,1,0:T(8,128)(2,1)}, u32[]{:S(2)}, u32[]{:S(2)}) collective-permute-start(bf16[1,2,192,512]{3,2,1,0:T(8,128)(2,1)} %constant_dynamic-slice_fusion.2), channel_id=1, source_target_pairs={{0,8},{4,12},{8,0},{12,4},{16,24},{20,28},{24,16},{28,20},{1,9},{5... | collective-permute-start | bytes 1179656 | tf_op jit(solution)/shard_map/ppermute | solution.py:542
  416.5 9.6 %collective-permute-start.20 = (bf16[1,192,384]{2,1,0:T(8,128)(2,1)S(1)}, bf16[1,192,384]{2,1,0:T(8,128)(2,1)S(1)}, u32[]{:S(2)}, u32[]{:S(2)}) collective-permute-start(bf16[1,192,384]{2,1,0:T(8,128)(2,1)S(1)} %add_convert_fusion.17), channel_id=1, source_target_pairs={{0,16},{4,20},{8,24},{12,28},{16,0},{20,4},{24,8},{28,12},{1,17},{... | collective-permute-start | bytes 442376 | tf_op jit(solution)/shard_map/ppermute | solution.py:542
  416.7 1.3 copy-start.24
  426.1 11.0 %collective-permute-start.21 = (bf16[1,192,768]{2,1,0:T(8,128)(2,1)S(1)}, bf16[1,192,768]{2,1,0:T(8,128)(2,1)S(1)}, u32[]{:S(2)}, u32[]{:S(2)}) collective-permute-start(bf16[1,192,768]{2,1,0:T(8,128)(2,1)S(1)} %pad_maximum_fusion.6), channel_id=1, source_target_pairs={{0,8},{4,12},{8,0},{12,4},{16,24},{20,28},{24,16},{28,20},{1,9},{5... | collective-permute-start | bytes 884744 | tf_op jit(solution)/shard_map/ppermute | solution.py:542
  427.7 10.9 %copy-start.5 = (bf16[2,192,3072]{2,1,0:T(8,128)(2,1)S(1)}, bf16[2,192,3072]{2,1,0:T(8,128)(2,1)}, u32[]{:S(2)}) copy-start(bf16[2,192,3072]{2,1,0:T(8,128)(2,1)} %get-tuple-element.129.refs_0_) | copy-start | bytes 7077892
  427.8 16.1 %collective-permute-start.24 = (bf16[1,2,192,256]{3,2,1,0:T(8,128)(2,1)S(1)}, bf16[1,2,192,256]{3,2,1,0:T(8,128)(2,1)}, u32[]{:S(2)}, u32[]{:S(2)}) collective-permute-start(bf16[1,2,192,256]{3,2,1,0:T(8,128)(2,1)S(1)} %constant_dynamic-slice_fusion.1), channel_id=1, source_target_pairs={{0,16},{4,20},{8,24},{12,28},{16,0},{20,4},{24,8},{28,12},{1,17},{... | collective-permute-start | bytes 589832 | tf_op jit(solution)/shard_map/ppermute | solution.py:542
  438.0 14.5 %collective-permute-start.22 = (bf16[1,192,1536]{2,1,0:T(8,128)(2,1)}, bf16[1,192,1536]{2,1,0:T(8,128)(2,1)}, u32[]{:S(2)}, u32[]{:S(2)}) collective-permute-start(bf16[1,192,1536]{2,1,0:T(8,128)(2,1)} %pad_maximum_fusion.4), channel_id=1, source_target_pairs={{0,4},{4,0},{8,12},{12,8},{16,20},{20,16},{24,28},{28,24},{1,5},{5... | collective-permute-start | bytes 1769480 | tf_op jit(solution)/shard_map/ppermute | solution.py:542
  438.6 1.4 copy-start.2
  440.1 1.8 copy-start.3
  440.1 3.0 copy-start.19
  440.1 3.0 copy-start.22
  441.9 22.1 %collective-permute-start.10 = (bf16[1,192,3072]{2,1,0:T(8,128)(2,1)}, bf16[1,192,3072]{2,1,0:T(8,128)(2,1)S(1)}, u32[]{:S(2)}, u32[]{:S(2)}) collective-permute-start(bf16[1,192,3072]{2,1,0:T(8,128)(2,1)} %constant_dynamic-slice_fusion.9), channel_id=1, source_target_pairs={{0,2},{1,3},{2,0},{3,1},{4,6},{5,7},{6,4},{7,5},{8,10},{9,11},{10,... | collective-permute-start | bytes 3538952 | tf_op jit(solution)/shard_map/ppermute | solution.py:542
  452.5 11.4 %copy-start.4 = (bf16[2,192,3072]{2,1,0:T(8,128)(2,1)S(1)}, bf16[2,192,3072]{2,1,0:T(8,128)(2,1)}, u32[]{:S(2)}) copy-start(bf16[2,192,3072]{2,1,0:T(8,128)(2,1)} %copy-done.3) | copy-start | bytes 7077892
  464.4 12.9 %collective-permute-start.11 = (bf16[1,192,1536]{2,1,0:T(8,128)(2,1)S(1)}, bf16[1,192,1536]{2,1,0:T(8,128)(2,1)S(1)}, u32[]{:S(2)}, u32[]{:S(2)}) collective-permute-start(bf16[1,192,1536]{2,1,0:T(8,128)(2,1)S(1)} %constant_dynamic-slice_fusion.8), channel_id=1, source_target_pairs={{0,4},{4,0},{8,12},{12,8},{16,20},{20,16},{24,28},{28,24},{1,5},{5... | collective-permute-start | bytes 1769480 | tf_op jit(solution)/shard_map/ppermute | solution.py:542
  477.5 18.2 %collective-permute-start.12 = (bf16[1,192,768]{2,1,0:T(8,128)(2,1)S(1)}, bf16[1,192,768]{2,1,0:T(8,128)(2,1)S(1)}, u32[]{:S(2)}, u32[]{:S(2)}) collective-permute-start(bf16[1,192,768]{2,1,0:T(8,128)(2,1)S(1)} %constant_dynamic-slice_fusion.7), channel_id=1, source_target_pairs={{0,8},{4,12},{8,0},{12,4},{16,24},{20,28},{24,16},{28,20},{1,9},{5... | collective-permute-start | bytes 884744 | tf_op jit(solution)/shard_map/ppermute | solution.py:542
  496.4 13.7 %collective-permute-start.13 = (bf16[1,192,384]{2,1,0:T(8,128)(2,1)}, bf16[1,192,384]{2,1,0:T(8,128)(2,1)}, u32[]{:S(2)}, u32[]{:S(2)}) collective-permute-start(bf16[1,192,384]{2,1,0:T(8,128)(2,1)} %constant_dynamic-slice_fusion.6), channel_id=1, source_target_pairs={{0,16},{4,20},{8,24},{12,28},{16,0},{20,4},{24,8},{28,12},{1,17},{... | collective-permute-start | bytes 442376 | tf_op jit(solution)/shard_map/ppermute | solution.py:542
  511.1 7.6 %collective-permute-start.14 = (bf16[1,192,384]{2,1,0:T(8,128)(2,1)S(1)}, bf16[1,192,384]{2,1,0:T(8,128)(2,1)S(1)}, u32[]{:S(2)}, u32[]{:S(2)}) collective-permute-start(bf16[1,192,384]{2,1,0:T(8,128)(2,1)S(1)} %add_convert_fusion.18), channel_id=1, source_target_pairs={{0,16},{4,20},{8,24},{12,28},{16,0},{20,4},{24,8},{28,12},{1,17},{... | collective-permute-start | bytes 442376 | tf_op jit(solution)/shard_map/ppermute | solution.py:542
  518.7 11.1 %collective-permute-start.15 = (bf16[1,192,768]{2,1,0:T(8,128)(2,1)S(1)}, bf16[1,192,768]{2,1,0:T(8,128)(2,1)S(1)}, u32[]{:S(2)}, u32[]{:S(2)}) collective-permute-start(bf16[1,192,768]{2,1,0:T(8,128)(2,1)S(1)} %pad_maximum_fusion.5), channel_id=1, source_target_pairs={{0,8},{4,12},{8,0},{12,4},{16,24},{20,28},{24,16},{28,20},{1,9},{5... | collective-permute-start | bytes 884744 | tf_op jit(solution)/shard_map/ppermute | solution.py:542
  518.8 10.5 %copy-start.28 = (f32[1,768]{1,0:T(1,128)S(1)}, f32[1,768]{1,0:T(1,128)}, u32[]{:S(2)}) copy-start(f32[1,768]{1,0:T(1,128)} %get-tuple-element.133) | copy-start | bytes 9220
  518.8 10.6 %copy-start.27 = (f32[1,768]{1,0:T(1,128)S(1)}, f32[1,768]{1,0:T(1,128)}, u32[]{:S(2)}) copy-start(f32[1,768]{1,0:T(1,128)} %get-tuple-element.134) | copy-start | bytes 9220
  529.9 48.4 %collective-permute-start.16 = (bf16[1,192,1536]{2,1,0:T(8,128)(2,1)S(1)}, bf16[1,192,1536]{2,1,0:T(8,128)(2,1)S(1)}, u32[]{:S(2)}, u32[]{:S(2)}) collective-permute-start(bf16[1,192,1536]{2,1,0:T(8,128)(2,1)S(1)} %pad_maximum_fusion.3), channel_id=1, source_target_pairs={{0,4},{4,0},{8,12},{12,8},{16,20},{20,16},{24,28},{28,24},{1,5},{5... | collective-permute-start | bytes 1769480 | tf_op jit(solution)/shard_map/ppermute | solution.py:542
Sparse Core Ops, SparseCore 0:
  10.2 40.1 all-gather.7
  52.5 38.5 all-gather.5
  92.7 28.5 all-gather.11
  122.7 46.3 all-gather.9
  445.7 48.1 all-gather.13

commit v2 on v1

v2 whole, which is shorter than its diff:
```python
from functools import partial
import math

import jax
import jax.numpy as jnp
import numpy as np
from jax import lax
from jax.experimental import pallas as pl
from jax.experimental.pallas import tpu as pltpu
from jax.sharding import PartitionSpec as P

HEADS = 12
HEAD_DIM = 64
FF = 2048
NUM_BUCKETS = 32
SEQ = 512
D = 768
INNER = HEADS * HEAD_DIM
PAIRS = HEADS // 2
LANES = 128
SPAN = SEQ + LANES
FF_BLOCK = 512
ROWS = 256

eps = 1e-06
masked_score = -1e30
bf16 = jnp.bfloat16
f32 = jnp.float32
VMEM_LIMIT = 56 * 1024 * 1024

bucket_edges = np.array(
    list(range(1, 16)) + [int(math.ceil(16.0 * 8.0 ** ((b - 16) / 16.0))) for b in range(16, 32)],
    dtype=np.int32,
)

SELF_RANGES = ((0, 128), (0, 256), (0, 384), (128, 512))
CROSS_RANGES = ((0, 384), (0, 512), (0, 512), (128, 512))


def dot_nn(a, b):
    return lax.dot_general(a, b, (((1,), (0,)), ((), ())), preferred_element_type=f32)


def dot_nt(a, b):
    return lax.dot_general(a, b, (((1,), (1,)), ((), ())), preferred_element_type=f32)


def dot_tn(a, b):
    return lax.dot_general(a, b, (((0,), (0,)), ((), ())), preferred_element_type=f32)


def half_masks():
    lane = lax.broadcasted_iota(jnp.int32, (1, LANES), 1)
    low = (lane < HEAD_DIM).astype(f32)
    return low.astype(bf16), (1.0 - low).astype(bf16)


def pieces(value):
    lane = lax.broadcasted_iota(jnp.int32, value.shape, 1) % HEAD_DIM
    high = value.astype(bf16).astype(f32)
    rest = value - high
    middle = rest.astype(bf16).astype(f32)
    last = rest - middle
    return jnp.where(
        lane == 2, high, jnp.where(lane == 3, middle, jnp.where(lane == 4, last, 0.0))
    )


def stacked(block, low, high):
    return jnp.concatenate([block * low, block * high], axis=0)


def toeplitz(row):
    wide = jnp.broadcast_to(row, (LANES, SPAN))
    return pltpu.roll(wide, 0, 1, stride=1, stride_axis=0)[:, :SEQ]


def attend_forward_kernel(ranges, biased, waits, *refs):
    refs = refs[waits:]
    if biased:
        q_ref, k_ref, v_ref, qa_ref, ka_ref, g_ref, o_ref, l_ref, slab = refs

        @pl.when(pl.program_id(1) == 0)
        def _():
            slab[0:LANES] = toeplitz(g_ref[0, 0:1, :])
            slab[LANES : 2 * LANES] = toeplitz(g_ref[0, 1:2, :])
    else:
        q_ref, k_ref, v_ref, qa_ref, ka_ref, o_ref, l_ref = refs
    low, high = half_masks()
    keys = jnp.concatenate([k_ref[...], ka_ref[...]], axis=1)
    values = jnp.concatenate([v_ref[...], jnp.ones((SEQ, LANES), bf16)], axis=1)
    lane = lax.broadcasted_iota(jnp.int32, (LANES, LANES), 1)
    for block, (start, stop) in enumerate(ranges):
        rows = slice(block * LANES, (block + 1) * LANES)
        extra = qa_ref[rows, :]
        left = jnp.concatenate(
            [stacked(q_ref[rows, :], low, high), jnp.concatenate([extra, extra], axis=0)], axis=1
        )
        scores = dot_nt(left, keys[start:stop])
        if biased:
            scores = scores + slab[:, SEQ - (stop - start) :]
        top = jnp.max(scores, axis=1, keepdims=True)
        expd = jnp.exp(scores - top)
        mixed = dot_nn(expd.astype(bf16), values[start:stop])
        total = mixed[:, LANES:]
        mixed = mixed[:, :LANES] / total
        o_ref[rows, :] = jnp.where(lane < HEAD_DIM, mixed[:LANES], mixed[LANES:]).astype(bf16)
        negative = pieces(-(top + jnp.log(total)))
        l_ref[rows, :] = jnp.where(lane < HEAD_DIM, negative[:LANES], negative[LANES:]).astype(bf16)


def attend_forward(q, q_at, k, k_at, v, v_at, q_extra, k_extra, g, ranges, after=()):
    tokens = q.shape[0]
    sequences = tokens // SEQ
    biased = g is not None

    def block(at):
        return pl.BlockSpec((SEQ, LANES), lambda p, s: (s, at + p))

    shared = pl.BlockSpec((SEQ, LANES), lambda p, s: (s, 0))
    in_specs = [block(q_at), block(k_at), block(v_at), shared, shared]
    args = [q, k, v, q_extra, k_extra]
    scratch = []
    if biased:
        in_specs.append(pl.BlockSpec((1, 2, SPAN), lambda p, s: (p, 0, 0)))
        args.append(g)
        scratch.append(pltpu.VMEM((2 * LANES, SEQ), f32))
    seen = sum(stop - start for start, stop in ranges)
    return pl.pallas_call(
        partial(attend_forward_kernel, ranges, biased, len(after)),
        grid=(PAIRS, sequences),
        in_specs=[pl.BlockSpec(memory_space=pl.ANY)] * len(after) + in_specs,
        out_specs=[block(0), block(0)],
        out_shape=[jax.ShapeDtypeStruct((tokens, INNER), bf16)] * 2,
        scratch_shapes=scratch,
        compiler_params=pltpu.CompilerParams(vmem_limit_bytes=VMEM_LIMIT),
        cost_estimate=pl.CostEstimate(
            flops=2 * 2 * PAIRS * sequences * seen * 256 * 256,
            bytes_accessed=tokens * INNER * 10,
            transcendentals=PAIRS * sequences * seen * 256,
        ),
    )(*after, *args)


def attend_backward_kernel(ranges, biased, waits, *refs):
    refs = refs[waits:]
    if biased:
        (q_ref, k_ref, v_ref, qa_ref, ka_ref, l_ref, o_ref, d_ref, g_ref) = refs[:9]
        out_ref, rel_ref, dk, dv, slab, dslab = refs[9:]

        @pl.when(pl.program_id(1) == 0)
        def _():
            slab[:, 0:LANES] = toeplitz(g_ref[0, 0:1, :]).T
            slab[:, LANES : 2 * LANES] = toeplitz(g_ref[0, 1:2, :]).T
            dslab[...] = jnp.zeros_like(dslab)
    else:
        (q_ref, k_ref, v_ref, qa_ref, ka_ref, l_ref, o_ref, d_ref) = refs[:8]
        dq_ref, out_ref, dk, dv = refs[8:]
    low, high = half_masks()
    low_lane = lax.broadcasted_iota(jnp.int32, (LANES, LANES), 1) < HEAD_DIM
    low_row = lax.broadcasted_iota(jnp.int32, (LANES, LANES), 0) < HEAD_DIM
    keys = jnp.concatenate([k_ref[...], ka_ref[...]], axis=1)
    values = jnp.concatenate([v_ref[...], ka_ref[...]], axis=1)
    keys_t = k_ref[...].T
    dk[...] = jnp.zeros_like(dk)
    dv[...] = jnp.zeros_like(dv)
    for block, (start, stop) in enumerate(ranges):
        rows = slice(block * LANES, (block + 1) * LANES)
        seen = slice(start, stop)
        q2 = stacked(q_ref[rows, :], low, high)
        extra = qa_ref[rows, :]
        totals = l_ref[rows, :]
        q_right = jnp.concatenate(
            [q2, jnp.concatenate([extra + totals * low, extra + totals * high], axis=0)], axis=1
        )
        scores = dot_nt(keys[seen], q_right)
        if biased:
            scores = scores + slab[SEQ - (stop - start) :, :]
        probs = jnp.exp(scores)
        grad = d_ref[rows, :]
        d2 = stacked(grad, low, high)
        product = grad.astype(f32) * o_ref[rows, :].astype(f32)
        sum_low = jnp.sum(jnp.where(low_lane, product, 0.0), axis=1, keepdims=True)
        sum_high = jnp.sum(jnp.where(low_lane, 0.0, product), axis=1, keepdims=True)
        delta = pieces(
            -jnp.concatenate(
                [
                    jnp.broadcast_to(sum_low, (LANES, LANES)),
                    jnp.broadcast_to(sum_high, (LANES, LANES)),
                ],
                axis=0,
            )
        ).astype(bf16)
        lows = jnp.concatenate([delta[:LANES] * low, delta[LANES:] * high], axis=0)
        d_right = jnp.concatenate([d2, lows], axis=1)
        grad_scores = probs * dot_nt(values[seen], d_right)
        probs16 = probs.astype(bf16)
        scores16 = grad_scores.astype(bf16)
        dv[seen, :] += dot_nn(probs16, d2)
        dk[seen, :] += dot_nn(scores16, q2)
        dq = dot_nn(keys_t[:, seen], scores16)
        dq = jnp.where(low_row, dq[:, :LANES], dq[:, LANES:]).T.astype(bf16)
        if biased:
            out_ref[0, rows, :] = dq
            dslab[SEQ - (stop - start) :, :] += grad_scores
        else:
            dq_ref[rows, :] = dq
    first = 1 if biased else 0
    out_ref[first] = dk[...].astype(bf16)
    out_ref[first + 1] = dv[...].astype(bf16)
    if biased:

        @pl.when(pl.program_id(1) == pl.num_programs(1) - 1)
        def _():
            for head in range(2):
                square = dslab[:, head * LANES : (head + 1) * LANES].T
                wide = jnp.concatenate([square, jnp.zeros((LANES, LANES), f32)], axis=1)
                half = LANES // 2
                while half >= 1:
                    wide = wide[:half] + pltpu.roll(wide[half:], SPAN - half, 1)
                    half //= 2
                rel_ref[0, head : head + 1, :] = wide


def attend_backward(q, q_at, k, k_at, v, v_at, q_extra, k_extra, lows, mixed, grad, g, ranges, after=()):
    tokens = q.shape[0]
    sequences = tokens // SEQ
    biased = g is not None

    def block(at):
        return pl.BlockSpec((SEQ, LANES), lambda p, s: (s, at + p))

    shared = pl.BlockSpec((SEQ, LANES), lambda p, s: (s, 0))
    in_specs = [block(q_at), block(k_at), block(v_at), shared, shared, block(0), block(0), block(0)]
    args = [q, k, v, q_extra, k_extra, lows, mixed, grad]
    scratch = [pltpu.VMEM((SEQ, LANES), f32), pltpu.VMEM((SEQ, LANES), f32)]
    if biased:
        in_specs.append(pl.BlockSpec((1, 2, SPAN), lambda p, s: (p, 0, 0)))
        args.append(g)
        scratch += [pltpu.VMEM((SEQ, 2 * LANES), f32)] * 2
        out_specs = [
            pl.BlockSpec((3, SEQ, LANES), lambda p, s: (0, s, p)),
            pl.BlockSpec((1, 2, SPAN), lambda p, s: (p, 0, 0)),
        ]
        out_shape = [
            jax.ShapeDtypeStruct((3, tokens, INNER), bf16),
            jax.ShapeDtypeStruct((PAIRS, 2, SPAN), f32),
        ]
    else:
        out_specs = [block(0), pl.BlockSpec((2, SEQ, LANES), lambda p, s: (0, s, p))]
        out_shape = [
            jax.ShapeDtypeStruct((tokens, INNER), bf16),
            jax.ShapeDtypeStruct((2, tokens, INNER), bf16),
        ]
    seen = sum(stop - start for start, stop in ranges)
    return pl.pallas_call(
        partial(attend_backward_kernel, ranges, biased, len(after)),
        grid=(PAIRS, sequences),
        in_specs=[pl.BlockSpec(memory_space=pl.ANY)] * len(after) + in_specs,
        out_specs=out_specs,
        out_shape=out_shape,
        scratch_shapes=scratch,
        compiler_params=pltpu.CompilerParams(vmem_limit_bytes=VMEM_LIMIT),
        cost_estimate=pl.CostEstimate(
            flops=5 * 2 * PAIRS * sequences * seen * 256 * 256,
            bytes_accessed=tokens * INNER * 20,
            transcendentals=PAIRS * sequences * seen * 256,
        ),
    )(*after, *args)


def shares(core, value, keep_ref, send_ref, *at):
    rows, cols = value.shape
    parts = value.astype(bf16).reshape(2, 2, rows // 4, cols)
    for y in range(2):
        place = (y,) + at
        keep_ref[place] = jnp.where(core == 0, parts[y, 0], parts[y, 1])
        send_ref[place] = jnp.where(core == 0, parts[y, 1], parts[y, 0])


def place_pieces(where_ref, full, own, core, y, x, yc, xc):
    shard = where_ref[0]
    rows, cols = own.shape
    half = cols // 2

    def at(index):
        return pl.ds(pl.multiple_of(index * rows, rows), rows)

    full[at(shard), :] = own[...]
    full[at(shard ^ 1), :] = core[...]
    for bit in range(2):

        @pl.when(where_ref[1] == bit)
        def _():
            mine = slice(bit * half, (bit + 1) * half)
            other = slice((1 - bit) * half, (2 - bit) * half)
            full[at(shard ^ 2), mine] = y[...]
            full[at(shard ^ 2), other] = x[...]
            full[at(shard ^ 3), mine] = yc[...]
            full[at(shard ^ 3), other] = xc[...]


def whole_spec(array):
    return pl.BlockSpec(
        array.shape, lambda i, c: (0,) * array.ndim, pipeline_mode=pl.Buffered(1)
    )


def normed_rows(x, gain):
    factor = lax.rsqrt(jnp.mean(x * x, -1, keepdims=True) + eps)
    return (x * factor * gain).astype(bf16)


def first_kernel(where_ref, x_ref, onehot_ref, valid_ref, *refs):
    pieces_in = refs[:6]
    full, gains_ref, g_ref, n_ref, qkv_ref = refs[6:]

    @pl.when(pl.program_id(0) == 0)
    def _():
        place_pieces(where_ref, full, *pieces_in)
        small = full[:, 4 * INNER : 4 * INNER + LANES].astype(f32).T
        gains_ref[...] = small[0:8]
        table = small[16:32].astype(bf16)
        bias = jnp.where(valid_ref[...] > 0, dot_nn(table, onehot_ref[...]), masked_score)
        for pair in range(PAIRS):
            g_ref[pair] = bias[2 * pair : 2 * pair + 2]

    normed = normed_rows(x_ref[...].astype(f32), gains_ref[0:1, :])
    n_ref[...] = normed
    for part in range(3):
        columns = slice(part * D, (part + 1) * D)
        qkv_ref[:, columns] = dot_nn(normed, full[:, columns]).astype(bf16)


def first_step(where, x, pieces_in, onehot, valid):
    tokens = x.shape[0]
    width = pieces_in[0].shape[1]
    block = pl.BlockSpec((ROWS, D), lambda i, c: (i, 0))
    return pl.pallas_call(
        first_kernel,
        grid_spec=pltpu.PrefetchScalarGridSpec(
            num_scalar_prefetch=1,
            grid=(tokens // ROWS,),
            in_specs=[block, whole_spec(onehot), whole_spec(valid)]
            + [whole_spec(p) for p in pieces_in],
            out_specs=[
                pl.BlockSpec((D, width), lambda i, c: (0, 0)),
                pl.BlockSpec((8, D), lambda i, c: (0, 0)),
                pl.BlockSpec((PAIRS, 2, SPAN), lambda i, c: (0, 0, 0)),
                block,
                pl.BlockSpec((ROWS, 3 * INNER), lambda i, c: (i, 0)),
            ],
        ),
        out_shape=[
            jax.ShapeDtypeStruct((D, width), bf16),
            jax.ShapeDtypeStruct((8, D), f32),
            jax.ShapeDtypeStruct((PAIRS, 2, SPAN), f32),
            jax.ShapeDtypeStruct((tokens, D), bf16),
            jax.ShapeDtypeStruct((tokens, 3 * INNER), bf16),
        ],
        compiler_params=pltpu.CompilerParams(vmem_limit_bytes=VMEM_LIMIT),
        cost_estimate=pl.CostEstimate(
            flops=6 * tokens * D * D, bytes_accessed=tokens * D * 10 + D * width * 4,
            transcendentals=0,
        ),
    )(where, x, onehot, valid, *pieces_in)


def encoder_kernel(waits, where_ref, *refs):
    refs = refs[waits:]
    x_ref, pieces_in = refs[0], refs[1:7]
    full, kv_ref = refs[7:]

    @pl.when(pl.program_id(0) == 0)
    def _():
        place_pieces(where_ref, full, *pieces_in)

    for part in range(2):
        columns = slice(part * D, (part + 1) * D)
        kv_ref[:, columns] = dot_nn(x_ref[...], full[:, columns]).astype(bf16)


def encoder_step(where, x, pieces_in, after):
    tokens = x.shape[0]
    width = pieces_in[0].shape[1]
    return pl.pallas_call(
        partial(encoder_kernel, len(after)),
        grid_spec=pltpu.PrefetchScalarGridSpec(
            num_scalar_prefetch=1,
            grid=(tokens // ROWS,),
            in_specs=[pl.BlockSpec(memory_space=pl.ANY)] * len(after)
            + [pl.BlockSpec((ROWS, D), lambda i, c: (i, 0))]
            + [whole_spec(p) for p in pieces_in],
            out_specs=[
                pl.BlockSpec((D, width), lambda i, c: (0, 0)),
                pl.BlockSpec((ROWS, 2 * INNER), lambda i, c: (i, 0)),
            ],
        ),
        out_shape=[
            jax.ShapeDtypeStruct((D, width), bf16),
            jax.ShapeDtypeStruct((tokens, 2 * INNER), bf16),
        ],
        compiler_params=pltpu.CompilerParams(vmem_limit_bytes=VMEM_LIMIT),
        cost_estimate=pl.CostEstimate(
            flops=4 * tokens * D * D, bytes_accessed=tokens * D * 6 + D * width * 4,
            transcendentals=0,
        ),
    )(where, *after, x, *pieces_in)


def middle_kernel(x_ref, attn_ref, out_w_ref, gain_ref, q_w_ref, first_ref, n_ref, cq_ref):
    first = x_ref[...].astype(f32) + dot_nn(attn_ref[...], out_w_ref[...])
    first_ref[...] = first
    normed = normed_rows(first, gain_ref[...])
    n_ref[...] = normed
    cq_ref[...] = dot_nn(normed, q_w_ref[...]).astype(bf16)


def middle_step(x, attn, w_self, gain, w_cross):
    tokens = x.shape[0]
    block = pl.BlockSpec((ROWS, D), lambda i: (i, 0))
    return pl.pallas_call(
        middle_kernel,
        grid=(tokens // ROWS,),
        in_specs=[
            block,
            block,
            pl.BlockSpec((D, D), lambda i: (0, 3)),
            pl.BlockSpec((1, D), lambda i: (0, 0)),
            pl.BlockSpec((D, D), lambda i: (0, 2)),
        ],
        out_specs=[block] * 3,
        out_shape=[
            jax.ShapeDtypeStruct((tokens, D), f32),
            jax.ShapeDtypeStruct((tokens, D), bf16),
            jax.ShapeDtypeStruct((tokens, D), bf16),
        ],
        compiler_params=pltpu.CompilerParams(vmem_limit_bytes=VMEM_LIMIT),
        cost_estimate=pl.CostEstimate(
            flops=4 * tokens * D * D, bytes_accessed=tokens * D * 12 + D * D * 4, transcendentals=0
        ),
    )(x, attn, w_self, gain, w_cross)


def shares(core, value, keep_ref, send_ref, *at):
    rows, cols = value.shape
    parts = value.astype(bf16).reshape(2, 2, rows // 4, cols)
    columns = slice(0, cols)
    for y in range(2):
        place = (y,) + at + (slice(None), columns)
        keep_ref[place] = jnp.where(core == 0, parts[y, 0], parts[y, 1])
        send_ref[place] = jnp.where(core == 0, parts[y, 1], parts[y, 0])


def feed_forward_kernel(
    where_ref, x1_ref, attn_ref, w2_ref, gain_ref, dout_ref,
    own_g, own_u, core_g, core_u, y_in, x_in, yc_in, xc_in,
    own_o, core_o, y_o, x_o, yc_o, xc_o,
    layer_ref, gx_ref, gx16_ref, gk_ref, gs_ref, ok_ref, os_ref,
    wg, wu, wo, n3, n3t, acc, dn, hid, dgate, dup,
):
    step = pl.program_id(0)
    shard, across = where_ref[0], where_ref[1]
    tokens = x1_ref.shape[0]
    chunks = tokens // ROWS
    rows_in = own_g.shape[0]

    def at(index):
        return pl.ds(pl.multiple_of(index * rows_in, rows_in), rows_in)

    wg[at(shard), :] = own_g[...]
    wu[at(shard), :] = own_u[...]
    wg[at(shard ^ 1), :] = core_g[...]
    wu[at(shard ^ 1), :] = core_u[...]

    @pl.when(across == 0)
    def _():
        wg[at(shard ^ 2), :] = y_in[...]
        wu[at(shard ^ 2), :] = x_in[...]
        wg[at(shard ^ 3), :] = yc_in[...]
        wu[at(shard ^ 3), :] = xc_in[...]

    @pl.when(across == 1)
    def _():
        wg[at(shard ^ 2), :] = x_in[...]
        wu[at(shard ^ 2), :] = y_in[...]
        wg[at(shard ^ 3), :] = xc_in[...]
        wu[at(shard ^ 3), :] = yc_in[...]

    half = D // 2
    for turn, whole in ((0, own_o), (1, core_o)):

        @pl.when(step == turn)
        def _():
            wo[...] = whole[...]

    for turn, near, far in ((2, y_o, x_o), (3, yc_o, xc_o)):
        for bit in range(2):

            @pl.when((step == turn) & (across == bit))
            def _():
                wo[:, bit * half : (bit + 1) * half] = near[...]
                wo[:, (1 - bit) * half : (2 - bit) * half] = far[...]

    @pl.when(step == 0)
    def _():
        gain = gain_ref[...]
        for chunk in range(chunks):
            rows = slice(chunk * ROWS, (chunk + 1) * ROWS)
            x = x1_ref[rows, :] + dot_nn(attn_ref[rows, :], w2_ref[...])
            gx_ref[rows, :] = x
            normed = normed_rows(x, gain)
            n3[rows, :] = normed
            n3t[:, rows] = normed.T
            acc[rows, :] = jnp.zeros((ROWS, D), f32)
            dn[rows, :] = jnp.zeros((ROWS, D), f32)

    c = math.sqrt(2.0 / math.pi)
    for chunk in range(chunks):
        rows = slice(chunk * ROWS, (chunk + 1) * ROWS)
        normed = n3[rows, :]
        gate = dot_nn(normed, wg[...])
        up = dot_nn(normed, wu[...])
        dhidden = dot_nt(dout_ref[rows, :], wo[...]).astype(bf16).astype(f32)
        square = gate * gate
        t = jnp.tanh(c * gate * (1.0 + 0.044715 * square))
        mid = 0.5 * (1.0 + t)
        act = gate * mid
        slope = mid + (0.5 * c) * gate * (1.0 - t * t) * (1.0 + (3.0 * 0.044715) * square)
        hid[rows, :] = (act * up).astype(bf16)
        dgate[rows, :] = (dhidden * up * slope).astype(bf16)
        dup[rows, :] = (dhidden * act).astype(bf16)
        acc[rows, :] += dot_nn(hid[rows, :], wo[...])
        dn[rows, :] += dot_nt(dgate[rows, :], wg[...]) + dot_nt(dup[rows, :], wu[...])
    core = shard % 2
    shares(core, dot_nn(n3t[...], dgate[...]), gk_ref, gs_ref, 0)
    shares(core, dot_nn(n3t[...], dup[...]), gk_ref, gs_ref, 1)
    out_grad = dot_tn(hid[...], dout_ref[...]).astype(bf16)

    @pl.when(step % 2 == 0)
    def _():
        ok_ref[0] = out_grad

    @pl.when(step % 2 == 1)
    def _():
        os_ref[0] = out_grad

    @pl.when(step == pl.num_programs(0) - 1)
    def _():
        gain = gain_ref[...]
        for chunk in range(chunks):
            rows = slice(chunk * ROWS, (chunk + 1) * ROWS)
            x = gx_ref[rows, :]
            layer_ref[rows, :] = (x + acc[rows, :]).astype(bf16)
            factor = lax.rsqrt(jnp.mean(x * x, -1, keepdims=True) + eps)
            d = dn[rows, :]
            weighted = d * gain
            back = factor * weighted - x * (
                factor * factor * factor * jnp.mean(weighted * x, -1, keepdims=True)
            )
            gx = dout_ref[rows, :].astype(f32) + back
            gx_ref[rows, :] = gx
            gx16_ref[rows, :] = gx.astype(bf16)


def feed_forward(where, x1, attn, w_cross, gain, dout, in_pieces, out_pieces):
    tokens = x1.shape[0]
    steps = FF // FF_BLOCK
    one = pl.Buffered(1)
    rows_in = in_pieces[0].shape[0]

    def whole(width=D):
        return pl.BlockSpec((tokens, width), lambda f, c: (0, 0), pipeline_mode=one)

    def streamed(at):
        return pl.BlockSpec((rows_in, FF_BLOCK), lambda f, c: (0, at + (c[0] ^ f)))

    resident = pl.BlockSpec((tokens, D), lambda f, c: (0, 0))
    in_share = pl.BlockSpec((2, 2, D // 4, FF_BLOCK), lambda f, c: (0, 0, 0, c[0] ^ f))
    out_share = pl.BlockSpec((1, FF_BLOCK, D), lambda f, c: ((c[0] ^ f) // 2, 0, 0))
    in_type = jax.ShapeDtypeStruct((2, 2, D // 4, FF), bf16)
    out_type = jax.ShapeDtypeStruct((2, FF_BLOCK, D), bf16)
    own_i, core_i, *halves_i = in_pieces
    return pl.pallas_call(
        feed_forward_kernel,
        grid_spec=pltpu.PrefetchScalarGridSpec(
            num_scalar_prefetch=1,
            grid=(steps,),
            in_specs=[
                whole(),
                whole(),
                pl.BlockSpec((D, D), lambda f, c: (0, 3), pipeline_mode=one),
                pl.BlockSpec((1, D), lambda f, c: (0, 0)),
                whole(),
                streamed(0), streamed(steps), streamed(0), streamed(steps),
                streamed(0), streamed(0), streamed(0), streamed(0),
            ]
            + [whole_spec(p) for p in out_pieces],
            out_specs=[resident, resident, resident, in_share, in_share, out_share, out_share],
            scratch_shapes=[
                pltpu.VMEM((D, FF_BLOCK), bf16),
                pltpu.VMEM((D, FF_BLOCK), bf16),
                pltpu.VMEM((FF_BLOCK, D), bf16),
                pltpu.VMEM((tokens, D), bf16),
                pltpu.VMEM((D, tokens), bf16),
                pltpu.VMEM((tokens, D), f32),
                pltpu.VMEM((tokens, D), f32),
                pltpu.VMEM((tokens, FF_BLOCK), bf16),
                pltpu.VMEM((tokens, FF_BLOCK), bf16),
                pltpu.VMEM((tokens, FF_BLOCK), bf16),
            ],
        ),
        out_shape=[
            jax.ShapeDtypeStruct((tokens, D), bf16),
            jax.ShapeDtypeStruct((tokens, D), f32),
            jax.ShapeDtypeStruct((tokens, D), bf16),
            in_type, in_type, out_type, out_type,
        ],
        compiler_params=pltpu.CompilerParams(vmem_limit_bytes=VMEM_LIMIT),
        cost_estimate=pl.CostEstimate(
            flops=18 * tokens * D * FF,
            bytes_accessed=tokens * D * 16 + 12 * D * FF,
            transcendentals=tokens * FF,
        ),
    )(where, x1, attn, w_cross, gain, dout, own_i, own_i, core_i, core_i, *halves_i, *out_pieces)


def weight_grad_kernel(counts, firsts, waits, core_ref, *refs):
    refs = refs[waits:]
    terms = len(counts)
    lefts, rights = refs[0:terms], refs[terms : 2 * terms]
    refs = refs[2 * terms :]
    second = firsts is not None
    if second:
        tiny_ref, keep_ref, send_ref, keep2_ref, send2_ref, left_t = refs
    else:
        keep_ref, send_ref, left_t = refs
    step = pl.program_id(0)
    core = core_ref[0] % 2
    at = 0
    for left, right, count in zip(lefts, rights, counts):

        @pl.when(step == at)
        def _():
            left_t[...] = left[...].T

        @pl.when((step >= at) & (step < at + count))
        def _():
            block = right[...] if len(right.shape) == 2 else right[0]
            value = dot_nn(left_t[...], block)
            if not second:
                shares(core, value, keep_ref, send_ref)
            else:

                @pl.when(step < firsts)
                def _():
                    shares(core, value, keep_ref, send_ref)

                @pl.when(step >= firsts)
                def _():
                    shares(core, value, keep2_ref, send2_ref)
                    tiny = tiny_ref[...]
                    for y in range(2):
                        keep2_ref[y, :, D:] = jnp.where(core == 0, tiny[y, 0], tiny[y, 1])
                        send2_ref[y, :, D:] = jnp.where(core == 0, tiny[y, 1], tiny[y, 0])

        at += count


def weight_grad(where, terms, tiny=None, after=()):
    tokens = terms[0][0].shape[0]
    counts = []
    rights = []
    at = 0
    for _, right in terms:
        deep = right.ndim == 3
        count = right.shape[0] if deep else 1

        def place(j, c, at=at, count=count, deep=deep):
            return (jnp.clip(j - at, 0, count - 1), 0, 0) if deep else (0, 0)

        rights.append(pl.BlockSpec((1, tokens, D) if deep else (tokens, D), place))
        counts.append(count)
        at += count
    firsts = None if tiny is None else at - 1
    blocks = at if tiny is None else at - 1
    share = pl.BlockSpec((2, D // 4, D), lambda j, c: (0, 0, jnp.minimum(j, blocks - 1)))
    out_specs = [share, share]
    out_shape = [jax.ShapeDtypeStruct((2, D // 4, blocks * D), bf16)] * 2
    extra_specs, extra = [], []
    if tiny is not None:
        extra_specs, extra = [pl.BlockSpec(tiny.shape, lambda j, c: (0, 0, 0, 0))], [tiny]
        wide = D + tiny.shape[-1]
        out_specs += [pl.BlockSpec((2, D // 4, wide), lambda j, c: (0, 0, 0))] * 2
        out_shape += [jax.ShapeDtypeStruct((2, D // 4, wide), bf16)] * 2
    return pl.pallas_call(
        partial(weight_grad_kernel, counts, firsts, len(after)),
        grid_spec=pltpu.PrefetchScalarGridSpec(
            num_scalar_prefetch=1,
            grid=(at,),
            in_specs=[pl.BlockSpec(memory_space=pl.ANY)] * len(after)
            + [pl.BlockSpec((tokens, D), lambda j, c: (0, 0))] * len(terms)
            + rights
            + extra_specs,
            out_specs=out_specs,
            scratch_shapes=[pltpu.VMEM((D, tokens), bf16)],
        ),
        out_shape=out_shape,
        compiler_params=pltpu.CompilerParams(vmem_limit_bytes=VMEM_LIMIT),
        cost_estimate=pl.CostEstimate(
            flops=2 * tokens * D * D * at,
            bytes_accessed=tokens * D * (len(terms) + at) * 2 + D * D * at * 2,
            transcendentals=0,
        ),
    )(where, *after, *[left for left, _ in terms], *[right for _, right in terms], *extra)


def norm_back_kernel(normed, onward, waits, *refs):
    refs = refs[waits:]
    grad_ref, w_ref = refs[:2]
    total = None
    for part in range(grad_ref.shape[0]):
        term = dot_nt(grad_ref[part], w_ref[:, part * D : (part + 1) * D])
        total = term if total is None else total + term
    if not normed:
        refs[2][...] = total.astype(refs[2].dtype)
        return
    x_ref, gain_ref, up_ref = refs[2:5]
    refs = refs[5:]
    if onward:
        next_ref, out_ref, gain_grad_ref, out16_ref, onward_ref = refs
    else:
        out_ref, gain_grad_ref = refs
    x = x_ref[...].astype(f32)
    factor = lax.rsqrt(jnp.mean(x * x, -1, keepdims=True) + eps)
    weighted = total * gain_ref[...]
    grad_gain = jnp.sum(total * x * factor, axis=0, keepdims=True)

    @pl.when(pl.program_id(0) == 0)
    def _():
        gain_grad_ref[...] = jnp.zeros_like(gain_grad_ref)

    gain_grad_ref[...] += grad_gain
    scale = factor * factor * factor * jnp.mean(weighted * x, -1, keepdims=True)
    out = up_ref[...] + factor * weighted - x * scale
    out_ref[...] = out
    if onward:
        out16 = out.astype(bf16)
        out16_ref[...] = out16
        onward_ref[...] = dot_nt(out16, next_ref[...]).astype(bf16)


def norm_back(
    grads, w, w_at, x=None, gain=None, upstream=None, w_next=None, next_at=0, after=(), kind=f32
):
    if grads.ndim == 2:
        grads = grads[None]
    parts, tokens, _ = grads.shape
    block = pl.BlockSpec((ROWS, D), lambda i: (i, 0))
    row = pl.BlockSpec((1, D), lambda i: (0, 0))
    in_specs = [pl.BlockSpec(memory_space=pl.ANY)] * len(after)
    in_specs += [
        pl.BlockSpec((parts, ROWS, D), lambda i: (0, i, 0)),
        pl.BlockSpec((D, parts * D), lambda i: (0, w_at)),
    ]
    args = [*after, grads, w]
    wide = jax.ShapeDtypeStruct((tokens, D), kind)
    half = jax.ShapeDtypeStruct((tokens, D), bf16)
    out_specs, out_shape = [block], [wide]
    if x is not None:
        in_specs += [block, row, block]
        args += [x, gain, upstream]
        out_specs.append(row)
        out_shape.append(jax.ShapeDtypeStruct((1, D), f32))
        if w_next is not None:
            in_specs.append(pl.BlockSpec((D, D), lambda i: (0, next_at)))
            args.append(w_next)
            out_specs += [block, block]
            out_shape += [half, half]
    return pl.pallas_call(
        partial(norm_back_kernel, x is not None, w_next is not None, len(after)),
        grid=(tokens // ROWS,),
        in_specs=in_specs,
        out_specs=out_specs,
        out_shape=out_shape,
        compiler_params=pltpu.CompilerParams(vmem_limit_bytes=VMEM_LIMIT),
        cost_estimate=pl.CostEstimate(
            flops=2 * tokens * D * D * (parts + (w_next is not None)),
            bytes_accessed=tokens * D * (2 * parts + 12) + D * D * 2 * parts,
            transcendentals=0,
        ),
    )(*args)


def exchange(array, axis, size, bit):
    return lax.ppermute(array, axis, [(i, i ^ bit) for i in range(size)])


def part_of(array, dim, index):
    half = array.shape[dim] // 2
    return lax.dynamic_slice_in_dim(array, index * half, half, dim)


def tie(value, *others):
    return lax.optimization_barrier((value, *others))[0]


class Gather:
    def __init__(self, own, sizes, *after):
        self.sizes = sizes
        self.own = own
        half = part_of(own, 1, lax.axis_index("rep") % 2)
        if after:
            half = tie(half, *after)
        self.half = half
        self.y = exchange(half, "shard", sizes[0], 2)

    def cross(self, *after):
        if after:
            self.y = tie(self.y, *after)
        self.x = exchange(self.y, "rep", self.sizes[1], 1)
        self.core = exchange(tie(self.own, self.y), "shard", self.sizes[0], 1)
        self.yc = exchange(self.y, "shard", self.sizes[0], 1)

    def pieces(self, *after):
        if after:
            self.x = tie(self.x, *after)
        xc = exchange(self.x, "shard", self.sizes[0], 1)
        return self.own, self.core, self.y, self.x, self.yc, xc


class Chain:
    def __init__(self, keep, send, sizes, dims, order):
        self.shards, self.reps = sizes
        self.bits = [1 << b for b in range(self.reps.bit_length() - 1)]
        self.dims = [dims[min(i, len(dims) - 1)] for i in range(len(self.bits))]
        steps = []
        for name in order:
            if name == "y":
                steps.append(("shard", 2, 0))
            else:
                steps += [("rep", bit, dim) for bit, dim in zip(self.bits, self.dims)]
        self.steps = steps
        self.kept = [keep]
        self.got = exchange(send, "shard", self.shards, 1)
        self.sent = send
        self.at = 0

    def own(self):
        while self.at < len(self.steps):
            self.advance()
        total = self.got.astype(f32)
        for part in self.kept:
            total = total + part.astype(f32)
        return total.astype(bf16)

    def advance(self, *after):
        if after:
            self.got = tie(self.got, *after)
        axis, bit, dim = self.steps[self.at]
        self.at += 1
        mine = (lax.axis_index(axis) // bit) % 2
        size = self.shards if axis == "shard" else self.reps
        parts = self.kept + [self.got]
        total = None
        for part in parts:
            term = part_of(part, dim, 1 - mine).astype(f32)
            total = term if total is None else total + term
        self.sent = total.astype(bf16)
        self.kept = [part_of(part, dim, mine) for part in parts]
        self.got = exchange(self.sent, axis, size, bit)
        return self.got


def spread(own, sizes, bits, dims):
    rep = lax.axis_index("rep")
    for bit, dim in zip(reversed(bits), reversed(dims)):
        got = exchange(own, "rep", sizes[1], bit)
        mine = (rep // bit) % 2
        low = jnp.where(mine == 0, own, got)
        high = jnp.where(mine == 0, got, own)
        own = jnp.concatenate([low, high], axis=dim)
    return own


def unpack_kernel(blocks_ref, w_ref, in_ref, out_ref, sum_ref):
    reps, _, rows, cols = blocks_ref.shape
    out_rows = out_ref.shape[0] // reps
    total = jnp.zeros((rows, LANES), f32)
    for rep in range(reps):
        turned = int(format(rep, "0%db" % (reps.bit_length() - 1))[::-1], 2)
        for part in range(2):
            place = slice(part * FF + turned * cols, part * FF + (turned + 1) * cols)
            block = blocks_ref[rep, part].astype(f32)
            in_ref[:, place] = block
            product = block * w_ref[:, place].astype(f32)
            for lane in range(0, cols, LANES):
                total = total + product[:, lane : lane + LANES]
        out_place = slice(turned * out_rows, (turned + 1) * out_rows)
        for group in range(D // cols):
            out_ref[out_place, group * cols : (group + 1) * cols] = blocks_ref[
                rep, 2, group * out_rows : (group + 1) * out_rows, :
            ].astype(f32)
    row = jnp.broadcast_to(jnp.sum(total, axis=1, keepdims=True), (rows, LANES)).T
    sum_ref[...] = row[0:8]


def unpack(blocks, w):
    reps, _, rows, cols = blocks.shape
    return pl.pallas_call(
        unpack_kernel,
        out_shape=[
            jax.ShapeDtypeStruct((rows, 2 * FF), f32),
            jax.ShapeDtypeStruct((FF * rows // D, D), f32),
            jax.ShapeDtypeStruct((8, rows), f32),
        ],
        compiler_params=pltpu.CompilerParams(vmem_limit_bytes=VMEM_LIMIT),
        cost_estimate=pl.CostEstimate(
            flops=4 * rows * FF, bytes_accessed=rows * FF * 16, transcendentals=0
        ),
    )(blocks, w)


def bias_rows(shards):
    lane = np.arange(SPAN)
    distance = np.where(lane < SEQ, SEQ - LANES - lane, 2 * SEQ - lane)
    bucket = np.zeros(SPAN, np.int64)
    for edge in bucket_edges:
        bucket += distance >= edge
    valid = (distance >= 0) & (distance < SEQ)
    onehot = np.zeros((SPAN, NUM_BUCKETS), np.float32)
    onehot[np.arange(SPAN)[valid], bucket[valid]] = 1.0
    own = NUM_BUCKETS // shards
    rows = np.arange(NUM_BUCKETS) // own * (D // shards) + np.arange(NUM_BUCKETS) % own
    placed = np.zeros((D, SPAN), np.float32)
    placed[rows] = onehot.T
    return onehot, placed, valid[None].astype(np.float32)


def local(
    sizes,
    hidden_in,
    enc_states,
    dec_segments,
    enc_segments,
    out_grad,
    gains,
    rel_table,
    self_qkv,
    self_out,
    cross_q,
    cross_kv,
    cross_out,
    ff_in,
    ff_out,
):
    shards, reps = sizes
    own_rows = D // shards
    own_buckets = NUM_BUCKETS // shards
    width = reps.bit_length() - 1
    shard = lax.axis_index("shard")
    where = jnp.stack([shard, lax.axis_index("rep") % 2]).astype(jnp.int32)
    small = jnp.concatenate(
        [
            gains.T,
            jnp.zeros((own_rows, 13), bf16),
            jnp.pad(rel_table, ((0, own_rows - own_buckets), (0, 2 * LANES - 16 - HEADS))),
        ],
        axis=1,
    )
    self_set = Gather(jnp.concatenate([self_qkv, self_out, small], axis=1), sizes)
    self_set.cross()
    cross_set = Gather(
        jnp.concatenate([cross_kv, cross_q, cross_out], axis=1), sizes, self_set.y
    )
    self_pieces = self_set.pieces()

    lane = jnp.arange(LANES, dtype=jnp.int32)[None, :]
    dec_ids = dec_segments[:, None]
    enc_ids = enc_segments[:, None]
    ones = ((lane % HEAD_DIM >= 2) & (lane % HEAD_DIM <= 4)).astype(f32)

    def key_extra(ids):
        return jnp.where(lane < 2, jnp.where(lane != ids, masked_score, 0.0), ones).astype(bf16)

    q_extra = ((lane < 2) & (lane == dec_ids)).astype(bf16)
    self_extra = key_extra(dec_ids)
    cross_extra = key_extra(enc_ids)
    onehot, placed, valid = bias_rows(shards)
    w_self, gains_all, g, normed_one, qkv = first_step(
        where, hidden_in, self_pieces, placed.astype(bf16), valid
    )
    cross_set.cross(normed_one)
    out_set = Gather(ff_out, sizes, cross_set.y, normed_one)
    in_set = Gather(ff_in, sizes, cross_set.y, normed_one)
    attn_one, lows_one = attend_forward(
        qkv, 0, qkv, PAIRS, qkv, 2 * PAIRS, q_extra, self_extra, g, SELF_RANGES,
        after=[out_set.half, in_set.half],
    )
    cross_pieces = cross_set.pieces(attn_one)
    out_set.cross(attn_one)
    in_set.cross(attn_one)
    w_cross, ckv = encoder_step(where, enc_states, cross_pieces, [attn_one])
    first, normed_two, cq = middle_step(hidden_in, attn_one, w_self, gains_all[1:2], w_cross)
    attn_two, lows_two = attend_forward(
        cq, 0, ckv, 0, ckv, PAIRS, q_extra, cross_extra, None, CROSS_RANGES
    )
    ff_out_pieces = out_set.pieces(attn_two)
    ff_in_pieces = in_set.pieces(attn_two)
    layer_out, grad_second, out_two, in_keep, in_send, out_keep, out_send = feed_forward(
        where, first, attn_two, w_cross, gains_all[2:3], out_grad, ff_in_pieces, ff_out_pieces
    )
    ff_in_chain = Chain(in_keep, in_send, sizes, [3], "yr")
    ff_out_chain = Chain(out_keep, out_send, sizes, [1], "ry")
    (grad_attn_two,) = norm_back(out_two, w_cross, 3, kind=bf16, after=[layer_out])
    ff_out_chain.advance(grad_attn_two)
    ff_in_chain.advance(grad_attn_two)
    grad_cq, grad_ckv = attend_backward(
        cq, 0, ckv, 0, ckv, PAIRS, q_extra, cross_extra, lows_two, attn_two, grad_attn_two,
        None, CROSS_RANGES, after=[ff_in_chain.sent, ff_out_chain.sent],
    )
    ff_out_chain.advance(grad_cq)
    grad_first, _, out_one, grad_attn_one = norm_back(
        grad_cq, w_cross, 2, first, gains_all[1:2], grad_second, w_self, 3,
        after=[ff_out_chain.sent],
    )
    ff_in_chain.advance(grad_attn_one)
    ff_out_chain.advance(grad_attn_one)
    cross_keep, cross_send = weight_grad(
        where,
        [(enc_states, grad_ckv), (normed_two, grad_cq), (attn_two, out_two), (attn_one, out_one)],
        after=[ff_in_chain.sent, ff_out_chain.sent],
    )
    cross_chain = Chain(cross_keep, cross_send, sizes, [2, 1], "yr")
    (enc_grad,) = norm_back(grad_ckv, w_cross, 0, after=[cross_keep])
    ff_in_chain.advance(enc_grad)
    ff_out_chain.advance(enc_grad)
    cross_chain.advance(enc_grad)
    grad_qkv, rel_part = attend_backward(
        qkv, 0, qkv, PAIRS, qkv, 2 * PAIRS, q_extra, self_extra, lows_one, attn_one,
        grad_attn_one, g, SELF_RANGES,
        after=[cross_chain.sent, ff_out_chain.sent, ff_in_chain.sent],
    )
    ff_in_chain.advance(grad_qkv)
    cross_chain.advance(grad_qkv)
    table_part = jnp.einsum(
        "hu,ub->bh",
        rel_part.reshape(HEADS, SPAN),
        onehot,
        precision=lax.Precision.HIGHEST,
        preferred_element_type=f32,
    )
    tiny = table_part.reshape(2, 2, own_buckets, HEADS).astype(bf16)
    tiny = jnp.pad(tiny, ((0, 0), (0, 0), (0, own_rows - own_buckets), (0, 2 * LANES - HEADS)))
    self_keep, self_send, last_keep, last_send = weight_grad(
        where, [(normed_one, grad_qkv)], tiny=tiny, after=[ff_in_chain.sent, cross_chain.sent]
    )
    self_chain = Chain(self_keep, self_send, sizes, [2, 1], "yr")
    last_chain = Chain(last_keep, last_send, sizes, [2, 1], "ry")
    cross_chain.advance(self_keep)
    in_own = ff_in_chain.own()[0]
    out_own = ff_out_chain.own()[0]
    rows, columns = in_own.shape[1:]
    out_rows = out_own.shape[0]
    out_own = out_own.reshape(out_rows, -1, columns).transpose(1, 0, 2).reshape(1, rows, columns)
    blocks = lax.all_gather(
        tie(jnp.concatenate([in_own, out_own], axis=0), self_keep), "rep", axis=0
    )
    self_chain.advance(self_keep)
    last_chain.advance(self_keep)
    in_grad, _ = norm_back(
        grad_qkv, w_self, 0, hidden_in, gains_all[0:1], grad_first,
        after=[self_chain.sent, last_chain.sent, cross_chain.sent],
    )
    self_chain.advance(in_grad)
    last_chain.advance(in_grad)
    cross_chain.advance(in_grad)
    while last_chain.at < len(last_chain.steps):
        if self_chain.at < len(self_chain.steps):
            self_chain.advance()
        last_chain.advance()
    cross_grad = spread(cross_chain.own(), sizes, cross_chain.bits, cross_chain.dims)
    self_width = self_chain.own().shape[2]
    self_own = jnp.concatenate([self_chain.own(), last_chain.own()], axis=2)
    self_all = spread(self_own, sizes, self_chain.bits[1:], self_chain.dims[1:])
    other = exchange(self_all, "rep", reps, 1)
    here = lax.axis_index("rep") % 2
    low = jnp.where(here == 0, self_all, other)[0]
    high = jnp.where(here == 0, other, self_all)[0]
    self_grad = jnp.concatenate(
        [low[:, :self_width], high[:, :self_width], low[:, self_width:], high[:, self_width:]],
        axis=1,
    ).astype(f32)
    cross_grad = cross_grad[0].astype(f32)

    if reps == 8:
        ff_in_grad, ff_out_grad, in_sums = unpack(blocks, ff_in)
        in_sums = in_sums[0]
    else:
        blocks = blocks.reshape((2,) * width + blocks.shape[1:])
        order = list(reversed(range(width)))
        in_grads = blocks[..., :2, :, :].transpose([width + 1, width] + order + [width + 2])
        ff_in_grad = in_grads.reshape(own_rows, 2 * FF).astype(f32)
        out_grads = blocks[..., 2, :, :].reshape((2,) * width + (-1, out_rows, columns))
        out_grads = out_grads.transpose(order + [width + 1, width, width + 2])
        ff_out_grad = out_grads.reshape(ff_out.shape).astype(f32)
        in_sums = jnp.sum(ff_in.astype(f32) * ff_in_grad, axis=1)

    self_qkv_grad = self_grad[:, : 3 * INNER]
    cross_query_gradient = cross_grad[:, 2 * INNER : 3 * INNER]

    sums = jnp.stack(
        [
            jnp.sum(self_qkv.astype(f32) * self_qkv_grad, axis=1),
            jnp.sum(cross_q.astype(f32) * cross_query_gradient, axis=1),
            in_sums,
        ]
    )
    gains_grad = sums / gains.astype(f32)
    rel_table_grad = self_grad[:own_buckets, 3 * INNER : 3 * INNER + HEADS]
    return (
        layer_out,
        in_grad,
        enc_grad,
        gains_grad,
        rel_table_grad,
        self_qkv_grad,
        cross_grad[:, 3 * INNER + D :],
        cross_query_gradient,
        cross_grad[:, : 2 * INNER],
        cross_grad[:, 3 * INNER : 3 * INNER + D],
        ff_in_grad,
        ff_out_grad,
    )


def solution(mesh):
    tokens = P(("rep", "shard"), None)
    ids = P(("rep", "shard"))
    rows = P("shard", None)
    columns = P(None, "shard")
    in_specs = (tokens, tokens, ids, ids, tokens, columns) + (rows,) * 8
    out_specs = (tokens, tokens, tokens, columns) + (rows,) * 8
    sizes = (mesh.shape["shard"], mesh.shape["rep"])
    return jax.shard_map(
        partial(local, sizes), mesh=mesh, in_specs=in_specs, out_specs=out_specs, check_vma=False
    )
```

time: 598 us -> 501 us (0.84)
  blocking collectives: 80.4 us -> 0 us
  Pallas kernels: 181 us -> 219 us
  matrix products: 32.4 us -> 1.25 us
  waiting for transfers between devices: 165 us -> 137 us
  local copies, waits for them, and re-layouts: 45.3 us -> 18.4 us
  other arithmetic: 34.3 us -> 54.5 us
  starting transfers between devices: 34 us -> 47.6 us
    all_gather x2 -> x0, blocking collectives: 80.4 us -> none  [the longest x1 46.3 us: local(): tiny = jnp.sum(lax.all_gather(tiny, ('rep', 'shard'), axis=0), axis=0)]
    all_gather x5 -> x1, waiting for transfers between devices: 90.4 us -> 24.9 us  [local(): lax.all_gather(tie(jnp.concatenate([in_own, out_own], axis=0), self_keep)...]
    ppermute x26 -> x51, waiting for transfers between devices: 73.6 us -> 112 us  [exchange(): return lax.ppermute(array, axis, [(i, i ^ bit) for i in range(size)])]
    dot_general x7 -> x0, matrix products: 31.8 us -> none  [the longest x5 27.2 us: dot_nn(): lax.dot_general(a, b, (((1,), (0,)), ((), ())), preferred_element_type=f32)]
    pallas_call x4 -> x8, Pallas kernels: 63.4 us -> 91.7 us  [the longest x2 33.8 us: attend_forward(): pl.pallas_call(partial(attend_forward_kernel, ranges, biased, len(after))...]
    convert_element_type x27 -> x26, other arithmetic: 18.7 us -> 43.7 us  [the longest x20 37.6 us: advance(): self.sent = total.astype(bf16)]
    slice x14 -> x6, local copies, waits for them, and re-layouts: 22.4 us -> 2.2 us  [the longest x1 1.44 us: local(): gains_all[0:1]]
    ppermute x26 -> x51, starting transfers between devices: 33.8 us -> 47.6 us  [exchange(): return lax.ppermute(array, axis, [(i, i ^ bit) for i in range(size)])]
  transfers between devices with their start and end apart: 31 -> 52, of which waited for: 13 -> 20; matrix products, arithmetic and copies ran while one was open for 17% -> 11% of each run, Pallas kernels for 24% -> 29%
where the time goes in v2:
time: 501 us; the launch traced here: 493 us
  Pallas kernels  219 us (44%)
  waiting for transfers between devices  137 us (27%)
  other arithmetic  54.5 us (11%)
  starting transfers between devices  47.6 us (10%)
  local copies, waits for them, and re-layouts  18.4 us (4%)
  between operations  15.2 us (3%)
    ppermute x51, waiting for transfers between devices, exchange(): return lax.ppermute(array, axis, [(i, i ^ bit) for i in range(size)])  112 us
    pallas_call x2, Pallas kernels, attend_backward(): pl.pallas_call(partial(attend_backward_kernel, ranges, biased, len(after)...  49.8 us
    ppermute x51, starting transfers between devices, exchange(): return lax.ppermute(array, axis, [(i, i ^ bit) for i in range(size)])  47.6 us
    pallas_call x1, Pallas kernels, feed_forward(): pl.pallas_call(feed_forward_kernel, grid_spec=pltpu.PrefetchScalarGridSpe...  45.9 us
    convert_element_type x20, other arithmetic, advance(): self.sent = total.astype(bf16)  37.6 us
    pallas_call x2, Pallas kernels, attend_forward(): pl.pallas_call(partial(attend_forward_kernel, ranges, biased, len(after))...  33.8 us
    pallas_call x4, Pallas kernels, norm_back(): pl.pallas_call(partial(norm_back_kernel, x is not None, w_next is not Non...  31.3 us
    pallas_call x2, Pallas kernels, weight_grad(): pl.pallas_call(partial(weight_grad_kernel, counts, firsts, len(after)), g...  25.5 us
  transfers between devices with their start and end apart: 52, of which 20 were waited for; matrix products, arithmetic and copies ran while one was open for 11% of the time, Pallas kernels for 29%

profile of v2, /device:TPU:0, one launch (start us, length us, event | category | flops | bytes accessed | tf_op | source)
XLA Modules:
  0.0 492.7 jit_solution(5024731444188584777)
XLA Ops:
  8.8 2.2 concatenate.31.refs_0_
  11.2 3.0 collective-permute-start
  14.2 14.5 %collective-permute-done.refs_2_ = bf16[192,1664]{1,0:T(8,128)(2,1)} collective-permute-done((bf16[192,1664]{1,0:T(8,128)(2,1)S(1)}, bf16[192,1664]{1,0:T(8,128)(2,1)}, u32[]{:S(2)}, u32[]{:S(2)}) %collective-permute-start) | collective-permute-done | bytes 639008 | tf_op jit(solution)/shard_map/ppermute | solution.py:796
  28.7 1.7 collective-permute-start.3
  34.2 10.4 %collective-permute-done.3.refs_3_ = bf16[192,1664]{1,0:T(8,128)(2,1)} collective-permute-done((bf16[192,1664]{1,0:T(8,128)(2,1)}, bf16[192,1664]{1,0:T(8,128)(2,1)}, u32[]{:S(2)}, u32[]{:S(2)}) %collective-permute-start.3) | collective-permute-done | bytes 639008 | tf_op jit(solution)/shard_map/ppermute | solution.py:796
  45.7 1.5 collective-permute-start.1
  49.0 11.2 %shard_map.256 = (bf16[768,3328]{1,0:T(8,128)(2,1)}, f32[8,768]{1,0:T(8,128)}, f32[6,2,640]{2,1,0:T(2,128)}, bf16[1024,768]{1,0:T(8,128)(2,1)}, bf16[1024,2304]{1,0:T(8,128)(2,1)}) custom-call(s32[2]{0:T(128)} %pad_add_fusion.where_ref.core_ref, bf16[1024,768]{1,0:T(8,128)(2,1)} %refs_5_.1, bf16[768,640]{1,0:T(8,128)(2,1)} %constant.1616.clone.onehot_ref, ...), custom_call_target="tpu_custom_call" | custom-call | flops 3623878656 | bytes 18087936 | tf_op jit(solution)/shard_map/pallas_call | solution.py:339
  64.4 1.5 collective-permute-start.10
  65.9 18.5 %shard_map.257 = (bf16[1024,768]{1,0:T(8,128)(2,1)}, bf16[1024,768]{1,0:T(8,128)(2,1)}) custom-call(bf16[512,384]{1,0:T(8,128)(2,1)} %constant_dynamic-slice_fusion.3.refs_0_, bf16[192,2048]{1,0:T(8,128)(2,1)} %copy-done.3, bf16[1024,2304]{1,0:T(8,128)(2,1)} %get-tuple-element.86.refs_2_.refs_3_.refs_4_.refs_5_, ...), custom_call_target="tpu_custom_call" | custom-call | flops 3623878656 | bytes 7864320 | tf_op jit(solution)/shard_map/pallas_call | solution.py:129
  86.7 9.3 %collective-permute-done.15.y_o = bf16[512,384]{1,0:T(8,128)(2,1)S(1)} collective-permute-done((bf16[512,384]{1,0:T(8,128)(2,1)S(1)}, bf16[512,384]{1,0:T(8,128)(2,1)S(1)}, u32[]{:S(2)}, u32[]{:S(2)}) %collective-permute-start.15) | collective-permute-done | bytes 393248 | tf_op jit(solution)/shard_map/ppermute | solution.py:796
  97.2 1.5 collective-permute-start.12
  99.7 9.0 %shard_map.258 = (bf16[768,3072]{1,0:T(8,128)(2,1)}, bf16[1024,1536]{1,0:T(8,128)(2,1)}) custom-call(s32[2]{0:T(128)} %pad_add_fusion.where_ref.core_ref, bf16[1024,768]{1,0:T(8,128)(2,1)} %get-tuple-element.88.refs_0_.attn_ref.refs_5_.refs_9_, bf16[1024,768]{1,0:T(8,128)(2,1)} %refs_2_.1, bf16[192,3072]{1,0:T(8,128)(2,1)} %constant_dynamic-update-slice_fusion.refs_2_, ...), custom_call_target="tpu_custom_call" | custom-call | flops 2415919104 | bytes 14155776 | tf_op jit(solution)/shard_map/pallas_call | solution.py:386
  108.7 7.4 %shard_map.259 = (f32[1024,768]{1,0:T(8,128)}, bf16[1024,768]{1,0:T(8,128)(2,1)}, bf16[1024,768]{1,0:T(8,128)(2,1)}) custom-call(bf16[1024,768]{1,0:T(8,128)(2,1)} %refs_5_.1, bf16[1024,768]{1,0:T(8,128)(2,1)} %get-tuple-element.88.refs_0_.attn_ref.refs_5_.refs_9_, bf16[768,3328]{1,0:T(8,128)(2,1)} %get-tuple-element.89.out_w_ref.refs_6_.refs_4_, ...), custom_call_target="tpu_custom_call" | custom-call | flops 2415919104 | bytes 11796480 | tf_op jit(solution)/shard_map/pallas_call | solution.py:422
  116.2 15.4 %shard_map.260 = (bf16[1024,768]{1,0:T(8,128)(2,1)}, bf16[1024,768]{1,0:T(8,128)(2,1)}) custom-call(bf16[1024,768]{1,0:T(8,128)(2,1)} %get-tuple-element.95.refs_0_.refs_2_, bf16[1024,1536]{1,0:T(8,128)(2,1)} %get-tuple-element.96.refs_1_.refs_2_.refs_3_.refs_4_, bf16[1024,1536]{1,0:T(8,128)(2,1)} %get-tuple-element.96.refs_1_.refs_2_.refs_3_.refs_4_, ...), custom_call_target="tpu_custom_call" | custom-call | flops 5637144576 | bytes 7864320 | tf_op jit(solution)/shard_map/pallas_call | solution.py:129
  132.3 1.7 collective-permute-done.13.yc_in
  133.9 1.7 collective-permute-done.19.xc_o
  137.7 45.9 %shard_map.261 = (bf16[1024,768]{1,0:T(8,128)(2,1)}, f32[1024,768]{1,0:T(8,128)}, bf16[1024,768]{1,0:T(8,128)(2,1)}, bf16[2,2,192,2048]{3,2,1,0:T(8,128)(2,1)}, ...) custom-call(s32[2]{0:T(128)} %pad_add_fusion.where_ref.core_ref, ...), custom_call_target="tpu_custom_call" | custom-call | flops 28991029248 | bytes 31457280 | tf_op jit(solution)/shard_map/pallas_call | solution.py:584
  184.2 5.2 %shard_map.262.refs_9_ = bf16[1024,768]{1,0:T(8,128)(2,1)} custom-call(bf16[1024,768]{1,0:T(8,128)(2,1)} %get-tuple-element.68.refs_0_, bf16[1,1024,768]{2,1,0:T(8,128)(2,1)} %bitcast.27, bf16[768,3072]{1,0:T(8,128)(2,1)} %get-tuple-element.93.q_w_ref.w2_ref.refs_2_), custom_call_target="tpu_custom_call" | custom-call | flops 1207959552 | bytes 12189696 | tf_op jit(solution)/shard_map/pallas_call | solution.py:780
  189.4 2.5 collective-permute-done.22
  194.0 3.2 add_convert_fusion.refs_0_
  197.7 22.6 %shard_map.263 = (bf16[1024,768]{1,0:T(8,128)(2,1)}, bf16[2,1024,768]{2,1,0:T(8,128)(2,1)}) custom-call(bf16[1,2,192,2048]{3,2,1,0:T(8,128)(2,1)} %add_convert_fusion.refs_0_, bf16[2,256,768]{2,1,0:T(8,128)(2,1)} %copy-done.17, bf16[1024,768]{1,0:T(8,128)(2,1)} %get-tuple-element.95.refs_0_.refs_2_, ...), custom_call_target="tpu_custom_call" | custom-call | flops 14092861440 | bytes 15728640 | tf_op jit(solution)/shard_map/pallas_call | solution.py:256
  220.3 1.5 add_convert_fusion.8.refs_0_
  221.8 1.6 collective-permute-start.25
  223.5 9.0 %shard_map.264 = (f32[1024,768]{1,0:T(8,128)}, f32[1,768]{1,0:T(1,128)}, bf16[1024,768]{1,0:T(8,128)(2,1)}, bf16[1024,768]{1,0:T(8,128)(2,1)}) custom-call(bf16[2,128,768]{2,1,0:T(8,128)(2,1)} %copy-done.9, bf16[1,1024,768]{2,1,0:T(8,128)(2,1)} %bitcast.28, bf16[768,3072]{1,0:T(8,128)(2,1)} %get-tuple-element.93.q_w_ref.w2_ref.refs_2_, ...), custom_call_target="tpu_custom_call" | custom-call | flops 2415919104 | bytes 12189696 | tf_op jit(solution)/shard_map/pallas_call | solution.py:780
  232.6 2.1 add_convert_fusion.14.refs_1_
  234.7 3.1 add_convert_fusion.2.refs_0_
  237.9 15.8 %shard_map.265 = (bf16[2,192,3840]{2,1,0:T(8,128)(2,1)}, bf16[2,192,3840]{2,1,0:T(8,128)(2,1)}) custom-call(s32[2]{0:T(128)} %pad_add_fusion.where_ref.core_ref, bf16[1,2,192,1024]{3,2,1,0:T(8,128)(2,1)} %add_convert_fusion.2.refs_0_, bf16[2,64,768]{2,1,0:T(8,128)(2,1)} %add_convert_fusion.14.refs_1_, bf16[1024,768]{1,0:T(8,128)(2,1)} %refs_2_.1, ...), custom_call_target="tpu_custom_call" | custom-call | flops 6039797760 | bytes 20054016 | tf_op jit(solution)/shard_map/pallas_call | solution.py:696
  253.7 2.7 collective-permute-start.28
  257.7 7.1 %shard_map.266 = f32[1024,768]{1,0:T(8,128)} custom-call(bf16[2,192,3840]{2,1,0:T(8,128)(2,1)} %get-tuple-element.122.refs_0_, bf16[2,1024,768]{2,1,0:T(8,128)(2,1)} %get-tuple-element.120.refs_6_.refs_1_, bf16[768,3072]{1,0:T(8,128)(2,1)} %get-tuple-element.93.q_w_ref.w2_ref.refs_2_), custom_call_target="tpu_custom_call" | custom-call | flops 2415919104 | bytes 14942208 | tf_op jit(solution)/shard_map/pallas_call | solution.py:780
  264.8 1.7 add_convert_fusion.1.refs_0_
  266.8 1.5 collective-permute-start.29
  268.3 1.9 add_convert_fusion.20.refs_1_
  270.2 6.1 %collective-permute-done.24 = bf16[1,2,192,1024]{3,2,1,0:T(8,128)(2,1)} collective-permute-done((bf16[1,2,192,1024]{3,2,1,0:T(8,128)(2,1)}, bf16[1,2,192,1024]{3,2,1,0:T(8,128)(2,1)}, u32[]{:S(2)}, u32[]{:S(2)}) %collective-permute-start.24) | collective-permute-done | bytes 786464 | tf_op jit(solution)/shard_map/ppermute | solution.py:796
  276.3 2.8 add_convert_fusion.7.refs_2_
  279.1 1.7 collective-permute-start.26
  280.8 27.3 %shard_map.267 = (bf16[3,1024,768]{2,1,0:T(8,128)(2,1)}, f32[6,2,640]{2,1,0:T(2,128)}) custom-call(bf16[1,192,3840]{2,1,0:T(8,128)(2,1)} %add_convert_fusion.1.refs_0_, bf16[1,64,768]{2,1,0:T(8,128)(2,1)} %add_convert_fusion.20.refs_1_, bf16[1,2,192,512]{3,2,1,0:T(8,128)(2,1)} %add_convert_fusion.7.refs_2_, ...), custom_call_target="tpu_custom_call" | custom-call | flops 9059696640 | bytes 15728640 | tf_op jit(solution)/shard_map/pallas_call | solution.py:256
  311.0 2.4 add_convert_fusion.13.refs_0_
  313.4 3.0 add_convert_fusion.4.refs_1_
  316.4 9.7 %shard_map.268 = (bf16[2,192,1536]{2,1,0:T(8,128)(2,1)}, bf16[2,192,1536]{2,1,0:T(8,128)(2,1)}, bf16[2,192,1024]{2,1,0:T(8,128)(2,1)}, bf16[2,192,1024]{2,1,0:T(8,128)(2,1)}) custom-call(s32[2]{0:T(128)} %pad_add_fusion.where_ref.core_ref, bf16[1,2,192,256]{3,2,1,0:T(8,128)(2,1)} %add_convert_fusion.13.refs_0_, ...), custom_call_target="tpu_custom_call" | custom-call | flops 3623878656 | bytes 9830400 | tf_op jit(solution)/shard_map/pallas_call | solution.py:696
  327.6 17.8 %collective-permute-done.32 = bf16[1,192,1920]{2,1,0:T(8,128)(2,1)} collective-permute-done((bf16[1,192,1920]{2,1,0:T(8,128)(2,1)}, bf16[1,192,1920]{2,1,0:T(8,128)(2,1)}, u32[]{:S(2)}, u32[]{:S(2)}) %collective-permute-start.32) | collective-permute-done | bytes 737312 | tf_op jit(solution)/shard_map/ppermute | solution.py:796
  345.3 1.8 add_convert_fusion.9.refs_2_
  350.1 2.1 add_convert_fusion.5.refs_0_
  352.1 10.0 %shard_map.269 = (f32[1024,768]{1,0:T(8,128)}, f32[1,768]{1,0:T(1,128)}) custom-call(bf16[1,192,1536]{2,1,0:T(8,128)(2,1)} %add_convert_fusion.5.refs_0_, bf16[2,192,512]{2,1,0:T(8,128)(2,1)} %copy-done.10, bf16[1,96,1920]{2,1,0:T(8,128)(2,1)} %copy-done.12, bf16[3,1024,768]{2,1,0:T(8,128)(2,1)} %get-tuple-element.128.refs_3_, ...), custom_call_target="tpu_custom_call" | custom-call | flops 3623878656 | bytes 17694720 | tf_op jit(solution)/shard_map/pallas_call | solution.py:780
  362.9 2.2 add_convert_fusion.16
  365.4 1.5 collective-permute-start.50
  368.3 1.7 collective-permute-start.38
  370.0 6.0 %collective-permute-done.45 = bf16[1,48,1920]{2,1,0:T(8,128)(2,1)} collective-permute-done((bf16[1,48,1920]{2,1,0:T(8,128)(2,1)}, bf16[1,48,1920]{2,1,0:T(8,128)(2,1)}, u32[]{:S(2)}, u32[]{:S(2)}) %collective-permute-start.45) | collective-permute-done | bytes 184352 | tf_op jit(solution)/shard_map/ppermute | solution.py:796
  376.0 2.3 add_convert_fusion.15
  379.6 3.0 collective-permute-start.39
  384.0 1.5 collective-permute-start.33
  385.6 11.3 %collective-permute-done.39 = bf16[2,48,512]{2,1,0:T(8,128)(2,1)S(1)} collective-permute-done((bf16[2,48,512]{2,1,0:T(8,128)(2,1)S(1)}, bf16[2,48,512]{2,1,0:T(8,128)(2,1)S(1)}, u32[]{:S(2)}, u32[]{:S(2)}) %collective-permute-start.39) | collective-permute-done | bytes 98336 | tf_op jit(solution)/shard_map/ppermute | solution.py:796
  398.0 1.6 collective-permute-start.40
  402.8 1.6 fusion.4
  405.6 4.9 %collective-permute-done.34 = bf16[1,192,768]{2,1,0:T(8,128)(2,1)S(1)} collective-permute-done((bf16[1,192,768]{2,1,0:T(8,128)(2,1)S(1)}, bf16[1,192,768]{2,1,0:T(8,128)(2,1)S(1)}, u32[]{:S(2)}, u32[]{:S(2)}) %collective-permute-start.34) | collective-permute-done | bytes 294944 | tf_op jit(solution)/shard_map/ppermute | solution.py:796
  411.7 1.8 collective-permute-start.35
  413.6 3.3 collective-permute-done.35
  420.7 2.6 collective-permute-done.36
  426.5 4.0 collective-permute-done.41
  430.5 2.8 collective-permute-start.42
  434.8 7.3 %collective-permute-done.42 = bf16[1,96,1280]{2,1,0:T(8,128)(2,1)S(1)} collective-permute-done((bf16[1,96,1280]{2,1,0:T(8,128)(2,1)S(1)}, bf16[1,96,1280]{2,1,0:T(8,128)(2,1)S(1)}, u32[]{:S(2)}, u32[]{:S(2)}) %collective-permute-start.42) | collective-permute-done | bytes 245792 | tf_op jit(solution)/shard_map/ppermute | solution.py:796
  444.9 6.1 %collective-permute-done.43 = bf16[1,192,1280]{2,1,0:T(8,128)(2,1)S(1)} collective-permute-done((bf16[1,192,1280]{2,1,0:T(8,128)(2,1)S(1)}, bf16[1,192,1280]{2,1,0:T(8,128)(2,1)S(1)}, u32[]{:S(2)}, u32[]{:S(2)}) %collective-permute-start.43) | collective-permute-done | bytes 491552 | tf_op jit(solution)/shard_map/ppermute | solution.py:796
  453.1 1.4 multiply_reduce_fusion
  454.5 24.9 %all-gather.3.cloned.1.call-done = bf16[24,192,256]{2,1,0:T(8,128)(2,1)} async-done(((bf16[3,192,256]{2,1,0:T(8,128)(2,1)}), bf16[24,192,256]{2,1,0:T(8,128)(2,1)}) %all-gather.3.cloned.1.call-update) | async-done | bytes 2359312 | tf_op jit(solution)/shard_map/all_gather | solution.py:1066
  479.4 4.7 shard_map.270
  (222 shorter events, 58.5 us)
Async XLA Ops:
  7.2 472.2 %all-gather.3.cloned.1.call-start = ((), (), s32[]{:S(2)}) async-start(), calls=%async_computation | async-start | bytes 2654208 | tf_op jit(solution)/shard_map/all_gather | solution.py:1066
  8.8 21.6 %copy-start.19 = (bf16[192,1536]{1,0:T(8,128)(2,1)S(1)}, bf16[192,1536]{1,0:T(8,128)(2,1)}, u32[]{:S(2)}) copy-start(bf16[192,1536]{1,0:T(8,128)(2,1)} %param.27) | copy-start | bytes 1769476
  11.1 21.7 %copy-start.6 = (bf16[192,3328]{1,0:T(8,128)(2,1)}, bf16[192,3328]{1,0:T(8,128)(2,1)S(1)}, u32[]{:S(2)}) copy-start(bf16[192,3328]{1,0:T(8,128)(2,1)S(1)} %concatenate.31.refs_0_) | copy-start | bytes 3833860
  11.1 20.2 %copy-start.13 = (bf16[192,768]{1,0:T(8,128)(2,1)S(1)}, bf16[192,768]{1,0:T(8,128)(2,1)}, u32[]{:S(2)}) copy-start(bf16[192,768]{1,0:T(8,128)(2,1)} %param.26) | copy-start | bytes 884740
  11.1 20.9 %copy-start.23 = (bf16[192,768]{1,0:T(8,128)(2,1)S(1)}, bf16[192,768]{1,0:T(8,128)(2,1)}, u32[]{:S(2)}) copy-start(bf16[192,768]{1,0:T(8,128)(2,1)} %param.28) | copy-start | bytes 884740
  11.1 21.7 %copy-start.31 = (s32[1024]{0:T(1024)S(1)}, s32[1024]{0:T(1024)}, u32[]{:S(2)}) copy-start(s32[1024]{0:T(1024)} %param.19) | copy-start | bytes 12292
  11.2 17.5 %collective-permute-start = (bf16[192,1664]{1,0:T(8,128)(2,1)S(1)}, bf16[192,1664]{1,0:T(8,128)(2,1)}, u32[]{:S(2)}, u32[]{:S(2)}) collective-permute-start(bf16[192,1664]{1,0:T(8,128)(2,1)S(1)} %constant_dynamic-slice_fusion.1), channel_id=1, source_target_pairs={{0,2},{1,3},{2,0},{3,1},{4,6},{5,7},{6,4},{7,5},{8,10},{9,11},{10,... | collective-permute-start | bytes 1916936 | tf_op jit(solution)/shard_map/ppermute | solution.py:796
  28.7 15.9 %collective-permute-start.3 = (bf16[192,1664]{1,0:T(8,128)(2,1)}, bf16[192,1664]{1,0:T(8,128)(2,1)}, u32[]{:S(2)}, u32[]{:S(2)}) collective-permute-start(bf16[192,1664]{1,0:T(8,128)(2,1)} %collective-permute-done.refs_2_), channel_id=1, source_target_pairs={{0,4},{4,0},{8,12},{12,8},{16,20},{20,16},{24,28},{28,24},{1,5},{5... | collective-permute-start | bytes 1916936 | tf_op jit(solution)/shard_map/ppermute | solution.py:796
  31.3 17.7 %collective-permute-start.2 = (bf16[192,3328]{1,0:T(8,128)(2,1)S(1)}, bf16[192,3328]{1,0:T(8,128)(2,1)}, u32[]{:S(2)}, u32[]{:S(2)}) collective-permute-start(bf16[192,3328]{1,0:T(8,128)(2,1)S(1)} %concatenate.31.refs_0_), channel_id=1, source_target_pairs={{0,1},{1,0},{2,3},{3,2},{4,5},{5,4},{6,7},{7,6},{8,9},{9,8},{10,11... | collective-permute-start | bytes 3833864 | tf_op jit(solution)/shard_map/ppermute | solution.py:796
  33.7 15.3 %collective-permute-start.4 = (bf16[192,1664]{1,0:T(8,128)(2,1)}, bf16[192,1664]{1,0:T(8,128)(2,1)}, u32[]{:S(2)}, u32[]{:S(2)}) collective-permute-start(bf16[192,1664]{1,0:T(8,128)(2,1)} %collective-permute-done.refs_2_), channel_id=1, source_target_pairs={{0,1},{1,0},{2,3},{3,2},{4,5},{5,4},{6,7},{7,6},{8,9},{9,8},{10,11... | collective-permute-start | bytes 1916936 | tf_op jit(solution)/shard_map/ppermute | solution.py:796
  44.6 4.4 collective-permute-start.5
  45.7 15.9 %collective-permute-start.1 = (bf16[192,1536]{1,0:T(8,128)(2,1)S(1)}, bf16[192,1536]{1,0:T(8,128)(2,1)}, u32[]{:S(2)}, u32[]{:S(2)}) collective-permute-start(bf16[192,1536]{1,0:T(8,128)(2,1)S(1)} %constant_dynamic-slice_fusion.2), channel_id=1, source_target_pairs={{0,2},{1,3},{2,0},{3,1},{4,6},{5,7},{6,4},{7,5},{8,10},{9,11},{10,... | collective-permute-start | bytes 1769480 | tf_op jit(solution)/shard_map/ppermute | solution.py:796
  61.6 22.8 %collective-permute-start.7 = (bf16[192,1536]{1,0:T(8,128)(2,1)}, bf16[192,1536]{1,0:T(8,128)(2,1)S(1)}, u32[]{:S(2)}, u32[]{:S(2)}) collective-permute-start(bf16[192,1536]{1,0:T(8,128)(2,1)} %collective-permute-done.1.refs_4_), channel_id=1, source_target_pairs={{0,4},{4,0},{8,12},{12,8},{16,20},{20,16},{24,28},{28,24},{1,5},{5... | collective-permute-start | bytes 1769480 | tf_op jit(solution)/shard_map/ppermute | solution.py:796
  63.0 35.7 %collective-permute-start.6 = (bf16[192,3072]{1,0:T(8,128)(2,1)}, bf16[192,3072]{1,0:T(8,128)(2,1)S(1)}, u32[]{:S(2)}, u32[]{:S(2)}) collective-permute-start(bf16[192,3072]{1,0:T(8,128)(2,1)} %constant_dynamic-update-slice_fusion.refs_2_), channel_id=1, source_target_pairs={{0,1},{1,0},{2,3},{3,2},{4,5},{5,4},{6,7},{7,6},{8,9},{9,8},{10,11... | collective-permute-start | bytes 3538952 | tf_op jit(solution)/shard_map/ppermute | solution.py:796
  63.9 32.7 %collective-permute-start.8 = (bf16[192,1536]{1,0:T(8,128)(2,1)}, bf16[192,1536]{1,0:T(8,128)(2,1)S(1)}, u32[]{:S(2)}, u32[]{:S(2)}) collective-permute-start(bf16[192,1536]{1,0:T(8,128)(2,1)} %collective-permute-done.1.refs_4_), channel_id=1, source_target_pairs={{0,1},{1,0},{2,3},{3,2},{4,5},{5,4},{6,7},{7,6},{8,9},{9,8},{10,11... | collective-permute-start | bytes 1769480 | tf_op jit(solution)/shard_map/ppermute | solution.py:796
  64.4 32.2 %collective-permute-start.10 = (bf16[192,2048]{1,0:T(8,128)(2,1)S(1)}, bf16[192,2048]{1,0:T(8,128)(2,1)S(1)}, u32[]{:S(2)}, u32[]{:S(2)}) collective-permute-start(bf16[192,2048]{1,0:T(8,128)(2,1)S(1)} %constant_dynamic-slice_fusion.refs_1_), channel_id=1, source_target_pairs={{0,2},{1,3},{2,0},{3,1},{4,6},{5,7},{6,4},{7,5},{8,10},{9,11},{10,... | collective-permute-start | bytes 2359304 | tf_op jit(solution)/shard_map/ppermute | solution.py:796
  65.9 18.6 %copy-start.11 = (bf16[512,384]{1,0:T(8,128)(2,1)S(1)}, bf16[512,384]{1,0:T(8,128)(2,1)}, u32[]{:S(2)}) copy-start(bf16[512,384]{1,0:T(8,128)(2,1)} %constant_dynamic-slice_fusion.3.refs_0_) | copy-start | bytes 1179652
  65.9 30.6 %copy-start.25 = (bf16[512,768]{1,0:T(8,128)(2,1)S(1)}, bf16[512,768]{1,0:T(8,128)(2,1)}, u32[]{:S(2)}) copy-start(bf16[512,768]{1,0:T(8,128)(2,1)} %own_o.1) | copy-start | bytes 2359300
  84.4 12.7 %collective-permute-start.9 = (bf16[192,1536]{1,0:T(8,128)(2,1)S(1)}, bf16[192,1536]{1,0:T(8,128)(2,1)S(1)}, u32[]{:S(2)}, u32[]{:S(2)}) collective-permute-start(bf16[192,1536]{1,0:T(8,128)(2,1)S(1)} %collective-permute-done.7.refs_5_), channel_id=1, source_target_pairs={{0,1},{1,0},{2,3},{3,2},{4,5},{5,4},{6,7},{7,6},{8,9},{9,8},{10,11... | collective-permute-start | bytes 1769480 | tf_op jit(solution)/shard_map/ppermute | solution.py:796
  84.5 11.5 %collective-permute-start.15 = (bf16[512,384]{1,0:T(8,128)(2,1)S(1)}, bf16[512,384]{1,0:T(8,128)(2,1)S(1)}, u32[]{:S(2)}, u32[]{:S(2)}) collective-permute-start(bf16[512,384]{1,0:T(8,128)(2,1)S(1)} %copy-done.11), channel_id=1, source_target_pairs={{0,2},{1,3},{2,0},{3,1},{4,6},{5,7},{6,4},{7,5},{8,10},{9,11},{10,... | collective-permute-start | bytes 1179656 | tf_op jit(solution)/shard_map/ppermute | solution.py:796
  96.0 20.1 %copy-start.44 = (bf16[512,384]{1,0:T(8,128)(2,1)}, bf16[512,384]{1,0:T(8,128)(2,1)S(1)}, u32[]{:S(2)}) copy-start(bf16[512,384]{1,0:T(8,128)(2,1)S(1)} %collective-permute-done.15.y_o) | copy-start | bytes 1179652
  96.0 35.6 %collective-permute-start.17 = (bf16[512,384]{1,0:T(8,128)(2,1)S(1)}, bf16[512,384]{1,0:T(8,128)(2,1)S(1)}, u32[]{:S(2)}, u32[]{:S(2)}) collective-permute-start(bf16[512,384]{1,0:T(8,128)(2,1)S(1)} %collective-permute-done.15.y_o), channel_id=1, source_target_pairs={{0,4},{4,0},{8,12},{12,8},{16,20},{20,16},{24,28},{28,24},{1,5},{5... | collective-permute-start | bytes 1179656 | tf_op jit(solution)/shard_map/ppermute | solution.py:796
  96.6 35.0 %copy-start.36 = (bf16[192,2048]{1,0:T(8,128)(2,1)}, bf16[192,2048]{1,0:T(8,128)(2,1)S(1)}, u32[]{:S(2)}) copy-start(bf16[192,2048]{1,0:T(8,128)(2,1)S(1)} %collective-permute-done.10.y_in) | copy-start | bytes 2359300
  96.6 35.6 %collective-permute-start.18 = (bf16[512,384]{1,0:T(8,128)(2,1)S(1)}, bf16[512,384]{1,0:T(8,128)(2,1)}, u32[]{:S(2)}, u32[]{:S(2)}) collective-permute-start(bf16[512,384]{1,0:T(8,128)(2,1)S(1)} %collective-permute-done.15.y_o), channel_id=1, source_target_pairs={{0,1},{1,0},{2,3},{3,2},{4,5},{5,4},{6,7},{7,6},{8,9},{9,8},{10,11... | collective-permute-start | bytes 1179656 | tf_op jit(solution)/shard_map/ppermute | solution.py:796
  96.6 35.6 %collective-permute-start.16 = (bf16[512,768]{1,0:T(8,128)(2,1)S(1)}, bf16[512,768]{1,0:T(8,128)(2,1)S(1)}, u32[]{:S(2)}, u32[]{:S(2)}) collective-permute-start(bf16[512,768]{1,0:T(8,128)(2,1)S(1)} %copy-done.25), channel_id=1, source_target_pairs={{0,1},{1,0},{2,3},{3,2},{4,5},{5,4},{6,7},{7,6},{8,9},{9,8},{10,11... | collective-permute-start | bytes 2359304 | tf_op jit(solution)/shard_map/ppermute | solution.py:796
  97.2 34.4 %collective-permute-start.12 = (bf16[192,2048]{1,0:T(8,128)(2,1)S(1)}, bf16[192,2048]{1,0:T(8,128)(2,1)S(1)}, u32[]{:S(2)}, u32[]{:S(2)}) collective-permute-start(bf16[192,2048]{1,0:T(8,128)(2,1)S(1)} %collective-permute-done.10.y_in), channel_id=1, source_target_pairs={{0,4},{4,0},{8,12},{12,8},{16,20},{20,16},{24,28},{28,24},{1,5},{5... | collective-permute-start | bytes 2359304 | tf_op jit(solution)/shard_map/ppermute | solution.py:796
  98.7 36.9 %collective-permute-start.11 = (bf16[192,4096]{1,0:T(8,128)(2,1)S(1)}, bf16[192,4096]{1,0:T(8,128)(2,1)S(1)}, u32[]{:S(2)}, u32[]{:S(2)}) collective-permute-start(bf16[192,4096]{1,0:T(8,128)(2,1)S(1)} %copy-done.1), channel_id=1, source_target_pairs={{0,1},{1,0},{2,3},{3,2},{4,5},{5,4},{6,7},{7,6},{8,9},{9,8},{10,11... | collective-permute-start | bytes 4718600 | tf_op jit(solution)/shard_map/ppermute | solution.py:796
  131.6 2.4 collective-permute-start.13
  131.7 3.9 collective-permute-start.14
  132.2 3.5 collective-permute-start.19
  183.6 10.5 %collective-permute-start.20 = (bf16[2,2,192,2048]{3,2,1,0:T(8,128)(2,1)}, bf16[2,2,192,2048]{3,2,1,0:T(8,128)(2,1)}, u32[]{:S(2)}, u32[]{:S(2)}) collective-permute-start(bf16[2,2,192,2048]{3,2,1,0:T(8,128)(2,1)} %get-tuple-element.106), channel_id=1, source_target_pairs={{0,1},{1,0},{2,3},{3,2},{4,5},{5,4},{6,7},{7,6},{8,9},{9,8},{10,11... | collective-permute-start | bytes 9437192 | tf_op jit(solution)/shard_map/ppermute | solution.py:796
  183.8 8.1 %collective-permute-start.22 = (bf16[2,512,768]{2,1,0:T(8,128)(2,1)}, bf16[2,512,768]{2,1,0:T(8,128)(2,1)}, u32[]{:S(2)}, u32[]{:S(2)}) collective-permute-start(bf16[2,512,768]{2,1,0:T(8,128)(2,1)} %get-tuple-element.110), channel_id=1, source_target_pairs={{0,1},{1,0},{2,3},{3,2},{4,5},{5,4},{6,7},{7,6},{8,9},{9,8},{10,11... | collective-permute-start | bytes 4718600 | tf_op jit(solution)/shard_map/ppermute | solution.py:796
  193.2 27.0 %collective-permute-start.23 = (bf16[2,256,768]{2,1,0:T(8,128)(2,1)S(1)}, bf16[2,256,768]{2,1,0:T(8,128)(2,1)S(1)}, u32[]{:S(2)}, u32[]{:S(2)}) collective-permute-start(bf16[2,256,768]{2,1,0:T(8,128)(2,1)S(1)} %add_convert_fusion.3.refs_1_), channel_id=1, source_target_pairs={{0,4},{4,0},{8,12},{12,8},{16,20},{20,16},{24,28},{28,24},{1,5},{5... | collective-permute-start | bytes 2359304 | tf_op jit(solution)/shard_map/ppermute | solution.py:796
  197.2 37.5 %collective-permute-start.21 = (bf16[1,2,192,2048]{3,2,1,0:T(8,128)(2,1)}, bf16[1,2,192,2048]{3,2,1,0:T(8,128)(2,1)}, u32[]{:S(2)}, u32[]{:S(2)}) collective-permute-start(bf16[1,2,192,2048]{3,2,1,0:T(8,128)(2,1)} %add_convert_fusion.refs_0_), channel_id=1, source_target_pairs={{0,2},{1,3},{2,0},{3,1},{4,6},{5,7},{6,4},{7,5},{8,10},{9,11},{10,... | collective-permute-start | bytes 4718600 | tf_op jit(solution)/shard_map/ppermute | solution.py:796
  221.8 10.8 %collective-permute-start.25 = (bf16[2,128,768]{2,1,0:T(8,128)(2,1)S(1)}, bf16[2,128,768]{2,1,0:T(8,128)(2,1)}, u32[]{:S(2)}, u32[]{:S(2)}) collective-permute-start(bf16[2,128,768]{2,1,0:T(8,128)(2,1)S(1)} %add_convert_fusion.8.refs_0_), channel_id=1, source_target_pairs={{0,8},{4,12},{8,0},{12,4},{16,24},{20,28},{24,16},{28,20},{1,9},{5... | collective-permute-start | bytes 1179656 | tf_op jit(solution)/shard_map/ppermute | solution.py:796
  253.7 11.1 %collective-permute-start.27 = (bf16[2,192,3840]{2,1,0:T(8,128)(2,1)}, bf16[2,192,3840]{2,1,0:T(8,128)(2,1)S(1)}, u32[]{:S(2)}, u32[]{:S(2)}) collective-permute-start(bf16[2,192,3840]{2,1,0:T(8,128)(2,1)} %get-tuple-element.124), channel_id=1, source_target_pairs={{0,1},{1,0},{2,3},{3,2},{4,5},{5,4},{6,7},{7,6},{8,9},{9,8},{10,11... | collective-permute-start | bytes 8847368 | tf_op jit(solution)/shard_map/ppermute | solution.py:796
  253.7 14.6 %collective-permute-start.28 = (bf16[2,64,768]{2,1,0:T(8,128)(2,1)S(1)}, bf16[2,64,768]{2,1,0:T(8,128)(2,1)S(1)}, u32[]{:S(2)}, u32[]{:S(2)}) collective-permute-start(bf16[2,64,768]{2,1,0:T(8,128)(2,1)S(1)} %copy-done.27), channel_id=1, source_target_pairs={{0,16},{4,20},{8,24},{12,28},{16,0},{20,4},{24,8},{28,12},{1,17},{... | collective-permute-start | bytes 589832 | tf_op jit(solution)/shard_map/ppermute | solution.py:796
  256.3 19.9 %collective-permute-start.24 = (bf16[1,2,192,1024]{3,2,1,0:T(8,128)(2,1)}, bf16[1,2,192,1024]{3,2,1,0:T(8,128)(2,1)}, u32[]{:S(2)}, u32[]{:S(2)}) collective-permute-start(bf16[1,2,192,1024]{3,2,1,0:T(8,128)(2,1)} %add_convert_fusion.2.refs_0_), channel_id=1, source_target_pairs={{0,4},{4,0},{8,12},{12,8},{16,20},{20,16},{24,28},{28,24},{1,5},{5... | collective-permute-start | bytes 2359304 | tf_op jit(solution)/shard_map/ppermute | solution.py:796
  266.8 46.6 %collective-permute-start.29 = (bf16[1,192,3840]{2,1,0:T(8,128)(2,1)}, bf16[1,192,3840]{2,1,0:T(8,128)(2,1)}, u32[]{:S(2)}, u32[]{:S(2)}) collective-permute-start(bf16[1,192,3840]{2,1,0:T(8,128)(2,1)} %add_convert_fusion.1.refs_0_), channel_id=1, source_target_pairs={{0,2},{1,3},{2,0},{3,1},{4,6},{5,7},{6,4},{7,5},{8,10},{9,11},{10,... | collective-permute-start | bytes 4423688 | tf_op jit(solution)/shard_map/ppermute | solution.py:796
  279.1 31.9 %collective-permute-start.26 = (bf16[1,2,192,512]{3,2,1,0:T(8,128)(2,1)}, bf16[1,2,192,512]{3,2,1,0:T(8,128)(2,1)S(1)}, u32[]{:S(2)}, u32[]{:S(2)}) collective-permute-start(bf16[1,2,192,512]{3,2,1,0:T(8,128)(2,1)} %add_convert_fusion.7.refs_2_), channel_id=1, source_target_pairs={{0,8},{4,12},{8,0},{12,4},{16,24},{20,28},{24,16},{28,20},{1,9},{5... | collective-permute-start | bytes 1179656 | tf_op jit(solution)/shard_map/ppermute | solution.py:796
  326.1 24.0 %collective-permute-start.30 = (bf16[2,192,1536]{2,1,0:T(8,128)(2,1)}, bf16[2,192,1536]{2,1,0:T(8,128)(2,1)}, u32[]{:S(2)}, u32[]{:S(2)}) collective-permute-start(bf16[2,192,1536]{2,1,0:T(8,128)(2,1)} %get-tuple-element.133), channel_id=1, source_target_pairs={{0,1},{1,0},{2,3},{3,2},{4,5},{5,4},{6,7},{7,6},{8,9},{9,8},{10,11... | collective-permute-start | bytes 3538952 | tf_op jit(solution)/shard_map/ppermute | solution.py:796
  326.1 19.2 %collective-permute-start.32 = (bf16[1,192,1920]{2,1,0:T(8,128)(2,1)}, bf16[1,192,1920]{2,1,0:T(8,128)(2,1)}, u32[]{:S(2)}, u32[]{:S(2)}) collective-permute-start(bf16[1,192,1920]{2,1,0:T(8,128)(2,1)} %add_convert_fusion.4.refs_1_), channel_id=1, source_target_pairs={{0,4},{4,0},{8,12},{12,8},{16,20},{20,16},{24,28},{28,24},{1,5},{5... | collective-permute-start | bytes 2211848 | tf_op jit(solution)/shard_map/ppermute | solution.py:796
  327.4 20.1 %collective-permute-start.31 = (bf16[2,192,1024]{2,1,0:T(8,128)(2,1)}, bf16[2,192,1024]{2,1,0:T(8,128)(2,1)}, u32[]{:S(2)}, u32[]{:S(2)}) collective-permute-start(bf16[2,192,1024]{2,1,0:T(8,128)(2,1)} %get-tuple-element.136), channel_id=1, source_target_pairs={{0,1},{1,0},{2,3},{3,2},{4,5},{5,4},{6,7},{7,6},{8,9},{9,8},{10,11... | collective-permute-start | bytes 2359304 | tf_op jit(solution)/shard_map/ppermute | solution.py:796
  327.6 22.5 %copy-start.15 = (bf16[2,192,1536]{2,1,0:T(8,128)(2,1)S(1)}, bf16[2,192,1536]{2,1,0:T(8,128)(2,1)}, u32[]{:S(2)}) copy-start(bf16[2,192,1536]{2,1,0:T(8,128)(2,1)} %get-tuple-element.132) | copy-start | bytes 3538948
  347.1 15.1 %collective-permute-start.44 = (bf16[1,96,1920]{2,1,0:T(8,128)(2,1)S(1)}, bf16[1,96,1920]{2,1,0:T(8,128)(2,1)S(1)}, u32[]{:S(2)}, u32[]{:S(2)}) collective-permute-start(bf16[1,96,1920]{2,1,0:T(8,128)(2,1)S(1)} %add_convert_fusion.9.refs_2_), channel_id=1, source_target_pairs={{0,8},{4,12},{8,0},{12,4},{16,24},{20,28},{24,16},{28,20},{1,9},{5... | collective-permute-start | bytes 1105928 | tf_op jit(solution)/shard_map/ppermute | solution.py:796
  348.8 18.1 %collective-permute-start.37 = (bf16[2,192,512]{2,1,0:T(8,128)(2,1)S(1)}, bf16[2,192,512]{2,1,0:T(8,128)(2,1)}, u32[]{:S(2)}, u32[]{:S(2)}) collective-permute-start(bf16[2,192,512]{2,1,0:T(8,128)(2,1)S(1)} %add_convert_fusion.6.refs_1_), channel_id=1, source_target_pairs={{0,4},{4,0},{8,12},{12,8},{16,20},{20,16},{24,28},{28,24},{1,5},{5... | collective-permute-start | bytes 1179656 | tf_op jit(solution)/shard_map/ppermute | solution.py:796
  365.1 10.9 %collective-permute-start.45 = (bf16[1,48,1920]{2,1,0:T(8,128)(2,1)}, bf16[1,48,1920]{2,1,0:T(8,128)(2,1)}, u32[]{:S(2)}, u32[]{:S(2)}) collective-permute-start(bf16[1,48,1920]{2,1,0:T(8,128)(2,1)} %add_convert_fusion.16), channel_id=1, source_target_pairs={{0,16},{4,20},{8,24},{12,28},{16,0},{20,4},{24,8},{28,12},{1,17},{... | collective-permute-start | bytes 552968 | tf_op jit(solution)/shard_map/ppermute | solution.py:796
  365.4 17.1 %collective-permute-start.50 = (bf16[1,64,768]{2,1,0:T(8,128)(2,1)}, bf16[1,64,768]{2,1,0:T(8,128)(2,1)S(1)}, u32[]{:S(2)}, u32[]{:S(2)}) collective-permute-start(bf16[1,64,768]{2,1,0:T(8,128)(2,1)} %add_convert_fusion.20.refs_1_), channel_id=1, source_target_pairs={{0,2},{1,3},{2,0},{3,1},{4,6},{5,7},{6,4},{7,5},{8,10},{9,11},{10,... | collective-permute-start | bytes 294920 | tf_op jit(solution)/shard_map/ppermute | solution.py:796
  368.3 10.0 %collective-permute-start.38 = (bf16[2,96,512]{2,1,0:T(8,128)(2,1)S(1)}, bf16[2,96,512]{2,1,0:T(8,128)(2,1)S(1)}, u32[]{:S(2)}, u32[]{:S(2)}) collective-permute-start(bf16[2,96,512]{2,1,0:T(8,128)(2,1)S(1)} %add_convert_fusion.12), channel_id=1, source_target_pairs={{0,8},{4,12},{8,0},{12,4},{16,24},{20,28},{24,16},{28,20},{1,9},{5... | collective-permute-start | bytes 589832 | tf_op jit(solution)/shard_map/ppermute | solution.py:796
  378.3 21.4 %collective-permute-start.46 = (bf16[1,48,1920]{2,1,0:T(8,128)(2,1)}, bf16[1,48,1920]{2,1,0:T(8,128)(2,1)S(1)}, u32[]{:S(2)}, u32[]{:S(2)}) collective-permute-start(bf16[1,48,1920]{2,1,0:T(8,128)(2,1)} %add_convert_fusion.15), channel_id=1, source_target_pairs={{0,16},{4,20},{8,24},{12,28},{16,0},{20,4},{24,8},{28,12},{1,17},{... | collective-permute-start | bytes 552968 | tf_op jit(solution)/shard_map/ppermute | solution.py:796
  379.6 21.2 %copy-start.16 = (bf16[2,192,1536]{2,1,0:T(8,128)(2,1)S(1)}, bf16[2,192,1536]{2,1,0:T(8,128)(2,1)}, u32[]{:S(2)}) copy-start(bf16[2,192,1536]{2,1,0:T(8,128)(2,1)} %get-tuple-element.132) | copy-start | bytes 3538948
  379.6 17.3 %collective-permute-start.39 = (bf16[2,48,512]{2,1,0:T(8,128)(2,1)S(1)}, bf16[2,48,512]{2,1,0:T(8,128)(2,1)S(1)}, u32[]{:S(2)}, u32[]{:S(2)}) collective-permute-start(bf16[2,48,512]{2,1,0:T(8,128)(2,1)S(1)} %add_convert_fusion.19), channel_id=1, source_target_pairs={{0,16},{4,20},{8,24},{12,28},{16,0},{20,4},{24,8},{28,12},{1,17},{... | collective-permute-start | bytes 294920 | tf_op jit(solution)/shard_map/ppermute | solution.py:796
  383.8 19.0 %copy-start.21 = (bf16[1,2,192,512]{3,2,1,0:T(8,128)(2,1)S(1)}, bf16[1,2,192,512]{3,2,1,0:T(8,128)(2,1)}, u32[]{:S(2)}) copy-start(bf16[1,2,192,512]{3,2,1,0:T(8,128)(2,1)} %copy-done.20) | copy-start | bytes 1179652
  383.9 18.9 %collective-permute-start.49 = (bf16[1,2,192,256]{3,2,1,0:T(8,128)(2,1)}, bf16[1,2,192,256]{3,2,1,0:T(8,128)(2,1)S(1)}, u32[]{:S(2)}, u32[]{:S(2)}) collective-permute-start(bf16[1,2,192,256]{3,2,1,0:T(8,128)(2,1)} %add_convert_fusion.13.refs_0_), channel_id=1, source_target_pairs={{0,16},{4,20},{8,24},{12,28},{16,0},{20,4},{24,8},{28,12},{1,17},{... | collective-permute-start | bytes 589832 | tf_op jit(solution)/shard_map/ppermute | solution.py:796
  384.0 16.7 %collective-permute-start.33 = (bf16[1,192,1536]{2,1,0:T(8,128)(2,1)S(1)}, bf16[1,192,1536]{2,1,0:T(8,128)(2,1)S(1)}, u32[]{:S(2)}, u32[]{:S(2)}) collective-permute-start(bf16[1,192,1536]{2,1,0:T(8,128)(2,1)S(1)} %copy-done.7), channel_id=1, source_target_pairs={{0,2},{1,3},{2,0},{3,1},{4,6},{5,7},{6,4},{7,5},{8,10},{9,11},{10,... | collective-permute-start | bytes 1769480 | tf_op jit(solution)/shard_map/ppermute | solution.py:796
  398.0 6.4 %collective-permute-start.40 = (bf16[1,48,512]{2,1,0:T(8,128)(2,1)S(1)}, bf16[1,48,512]{2,1,0:T(8,128)(2,1)S(1)}, u32[]{:S(2)}, u32[]{:S(2)}) collective-permute-start(bf16[1,48,512]{2,1,0:T(8,128)(2,1)S(1)} %add_convert_fusion.24), channel_id=1, source_target_pairs={{0,2},{1,3},{2,0},{3,1},{4,6},{5,7},{6,4},{7,5},{8,10},{9,11},{10,... | collective-permute-start | bytes 147464 | tf_op jit(solution)/shard_map/ppermute | solution.py:796
  400.6 12.8 %collective-permute-start.47 = (bf16[1,96,1920]{2,1,0:T(8,128)(2,1)S(1)}, bf16[1,96,1920]{2,1,0:T(8,128)(2,1)S(1)}, u32[]{:S(2)}, u32[]{:S(2)}) collective-permute-start(bf16[1,96,1920]{2,1,0:T(8,128)(2,1)S(1)} %pad_maximum_fusion.2), channel_id=1, source_target_pairs={{0,8},{4,12},{8,0},{12,4},{16,24},{20,28},{24,16},{28,20},{1,9},{5... | collective-permute-start | bytes 1105928 | tf_op jit(solution)/shard_map/ppermute | solution.py:796
  402.0 8.5 %collective-permute-start.34 = (bf16[1,192,768]{2,1,0:T(8,128)(2,1)S(1)}, bf16[1,192,768]{2,1,0:T(8,128)(2,1)S(1)}, u32[]{:S(2)}, u32[]{:S(2)}) collective-permute-start(bf16[1,192,768]{2,1,0:T(8,128)(2,1)S(1)} %add_convert_fusion.10), channel_id=1, source_target_pairs={{0,4},{4,0},{8,12},{12,8},{16,20},{20,16},{24,28},{28,24},{1,5},{5... | collective-permute-start | bytes 884744 | tf_op jit(solution)/shard_map/ppermute | solution.py:796
  411.7 5.2 %collective-permute-start.35 = (bf16[1,96,768]{2,1,0:T(8,128)(2,1)S(1)}, bf16[1,96,768]{2,1,0:T(8,128)(2,1)S(1)}, u32[]{:S(2)}, u32[]{:S(2)}) collective-permute-start(bf16[1,96,768]{2,1,0:T(8,128)(2,1)S(1)} %add_convert_fusion.17), channel_id=1, source_target_pairs={{0,8},{4,12},{8,0},{12,4},{16,24},{20,28},{24,16},{28,20},{1,9},{5... | collective-permute-start | bytes 442376 | tf_op jit(solution)/shard_map/ppermute | solution.py:796
  418.0 5.3 %collective-permute-start.36 = (bf16[1,48,768]{2,1,0:T(8,128)(2,1)S(1)}, bf16[1,48,768]{2,1,0:T(8,128)(2,1)S(1)}, u32[]{:S(2)}, u32[]{:S(2)}) collective-permute-start(bf16[1,48,768]{2,1,0:T(8,128)(2,1)S(1)} %add_convert_fusion.22), channel_id=1, source_target_pairs={{0,16},{4,20},{8,24},{12,28},{16,0},{20,4},{24,8},{28,12},{1,17},{... | collective-permute-start | bytes 221192 | tf_op jit(solution)/shard_map/ppermute | solution.py:796
  419.3 15.2 %collective-permute-start.48 = (bf16[1,192,1920]{2,1,0:T(8,128)(2,1)S(1)}, bf16[1,192,1920]{2,1,0:T(8,128)(2,1)S(1)}, u32[]{:S(2)}, u32[]{:S(2)}) collective-permute-start(bf16[1,192,1920]{2,1,0:T(8,128)(2,1)S(1)} %pad_maximum_fusion), channel_id=1, source_target_pairs={{0,4},{4,0},{8,12},{12,8},{16,20},{20,16},{24,28},{28,24},{1,5},{5... | collective-permute-start | bytes 2211848 | tf_op jit(solution)/shard_map/ppermute | solution.py:796
  424.4 6.1 %collective-permute-start.41 = (bf16[1,48,1280]{2,1,0:T(8,128)(2,1)S(1)}, bf16[1,48,1280]{2,1,0:T(8,128)(2,1)S(1)}, u32[]{:S(2)}, u32[]{:S(2)}) collective-permute-start(bf16[1,48,1280]{2,1,0:T(8,128)(2,1)S(1)} %pad_maximum_fusion.5), channel_id=1, source_target_pairs={{0,16},{4,20},{8,24},{12,28},{16,0},{20,4},{24,8},{28,12},{1,17},{... | collective-permute-start | bytes 368648 | tf_op jit(solution)/shard_map/ppermute | solution.py:796
  430.5 11.6 %collective-permute-start.42 = (bf16[1,96,1280]{2,1,0:T(8,128)(2,1)S(1)}, bf16[1,96,1280]{2,1,0:T(8,128)(2,1)S(1)}, u32[]{:S(2)}, u32[]{:S(2)}) collective-permute-start(bf16[1,96,1280]{2,1,0:T(8,128)(2,1)S(1)} %pad_maximum_fusion.4), channel_id=1, source_target_pairs={{0,8},{4,12},{8,0},{12,4},{16,24},{20,28},{24,16},{28,20},{1,9},{5... | collective-permute-start | bytes 737288 | tf_op jit(solution)/shard_map/ppermute | solution.py:796
  442.2 8.9 %collective-permute-start.43 = (bf16[1,192,1280]{2,1,0:T(8,128)(2,1)S(1)}, bf16[1,192,1280]{2,1,0:T(8,128)(2,1)S(1)}, u32[]{:S(2)}, u32[]{:S(2)}) collective-permute-start(bf16[1,192,1280]{2,1,0:T(8,128)(2,1)S(1)} %pad_maximum_fusion.1), channel_id=1, source_target_pairs={{0,4},{4,0},{8,12},{12,8},{16,20},{20,16},{24,28},{28,24},{1,5},{5... | collective-permute-start | bytes 1474568 | tf_op jit(solution)/shard_map/ppermute | solution.py:796
  (35 other events, 191.5 us)
Sparse Core Ops, SparseCore 0:
  426.6 52.7 all-gather.2

commit v3 on v2

--- a/solution.py
+++ b/solution.py
@@ -27,6 +27,7 @@
 bf16 = jnp.bfloat16
 f32 = jnp.float32
 VMEM_LIMIT = 56 * 1024 * 1024
+LIGHT = pl.CostEstimate(flops=1000000, bytes_accessed=100000, transcendentals=0)
 
 bucket_edges = np.array(
     list(range(1, 16)) + [int(math.ceil(16.0 * 8.0 ** ((b - 16) / 16.0))) for b in range(16, 32)],
@@ -134,11 +135,7 @@
         out_shape=[jax.ShapeDtypeStruct((tokens, INNER), bf16)] * 2,
         scratch_shapes=scratch,
         compiler_params=pltpu.CompilerParams(vmem_limit_bytes=VMEM_LIMIT),
-        cost_estimate=pl.CostEstimate(
-            flops=2 * 2 * PAIRS * sequences * seen * 256 * 256,
-            bytes_accessed=tokens * INNER * 10,
-            transcendentals=PAIRS * sequences * seen * 256,
-        ),
+        cost_estimate=LIGHT,
     )(*after, *args)
 
 
@@ -222,29 +219,30 @@
                 rel_ref[0, head : head + 1, :] = wide
 
 
-def attend_backward(q, q_at, k, k_at, v, v_at, q_extra, k_extra, lows, mixed, grad, g, ranges, after=()):
+def attend_backward(q, q_at, k, k_at, v, v_at, q_extra, k_extra, lows, mixed, grad, g, ranges, after=(),
+                    first=0, pairs=PAIRS, into=None):
     tokens = q.shape[0]
     sequences = tokens // SEQ
     biased = g is not None
 
     def block(at):
-        return pl.BlockSpec((SEQ, LANES), lambda p, s: (s, at + p))
+        return pl.BlockSpec((SEQ, LANES), lambda p, s: (s, at + first + p))
 
     shared = pl.BlockSpec((SEQ, LANES), lambda p, s: (s, 0))
     in_specs = [block(q_at), block(k_at), block(v_at), shared, shared, block(0), block(0), block(0)]
     args = [q, k, v, q_extra, k_extra, lows, mixed, grad]
     scratch = [pltpu.VMEM((SEQ, LANES), f32), pltpu.VMEM((SEQ, LANES), f32)]
     if biased:
-        in_specs.append(pl.BlockSpec((1, 2, SPAN), lambda p, s: (p, 0, 0)))
+        in_specs.append(pl.BlockSpec((1, 2, SPAN), lambda p, s: (first + p, 0, 0)))
         args.append(g)
         scratch += [pltpu.VMEM((SEQ, 2 * LANES), f32)] * 2
         out_specs = [
-            pl.BlockSpec((3, SEQ, LANES), lambda p, s: (0, s, p)),
+            pl.BlockSpec((3, SEQ, LANES), lambda p, s: (0, s, first + p)),
             pl.BlockSpec((1, 2, SPAN), lambda p, s: (p, 0, 0)),
         ]
         out_shape = [
             jax.ShapeDtypeStruct((3, tokens, INNER), bf16),
-            jax.ShapeDtypeStruct((PAIRS, 2, SPAN), f32),
+            jax.ShapeDtypeStruct((pairs, 2, SPAN), f32),
         ]
     else:
         out_specs = [block(0), pl.BlockSpec((2, SEQ, LANES), lambda p, s: (0, s, p))]
@@ -252,20 +250,20 @@
             jax.ShapeDtypeStruct((tokens, INNER), bf16),
             jax.ShapeDtypeStruct((2, tokens, INNER), bf16),
         ]
-    seen = sum(stop - start for start, stop in ranges)
+    aliases = {}
+    if into is not None:
+        after = [into, *after]
+        aliases = {0: 0}
     return pl.pallas_call(
         partial(attend_backward_kernel, ranges, biased, len(after)),
-        grid=(PAIRS, sequences),
+        grid=(pairs, sequences),
         in_specs=[pl.BlockSpec(memory_space=pl.ANY)] * len(after) + in_specs,
         out_specs=out_specs,
         out_shape=out_shape,
         scratch_shapes=scratch,
+        input_output_aliases=aliases,
         compiler_params=pltpu.CompilerParams(vmem_limit_bytes=VMEM_LIMIT),
-        cost_estimate=pl.CostEstimate(
-            flops=5 * 2 * PAIRS * sequences * seen * 256 * 256,
-            bytes_accessed=tokens * INNER * 20,
-            transcendentals=PAIRS * sequences * seen * 256,
-        ),
+        cost_estimate=LIGHT,
     )(*after, *args)
 
 
@@ -359,10 +357,7 @@
             jax.ShapeDtypeStruct((tokens, 3 * INNER), bf16),
         ],
         compiler_params=pltpu.CompilerParams(vmem_limit_bytes=VMEM_LIMIT),
-        cost_estimate=pl.CostEstimate(
-            flops=6 * tokens * D * D, bytes_accessed=tokens * D * 10 + D * width * 4,
-            transcendentals=0,
-        ),
+        cost_estimate=LIGHT,
     )(where, x, onehot, valid, *pieces_in)
 
 
@@ -401,10 +396,7 @@
             jax.ShapeDtypeStruct((tokens, 2 * INNER), bf16),
         ],
         compiler_params=pltpu.CompilerParams(vmem_limit_bytes=VMEM_LIMIT),
-        cost_estimate=pl.CostEstimate(
-            flops=4 * tokens * D * D, bytes_accessed=tokens * D * 6 + D * width * 4,
-            transcendentals=0,
-        ),
+        cost_estimate=LIGHT,
     )(where, *after, x, *pieces_in)
 
 
@@ -436,9 +428,7 @@
             jax.ShapeDtypeStruct((tokens, D), bf16),
         ],
         compiler_params=pltpu.CompilerParams(vmem_limit_bytes=VMEM_LIMIT),
-        cost_estimate=pl.CostEstimate(
-            flops=4 * tokens * D * D, bytes_accessed=tokens * D * 12 + D * D * 4, transcendentals=0
-        ),
+        cost_estimate=LIGHT,
     )(x, attn, w_self, gain, w_cross)
 
 
@@ -617,11 +607,7 @@
             in_type, in_type, out_type, out_type,
         ],
         compiler_params=pltpu.CompilerParams(vmem_limit_bytes=VMEM_LIMIT),
-        cost_estimate=pl.CostEstimate(
-            flops=18 * tokens * D * FF,
-            bytes_accessed=tokens * D * 16 + 12 * D * FF,
-            transcendentals=tokens * FF,
-        ),
+        cost_estimate=LIGHT,
     )(where, x1, attn, w_cross, gain, dout, own_i, own_i, core_i, core_i, *halves_i, *out_pieces)
 
 
@@ -707,11 +693,7 @@
         ),
         out_shape=out_shape,
         compiler_params=pltpu.CompilerParams(vmem_limit_bytes=VMEM_LIMIT),
-        cost_estimate=pl.CostEstimate(
-            flops=2 * tokens * D * D * at,
-            bytes_accessed=tokens * D * (len(terms) + at) * 2 + D * D * at * 2,
-            transcendentals=0,
-        ),
+        cost_estimate=LIGHT,
     )(where, *after, *[left for left, _ in terms], *[right for _, right in terms], *extra)
 
 
@@ -784,11 +766,7 @@
         out_specs=out_specs,
         out_shape=out_shape,
         compiler_params=pltpu.CompilerParams(vmem_limit_bytes=VMEM_LIMIT),
-        cost_estimate=pl.CostEstimate(
-            flops=2 * tokens * D * D * (parts + (w_next is not None)),
-            bytes_accessed=tokens * D * (2 * parts + 12) + D * D * 2 * parts,
-            transcendentals=0,
-        ),
+        cost_estimate=LIGHT,
     )(*args)
 
 
@@ -803,6 +781,13 @@
 
 def tie(value, *others):
     return lax.optimization_barrier((value, *others))[0]
+
+
+def meet(done, *moves):
+    *gots, done = lax.optimization_barrier((*[m.got for m in moves], done))
+    for move, got in zip(moves, gots):
+        move.got = got
+    return done
 
 
 class Gather:
@@ -813,18 +798,16 @@
         if after:
             half = tie(half, *after)
         self.half = half
-        self.y = exchange(half, "shard", sizes[0], 2)
-
-    def cross(self, *after):
-        if after:
-            self.y = tie(self.y, *after)
-        self.x = exchange(self.y, "rep", self.sizes[1], 1)
+        self.got = exchange(half, "shard", sizes[0], 2)
+
+    def cross(self):
+        self.y = self.got
+        self.got = exchange(self.y, "rep", self.sizes[1], 1)
         self.core = exchange(tie(self.own, self.y), "shard", self.sizes[0], 1)
         self.yc = exchange(self.y, "shard", self.sizes[0], 1)
 
-    def pieces(self, *after):
-        if after:
-            self.x = tie(self.x, *after)
+    def pieces(self):
+        self.x = self.got
         xc = exchange(self.x, "shard", self.sizes[0], 1)
         return self.own, self.core, self.y, self.x, self.yc, xc
 
@@ -854,9 +837,7 @@
             total = total + part.astype(f32)
         return total.astype(bf16)
 
-    def advance(self, *after):
-        if after:
-            self.got = tie(self.got, *after)
+    def advance(self):
         axis, bit, dim = self.steps[self.at]
         self.at += 1
         mine = (lax.axis_index(axis) // bit) % 2
@@ -872,53 +853,81 @@
         return self.got
 
 
-def spread(own, sizes, bits, dims):
-    rep = lax.axis_index("rep")
-    for bit, dim in zip(reversed(bits), reversed(dims)):
-        got = exchange(own, "rep", sizes[1], bit)
-        mine = (rep // bit) % 2
-        low = jnp.where(mine == 0, own, got)
-        high = jnp.where(mine == 0, got, own)
-        own = jnp.concatenate([low, high], axis=dim)
-    return own
-
-
-def unpack_kernel(blocks_ref, w_ref, in_ref, out_ref, sum_ref):
-    reps, _, rows, cols = blocks_ref.shape
-    out_rows = out_ref.shape[0] // reps
+class Spread:
+    def __init__(self, own, sizes, bits, dims):
+        self.own = own
+        self.reps = sizes[1]
+        self.left = list(zip(bits, dims))
+        self.got = None
+        self.advance()
+
+    def pair(self):
+        bit, _ = self.now
+        mine = (lax.axis_index("rep") // bit) % 2
+        low = jnp.where(mine == 0, self.own, self.got)
+        high = jnp.where(mine == 0, self.got, self.own)
+        return low, high
+
+    def advance(self):
+        if self.got is not None:
+            self.own = jnp.concatenate(self.pair(), axis=self.now[1])
+        self.now = self.left.pop()
+        self.got = exchange(self.own, "rep", self.reps, self.now[0])
+
+
+def together(*moves):
+    gots = lax.optimization_barrier(tuple(m.got for m in moves))
+    for move, got in zip(moves, gots):
+        move.got = got
+
+
+def unpack_kernel(where_ref, own_ref, got_ref, w_ref, in_ref, out_ref, sum_ref):
+    mine = where_ref[1]
+    half, _, rows, cols = own_ref.shape
+    out_rows = out_ref.shape[0] // (2 * half)
     total = jnp.zeros((rows, LANES), f32)
-    for rep in range(reps):
-        turned = int(format(rep, "0%db" % (reps.bit_length() - 1))[::-1], 2)
-        for part in range(2):
-            place = slice(part * FF + turned * cols, part * FF + (turned + 1) * cols)
-            block = blocks_ref[rep, part].astype(f32)
-            in_ref[:, place] = block
-            product = block * w_ref[:, place].astype(f32)
-            for lane in range(0, cols, LANES):
-                total = total + product[:, lane : lane + LANES]
-        out_place = slice(turned * out_rows, (turned + 1) * out_rows)
-        for group in range(D // cols):
-            out_ref[out_place, group * cols : (group + 1) * cols] = blocks_ref[
-                rep, 2, group * out_rows : (group + 1) * out_rows, :
-            ].astype(f32)
+    for blocks_ref, first in ((own_ref, mine * half), (got_ref, (1 - mine) * half)):
+        for block in range(half):
+            at = first + block
+            for part in range(2):
+                place = pl.ds(pl.multiple_of(part * FF + at * cols, cols), cols)
+                value = blocks_ref[block, part].astype(f32)
+                in_ref[:, place] = value
+                product = value * w_ref[:, place].astype(f32)
+                for lane in range(0, cols, LANES):
+                    total = total + product[:, lane : lane + LANES]
+            place = pl.ds(pl.multiple_of(at * out_rows, out_rows), out_rows)
+            for group in range(D // cols):
+                out_ref[place, group * cols : (group + 1) * cols] = blocks_ref[
+                    block, 2, group * out_rows : (group + 1) * out_rows, :
+                ].astype(f32)
     row = jnp.broadcast_to(jnp.sum(total, axis=1, keepdims=True), (rows, LANES)).T
     sum_ref[...] = row[0:8]
 
 
-def unpack(blocks, w):
-    reps, _, rows, cols = blocks.shape
+def unpack(where, own, got, w):
+    rows = own.shape[2]
+
+    def whole(shape):
+        return pl.BlockSpec(shape, lambda i, c: (0,) * len(shape))
+
+    outs = [
+        jax.ShapeDtypeStruct((rows, 2 * FF), f32),
+        jax.ShapeDtypeStruct((FF * rows // D, D), f32),
+        jax.ShapeDtypeStruct((8, rows), f32),
+    ]
     return pl.pallas_call(
         unpack_kernel,
-        out_shape=[
-            jax.ShapeDtypeStruct((rows, 2 * FF), f32),
-            jax.ShapeDtypeStruct((FF * rows // D, D), f32),
-            jax.ShapeDtypeStruct((8, rows), f32),
-        ],
+        grid_spec=pltpu.PrefetchScalarGridSpec(
+            num_scalar_prefetch=1,
+            grid=(1,),
+            in_specs=[whole(own.shape), whole(got.shape), whole(w.shape)],
+            out_specs=[whole(o.shape) for o in outs],
+        ),
+        out_shape=outs,
         compiler_params=pltpu.CompilerParams(vmem_limit_bytes=VMEM_LIMIT),
-        cost_estimate=pl.CostEstimate(
-            flops=4 * rows * FF, bytes_accessed=rows * FF * 16, transcendentals=0
-        ),
-    )(blocks, w)
+        cost_estimate=LIGHT,
+    )(where, own, got, w)
 
 
 def bias_rows(shards):
@@ -990,59 +999,83 @@
     w_self, gains_all, g, normed_one, qkv = first_step(
         where, hidden_in, self_pieces, placed.astype(bf16), valid
     )
-    cross_set.cross(normed_one)
-    out_set = Gather(ff_out, sizes, cross_set.y, normed_one)
-    in_set = Gather(ff_in, sizes, cross_set.y, normed_one)
+    meet(normed_one, cross_set)
+    cross_set.cross()
+    out_set = Gather(ff_out, sizes, cross_set.y)
+    in_set = Gather(ff_in, sizes, cross_set.y)
     attn_one, lows_one = attend_forward(
         qkv, 0, qkv, PAIRS, qkv, 2 * PAIRS, q_extra, self_extra, g, SELF_RANGES,
         after=[out_set.half, in_set.half],
     )
-    cross_pieces = cross_set.pieces(attn_one)
-    out_set.cross(attn_one)
-    in_set.cross(attn_one)
+    meet(attn_one, cross_set, out_set, in_set)
+    cross_pieces = cross_set.pieces()
+    out_set.cross()
+    in_set.cross()
     w_cross, ckv = encoder_step(where, enc_states, cross_pieces, [attn_one])
     first, normed_two, cq = middle_step(hidden_in, attn_one, w_self, gains_all[1:2], w_cross)
     attn_two, lows_two = attend_forward(
         cq, 0, ckv, 0, ckv, PAIRS, q_extra, cross_extra, None, CROSS_RANGES
     )
-    ff_out_pieces = out_set.pieces(attn_two)
-    ff_in_pieces = in_set.pieces(attn_two)
+    meet(attn_two, out_set, in_set)
+    ff_out_pieces = out_set.pieces()
+    ff_in_pieces = in_set.pieces()
     layer_out, grad_second, out_two, in_keep, in_send, out_keep, out_send = feed_forward(
         where, first, attn_two, w_cross, gains_all[2:3], out_grad, ff_in_pieces, ff_out_pieces
     )
     ff_in_chain = Chain(in_keep, in_send, sizes, [3], "yr")
     ff_out_chain = Chain(out_keep, out_send, sizes, [1], "ry")
     (grad_attn_two,) = norm_back(out_two, w_cross, 3, kind=bf16, after=[layer_out])
-    ff_out_chain.advance(grad_attn_two)
-    ff_in_chain.advance(grad_attn_two)
+    meet(grad_attn_two, ff_in_chain, ff_out_chain)
+    ff_out_chain.advance()
+    ff_in_chain.advance()
     grad_cq, grad_ckv = attend_backward(
         cq, 0, ckv, 0, ckv, PAIRS, q_extra, cross_extra, lows_two, attn_two, grad_attn_two,
         None, CROSS_RANGES, after=[ff_in_chain.sent, ff_out_chain.sent],
     )
-    ff_out_chain.advance(grad_cq)
+    meet(grad_cq, ff_out_chain)
+    ff_out_chain.advance()
     grad_first, _, out_one, grad_attn_one = norm_back(
         grad_cq, w_cross, 2, first, gains_all[1:2], grad_second, w_self, 3,
         after=[ff_out_chain.sent],
     )
-    ff_in_chain.advance(grad_attn_one)
-    ff_out_chain.advance(grad_attn_one)
+    meet(grad_attn_one, ff_in_chain, ff_out_chain)
+    ff_in_chain.advance()
+    ff_out_chain.advance()
     cross_keep, cross_send = weight_grad(
         where,
         [(enc_states, grad_ckv), (normed_two, grad_cq), (attn_two, out_two), (attn_one, out_one)],
         after=[ff_in_chain.sent, ff_out_chain.sent],
     )
+    cross_send = meet(cross_send, ff_in_chain, ff_out_chain)
+    ff_in_chain.advance()
+    ff_out_chain.advance()
     cross_chain = Chain(cross_keep, cross_send, sizes, [2, 1], "yr")
-    (enc_grad,) = norm_back(grad_ckv, w_cross, 0, after=[cross_keep])
-    ff_in_chain.advance(enc_grad)
-    ff_out_chain.advance(enc_grad)
-    cross_chain.advance(enc_grad)
-    grad_qkv, rel_part = attend_backward(
-        qkv, 0, qkv, PAIRS, qkv, 2 * PAIRS, q_extra, self_extra, lows_one, attn_one,
-        grad_attn_one, g, SELF_RANGES,
-        after=[cross_chain.sent, ff_out_chain.sent, ff_in_chain.sent],
-    )
-    ff_in_chain.advance(grad_qkv)
-    cross_chain.advance(grad_qkv)
+    (enc_grad,) = norm_back(
+        grad_ckv, w_cross, 0, after=[cross_keep, ff_in_chain.sent, ff_out_chain.sent]
+    )
+    meet(enc_grad, cross_chain, ff_in_chain, ff_out_chain)
+    cross_chain.advance()
+    ff_in_chain.advance()
+    out_own = ff_out_chain.own()[0]
+    backward = partial(
+        attend_backward, qkv, 0, qkv, PAIRS, qkv, 2 * PAIRS, q_extra, self_extra, lows_one,
+        attn_one, grad_attn_one, g, SELF_RANGES, pairs=PAIRS // 2,
+    )
+    some_qkv, some_rel = backward(after=[cross_chain.sent, ff_in_chain.sent, out_own])
+    some_qkv = meet(some_qkv, ff_in_chain)
+    in_own = ff_in_chain.own()[0]
+    rows, columns = in_own.shape[1:]
+    out_rows = out_own.shape[0]
+    out_own = out_own.reshape(out_rows, -1, columns).transpose(1, 0, 2).reshape(1, rows, columns)
+    bits = ff_in_chain.bits
+    blocks = Spread(
+        jnp.concatenate([in_own, out_own], axis=0)[None], sizes, bits, [0] * len(bits)
+    )
+    grad_qkv, more_rel = backward(after=[blocks.own], first=PAIRS // 2, into=some_qkv)
+    rel_part = jnp.concatenate([some_rel, more_rel], axis=0)
+    grad_qkv = meet(grad_qkv, cross_chain, blocks)
+    cross_chain.advance()
+    blocks.advance()
     table_part = jnp.einsum(
         "hu,ub->bh",
         rel_part.reshape(HEADS, SPAN),
@@ -1053,56 +1086,69 @@
     tiny = table_part.reshape(2, 2, own_buckets, HEADS).astype(bf16)
     tiny = jnp.pad(tiny, ((0, 0), (0, 0), (0, own_rows - own_buckets), (0, 2 * LANES - HEADS)))
     self_keep, self_send, last_keep, last_send = weight_grad(
-        where, [(normed_one, grad_qkv)], tiny=tiny, after=[ff_in_chain.sent, cross_chain.sent]
-    )
+        where, [(normed_one, grad_qkv)], tiny=tiny, after=[blocks.own, cross_chain.sent]
+    )
+    self_send = meet(self_send, blocks, cross_chain)
+    blocks.advance()
+    cross_chain.advance()
     self_chain = Chain(self_keep, self_send, sizes, [2, 1], "yr")
     last_chain = Chain(last_keep, last_send, sizes, [2, 1], "ry")
-    cross_chain.advance(self_keep)
-    in_own = ff_in_chain.own()[0]
-    out_own = ff_out_chain.own()[0]
-    rows, columns = in_own.shape[1:]
-    out_rows = out_own.shape[0]
-    out_own = out_own.reshape(out_rows, -1, columns).transpose(1, 0, 2).reshape(1, rows, columns)
-    blocks = lax.all_gather(
-        tie(jnp.concatenate([in_own, out_own], axis=0), self_keep), "rep", axis=0
-    )
-    self_chain.advance(self_keep)
-    last_chain.advance(self_keep)
+    self_chain.advance()
+    last_chain.advance()
     in_grad, _ = norm_back(
         grad_qkv, w_self, 0, hidden_in, gains_all[0:1], grad_first,
-        after=[self_chain.sent, last_chain.sent, cross_chain.sent],
-    )
-    self_chain.advance(in_grad)
-    last_chain.advance(in_grad)
-    cross_chain.advance(in_grad)
+        after=[self_chain.sent, last_chain.sent, cross_chain.sent, blocks.own],
+    )
+    meet(in_grad, self_chain, last_chain, cross_chain)
+    self_chain.advance()
+    last_chain.advance()
+    cross_chain.advance()
+    cross_spread = None
     while last_chain.at < len(last_chain.steps):
-        if self_chain.at < len(self_chain.steps):
-            self_chain.advance()
+        if last_chain.at == 3:
+            together(self_chain, last_chain, cross_spread or cross_chain, blocks)
+        else:
+            together(self_chain, last_chain, cross_spread or cross_chain)
+        if cross_spread is not None:
+            if cross_spread.left:
+                cross_spread.advance()
+        elif cross_chain.at < len(cross_chain.steps):
+            cross_chain.advance()
+        else:
+            cross_spread = Spread(cross_chain.own(), sizes, cross_chain.bits, cross_chain.dims)
+        self_chain.advance()
         last_chain.advance()
-    cross_grad = spread(cross_chain.own(), sizes, cross_chain.bits, cross_chain.dims)
-    self_width = self_chain.own().shape[2]
-    self_own = jnp.concatenate([self_chain.own(), last_chain.own()], axis=2)
-    self_all = spread(self_own, sizes, self_chain.bits[1:], self_chain.dims[1:])
-    other = exchange(self_all, "rep", reps, 1)
-    here = lax.axis_index("rep") % 2
-    low = jnp.where(here == 0, self_all, other)[0]
-    high = jnp.where(here == 0, other, self_all)[0]
+    together(self_chain, last_chain, cross_spread)
+    if cross_spread.left:
+        cross_spread.advance()
+    self_width = self_chain.got.shape[2]
+    self_spread = Spread(
+        jnp.concatenate([self_chain.own(), last_chain.own()], axis=2),
+        sizes, self_chain.bits, self_chain.dims,
+    )
+    while self_spread.left:
+        if cross_spread.left:
+            together(self_spread, cross_spread)
+            cross_spread.advance()
+        self_spread.advance()
+    low, high = self_spread.pair()
+    low, high = low[0], high[0]
     self_grad = jnp.concatenate(
         [low[:, :self_width], high[:, :self_width], low[:, self_width:], high[:, self_width:]],
         axis=1,
     ).astype(f32)
-    cross_grad = cross_grad[0].astype(f32)
+    cross_grad = jnp.concatenate(cross_spread.pair(), axis=2)[0].astype(f32)
 
     if reps == 8:
-        ff_in_grad, ff_out_grad, in_sums = unpack(blocks, ff_in)
+        ff_in_grad, ff_out_grad, in_sums = unpack(where, blocks.own, blocks.got, ff_in)
         in_sums = in_sums[0]
     else:
-        blocks = blocks.reshape((2,) * width + blocks.shape[1:])
-        order = list(reversed(range(width)))
-        in_grads = blocks[..., :2, :, :].transpose([width + 1, width] + order + [width + 2])
+        while blocks.left:
+            blocks.advance()
+        spread = jnp.concatenate(blocks.pair(), axis=0)
+        in_grads = spread[:, :2].transpose(2, 1, 0, 3)
         ff_in_grad = in_grads.reshape(own_rows, 2 * FF).astype(f32)
-        out_grads = blocks[..., 2, :, :].reshape((2,) * width + (-1, out_rows, columns))
-        out_grads = out_grads.transpose(order + [width + 1, width, width + 2])
+        out_grads = spread[:, 2].reshape(reps, -1, out_rows, columns).transpose(0, 2, 1, 3)
         ff_out_grad = out_grads.reshape(ff_out.shape).astype(f32)
         in_sums = jnp.sum(ff_in.astype(f32) * ff_in_grad, axis=1)
 

time: 501 us -> 453 us (0.904)
  waiting for transfers between devices: 137 us -> 94.6 us
  between operations: 15.2 us -> 2 us
    all_gather x1 -> x0, waiting for transfers between devices: 24.9 us -> none  [local(): lax.all_gather(tie(jnp.concatenate([in_own, out_own], axis=0), self_keep)...]
    ppermute x51 -> x54, waiting for transfers between devices: 112 us -> 94.6 us  [exchange(): return lax.ppermute(array, axis, [(i, i ^ bit) for i in range(size)])]
    unnamed x97 -> x121, local copies, waits for them, and re-layouts: 7.61 us -> 10.2 us
    ppermute x51 -> x54, starting transfers between devices: 47.6 us -> 50.2 us  [exchange(): return lax.ppermute(array, axis, [(i, i ^ bit) for i in range(size)])]
    pallas_call x2 -> x3, Pallas kernels: 49.8 us -> 52 us  [attend_backward(): pl.pallas_call(partial(attend_backward_kernel, ranges, biased, len(after)...]
  transfers between devices with their start and end apart: 52 -> 54, of which waited for: 20 -> 21; matrix products, arithmetic and copies ran while one was open for 11% -> 11% of each run, Pallas kernels for 29% -> 40%
where the time goes in v3:
time: 453 us; the launch traced here: 445 us
  Pallas kernels  222 us (49%)
  waiting for transfers between devices  94.6 us (21%)
  other arithmetic  55.2 us (12%)
  starting transfers between devices  50.2 us (11%)
  local copies, waits for them, and re-layouts  19.8 us (4%)
    ppermute x54, waiting for transfers between devices, exchange(): return lax.ppermute(array, axis, [(i, i ^ bit) for i in range(size)])  94.6 us
    pallas_call x3, Pallas kernels, attend_backward(): pl.pallas_call(partial(attend_backward_kernel, ranges, biased, len(after)...  52 us
    ppermute x54, starting transfers between devices, exchange(): return lax.ppermute(array, axis, [(i, i ^ bit) for i in range(size)])  50.2 us
    pallas_call x1, Pallas kernels, feed_forward(): pl.pallas_call(feed_forward_kernel, grid_spec=pltpu.PrefetchScalarGridSpe...  45.9 us
    convert_element_type x20, other arithmetic, advance(): self.sent = total.astype(bf16)  35.5 us
    pallas_call x2, Pallas kernels, attend_forward(): pl.pallas_call(partial(attend_forward_kernel, ranges, biased, len(after))...  33.7 us
    pallas_call x4, Pallas kernels, norm_back(): pl.pallas_call(partial(norm_back_kernel, x is not None, w_next is not Non...  31.3 us
    pallas_call x2, Pallas kernels, weight_grad(): pl.pallas_call(partial(weight_grad_kernel, counts, firsts, len(after)), g...  25.3 us
  transfers between devices with their start and end apart: 54, of which 21 were waited for; matrix products, arithmetic and copies ran while one was open for 11% of the time, Pallas kernels for 40%

profile of v3, /device:TPU:0, one launch (start us, length us, event | category | flops | bytes accessed | tf_op | source)
XLA Modules:
  0.0 444.6 jit_solution(474558234142340368)
XLA Ops:
  2.2 2.2 concatenate.40.refs_0_
  4.5 3.0 collective-permute-start
  7.5 14.5 %collective-permute-done.refs_2_ = bf16[192,1664]{1,0:T(8,128)(2,1)} collective-permute-done((bf16[192,1664]{1,0:T(8,128)(2,1)S(1)}, bf16[192,1664]{1,0:T(8,128)(2,1)}, u32[]{:S(2)}, u32[]{:S(2)}) %collective-permute-start) | collective-permute-done | bytes 639008 | tf_op jit(solution)/shard_map/ppermute | solution.py:774
  22.0 1.7 collective-permute-start.3
  25.5 12.4 %collective-permute-done.3.refs_3_ = bf16[192,1664]{1,0:T(8,128)(2,1)} collective-permute-done((bf16[192,1664]{1,0:T(8,128)(2,1)}, bf16[192,1664]{1,0:T(8,128)(2,1)}, u32[]{:S(2)}, u32[]{:S(2)}) %collective-permute-start.3) | collective-permute-done | bytes 639008 | tf_op jit(solution)/shard_map/ppermute | solution.py:774
  41.8 11.2 %shard_map.256 = (bf16[768,3328]{1,0:T(8,128)(2,1)}, f32[8,768]{1,0:T(8,128)}, f32[6,2,640]{2,1,0:T(2,128)}, bf16[1024,768]{1,0:T(8,128)(2,1)}, bf16[1024,2304]{1,0:T(8,128)(2,1)}) custom-call(s32[2]{0:T(128)} %pad_add_fusion.where_ref.core_ref, bf16[1024,768]{1,0:T(8,128)(2,1)} %refs_6_.1, bf16[768,640]{1,0:T(8,128)(2,1)} %constant.1626.clone.onehot_ref, ...), custom_call_target="tpu_custom_call" | custom-call | flops 1000000 | bytes 100000 | tf_op jit(solution)/shard_map/pallas_call | solution.py:337
  53.0 1.8 collective-permute-done.1.refs_4_
  56.3 1.6 collective-permute-start.7
  61.0 18.3 %shard_map.257 = (bf16[1024,768]{1,0:T(8,128)(2,1)}, bf16[1024,768]{1,0:T(8,128)(2,1)}) custom-call(bf16[512,384]{1,0:T(8,128)(2,1)} %copy-done.20, bf16[192,2048]{1,0:T(8,128)(2,1)} %copy-done.8, bf16[1024,2304]{1,0:T(8,128)(2,1)} %get-tuple-element.103.refs_2_.refs_3_.refs_4_.refs_5_, ...), custom_call_target="tpu_custom_call" | custom-call | flops 1000000 | bytes 100000 | tf_op jit(solution)/shard_map/pallas_call | solution.py:130
  79.4 3.1 collective-permute-done.8.y_o
  85.9 1.5 fusion.6
  87.4 1.6 collective-permute-done.11.refs_7_
  89.4 9.0 %shard_map.258 = (bf16[768,3072]{1,0:T(8,128)(2,1)}, bf16[1024,1536]{1,0:T(8,128)(2,1)}) custom-call(s32[2]{0:T(128)} %pad_add_fusion.where_ref.core_ref, bf16[1024,768]{1,0:T(8,128)(2,1)} %get-tuple-element.105.refs_0_.attn_ref.refs_5_.refs_9_.refs_8_, bf16[1024,768]{1,0:T(8,128)(2,1)} %refs_2_.1, bf16[192,3072]{1,0:T(8,128)(2,1)} %copy-done.5, ...), custom_call_target="tpu_custom_call" | custom-call | flops 1000000 | bytes 100000 | tf_op jit(solution)/shard_map/pallas_call | solution.py:381
  98.3 7.4 %shard_map.259 = (f32[1024,768]{1,0:T(8,128)}, bf16[1024,768]{1,0:T(8,128)(2,1)}, bf16[1024,768]{1,0:T(8,128)(2,1)}) custom-call(bf16[1024,768]{1,0:T(8,128)(2,1)} %refs_6_.1, bf16[1024,768]{1,0:T(8,128)(2,1)} %get-tuple-element.105.refs_0_.attn_ref.refs_5_.refs_9_.refs_8_, bf16[768,3328]{1,0:T(8,128)(2,1)} %get-tuple-element.106.out_w_ref.refs_6_.refs_5_, ...), custom_call_target="tpu_custom_call" | custom-call | flops 1000000 | bytes 100000 | tf_op jit(solution)/shard_map/pallas_call | solution.py:414
  105.8 15.4 %shard_map.260 = (bf16[1024,768]{1,0:T(8,128)(2,1)}, bf16[1024,768]{1,0:T(8,128)(2,1)}) custom-call(bf16[1024,768]{1,0:T(8,128)(2,1)} %get-tuple-element.112.refs_0_.refs_2_, bf16[1024,1536]{1,0:T(8,128)(2,1)} %get-tuple-element.113.refs_1_.refs_2_.refs_3_.refs_4_, bf16[1024,1536]{1,0:T(8,128)(2,1)} %get-tuple-element.113.refs_1_.refs_2_.refs_3_.refs_4_, ...), custom_call_target="tpu_custom_call" | custom-call | flops 1000000 | bytes 100000 | tf_op jit(solution)/shard_map/pallas_call | solution.py:130
  121.9 1.6 collective-permute-done.17.core_o
  123.5 1.7 collective-permute-done.19.xc_o
  127.3 45.9 %shard_map.261 = (bf16[1024,768]{1,0:T(8,128)(2,1)}, f32[1024,768]{1,0:T(8,128)}, bf16[1024,768]{1,0:T(8,128)(2,1)}, bf16[2,2,192,2048]{3,2,1,0:T(8,128)(2,1)}, ...) custom-call(s32[2]{0:T(128)} %pad_add_fusion.where_ref.core_ref, ...), custom_call_target="tpu_custom_call" | custom-call | flops 1000000 | bytes 100000 | tf_op jit(solution)/shard_map/pallas_call | solution.py:574
  173.8 5.2 %shard_map.262.refs_9_ = bf16[1024,768]{1,0:T(8,128)(2,1)} custom-call(bf16[1024,768]{1,0:T(8,128)(2,1)} %get-tuple-element.85.refs_0_, bf16[1,1024,768]{2,1,0:T(8,128)(2,1)} %bitcast.32, bf16[768,3072]{1,0:T(8,128)(2,1)} %get-tuple-element.110.q_w_ref.w2_ref.refs_2_.refs_4_), custom_call_target="tpu_custom_call" | custom-call | flops 1000000 | bytes 100000 | tf_op jit(solution)/shard_map/pallas_call | solution.py:762
  179.0 2.3 collective-permute-done.21
  181.4 1.6 copy-done.11
  183.0 2.0 add_convert_fusion.refs_0_
  185.0 1.6 collective-permute-start.22
  186.6 1.6 add_convert_fusion.3.refs_1_
  189.1 22.6 %shard_map.263 = (bf16[1024,768]{1,0:T(8,128)(2,1)}, bf16[2,1024,768]{2,1,0:T(8,128)(2,1)}) custom-call(bf16[1,2,192,2048]{3,2,1,0:T(8,128)(2,1)} %copy-done.3, bf16[2,256,768]{2,1,0:T(8,128)(2,1)} %copy-done.12, bf16[1024,768]{1,0:T(8,128)(2,1)} %get-tuple-element.112.refs_0_.refs_2_, bf16[1024,1536]{1,0:T(8,128)(2,1)} %get-tuple-element.113.refs_1_.refs_2_.refs_3_.refs_4_, ...), custom_call_target="tpu_custom_call" | custom-call | flops 1000000 | bytes 100000 | tf_op jit(solution)/shard_map/pallas_call | solution.py:257
  211.6 1.7 add_convert_fusion.8.refs_0_
  213.3 1.6 collective-permute-start.24
  214.9 9.0 %shard_map.264 = (f32[1024,768]{1,0:T(8,128)}, f32[1,768]{1,0:T(1,128)}, bf16[1024,768]{1,0:T(8,128)(2,1)}, bf16[1024,768]{1,0:T(8,128)(2,1)}) custom-call(bf16[2,128,768]{2,1,0:T(8,128)(2,1)} %copy-done.19, bf16[1,1024,768]{2,1,0:T(8,128)(2,1)} %bitcast.33, bf16[768,3072]{1,0:T(8,128)(2,1)} %get-tuple-element.110.q_w_ref.w2_ref.refs_2_.refs_4_, ...), custom_call_target="tpu_custom_call" | custom-call | flops 1000000 | bytes 100000 | tf_op jit(solution)/shard_map/pallas_call | solution.py:762
  224.4 2.6 add_convert_fusion.2.refs_0_
  229.3 2.6 collective-permute-start.26
  232.0 15.6 %shard_map.265 = (bf16[2,192,3840]{2,1,0:T(8,128)(2,1)}, bf16[2,192,3840]{2,1,0:T(8,128)(2,1)}) custom-call(s32[2]{0:T(128)} %pad_add_fusion.where_ref.core_ref, bf16[1,2,192,1024]{3,2,1,0:T(8,128)(2,1)} %copy-done.9, bf16[2,64,768]{2,1,0:T(8,128)(2,1)} %copy-done.30, bf16[1024,768]{1,0:T(8,128)(2,1)} %refs_2_.1, ...), custom_call_target="tpu_custom_call" | custom-call | flops 1000000 | bytes 100000 | tf_op jit(solution)/shard_map/pallas_call | solution.py:682
  247.7 2.1 add_convert_fusion.7.refs_1_
  249.9 1.7 collective-permute-start.28
  253.5 7.1 %shard_map.266 = f32[1024,768]{1,0:T(8,128)} custom-call(bf16[2,192,3840]{2,1,0:T(8,128)(2,1)} %get-tuple-element.143.refs_0_, bf16[1,2,192,512]{3,2,1,0:T(8,128)(2,1)} %copy-done.17, bf16[1,64,768]{2,1,0:T(8,128)(2,1)} %copy-done.43, bf16[2,1024,768]{2,1,0:T(8,128)(2,1)} %get-tuple-element.137.refs_6_.refs_3_, ...), custom_call_target="tpu_custom_call" | custom-call | flops 1000000 | bytes 100000 | tf_op jit(solution)/shard_map/pallas_call | solution.py:762
  261.4 2.8 add_convert_fusion.1.refs_0_
  264.9 1.7 add_convert_fusion.13.refs_1_
  269.4 14.7 %shard_map.267 = (bf16[3,1024,768]{2,1,0:T(8,128)(2,1)}, f32[3,2,640]{2,1,0:T(2,128)}) custom-call(bf16[1,192,3840]{2,1,0:T(8,128)(2,1)} %add_convert_fusion.1.refs_0_, bf16[1,2,192,256]{3,2,1,0:T(8,128)(2,1)} %copy-done.29, bf16[64,768]{1,0:T(8,128)(2,1)} %bitcast.34, bf16[1024,2304]{1,0:T(8,128)(2,1)} %get-tuple-element.103.refs_2_.refs_3_.refs_4_.refs_5_, ...), custom_call_target="tpu_custom_call" | custom-call | flops 1000000 | bytes 100000 | tf_op jit(solution)/shard_map/pallas_call | solution.py:257
  284.1 1.9 fusion.4
  286.7 2.2 collective-permute-start.32
  288.9 14.8 %shard_map.268 = (bf16[3,1024,768]{2,1,0:T(8,128)(2,1)}, f32[3,2,640]{2,1,0:T(2,128)}) custom-call(bf16[3,1024,768]{2,1,0:T(8,128)(2,1)} %get-tuple-element.150.refs_0_, bf16[1,3,192,256]{3,2,1,0:T(8,128)(2,1)} %copy-done.25, bf16[1024,2304]{1,0:T(8,128)(2,1)} %get-tuple-element.103.refs_2_.refs_3_.refs_4_.refs_5_, ...), custom_call_target="tpu_custom_call", output_to_operand_aliasing={{0}: (0, {})} | custom-call | flops 1000000 | bytes 100000 | tf_op jit(solution)/shard_map/pallas_call | solution.py:257
  303.7 3.2 add_convert_fusion.4.refs_1_
  309.8 1.5 collective-permute-start.33
  315.5 9.7 %shard_map.269 = (bf16[2,192,1536]{2,1,0:T(8,128)(2,1)}, bf16[2,192,1536]{2,1,0:T(8,128)(2,1)}, bf16[2,192,1024]{2,1,0:T(8,128)(2,1)}, bf16[2,192,1024]{2,1,0:T(8,128)(2,1)}) custom-call(s32[2]{0:T(128)} %pad_add_fusion.where_ref.core_ref, bf16[2,3,192,256]{3,2,1,0:T(8,128)(2,1)} %pad_maximum_fusion.2.refs_0_, ...), custom_call_target="tpu_custom_call" | custom-call | flops 1000000 | bytes 100000 | tf_op jit(solution)/shard_map/pallas_call | solution.py:682
  325.7 2.7 collective-permute-done.35
  328.4 1.5 add_convert_fusion.5.refs_0_
  331.2 1.8 add_convert_fusion.9.refs_2_
  339.2 10.0 %shard_map.270 = (f32[1024,768]{1,0:T(8,128)}, f32[1,768]{1,0:T(1,128)}) custom-call(bf16[1,192,1536]{2,1,0:T(8,128)(2,1)} %copy-done.13, bf16[2,192,512]{2,1,0:T(8,128)(2,1)} %copy-done.18, bf16[1,96,1920]{2,1,0:T(8,128)(2,1)} %copy-done.21, bf16[4,3,192,256]{3,2,1,0:T(8,128)(2,1)} %pad_maximum_fusion.refs_3_.own_ref, ...), custom_call_target="tpu_custom_call" | custom-call | flops 1000000 | bytes 100000 | tf_op jit(solution)/shard_map/pallas_call | solution.py:762
  349.3 2.2 add_convert_fusion.11
  352.8 2.1 add_convert_fusion.10
  356.1 2.1 add_convert_fusion.16
  358.9 9.4 %collective-permute-done.42 = bf16[1,48,1920]{2,1,0:T(8,128)(2,1)} collective-permute-done((bf16[1,48,1920]{2,1,0:T(8,128)(2,1)}, bf16[1,48,1920]{2,1,0:T(8,128)(2,1)}, u32[]{:S(2)}, u32[]{:S(2)}) %collective-permute-start.42) | collective-permute-done | bytes 184352 | tf_op jit(solution)/shard_map/ppermute | solution.py:774
  368.3 9.0 %collective-permute-done.40 = bf16[1,192,768]{2,1,0:T(8,128)(2,1)} collective-permute-done((bf16[1,192,768]{2,1,0:T(8,128)(2,1)}, bf16[1,192,768]{2,1,0:T(8,128)(2,1)}, u32[]{:S(2)}, u32[]{:S(2)}) %collective-permute-start.40) | collective-permute-done | bytes 294944 | tf_op jit(solution)/shard_map/ppermute | solution.py:774
  377.2 1.6 add_convert_fusion.15
  378.9 1.5 collective-permute-start.45
  383.7 2.3 collective-permute-start.44
  385.9 7.3 %collective-permute-done.44 = bf16[2,48,512]{2,1,0:T(8,128)(2,1)S(1)} collective-permute-done((bf16[2,48,512]{2,1,0:T(8,128)(2,1)S(1)}, bf16[2,48,512]{2,1,0:T(8,128)(2,1)S(1)}, u32[]{:S(2)}, u32[]{:S(2)}) %collective-permute-start.44) | collective-permute-done | bytes 98336 | tf_op jit(solution)/shard_map/ppermute | solution.py:774
  394.5 2.1 collective-permute-start.47
  398.6 3.3 collective-permute-done.48
  402.4 2.2 collective-permute-done.49
  408.2 5.6 %collective-permute-done.50 = bf16[1,48,1280]{2,1,0:T(8,128)(2,1)S(1)} collective-permute-done((bf16[1,48,1280]{2,1,0:T(8,128)(2,1)S(1)}, bf16[1,48,1280]{2,1,0:T(8,128)(2,1)S(1)}, u32[]{:S(2)}, u32[]{:S(2)}) %collective-permute-start.50) | collective-permute-done | bytes 122912 | tf_op jit(solution)/shard_map/ppermute | solution.py:774
  415.0 5.7 %shard_map.271 = (f32[192,4096]{1,0:T(8,128)}, f32[512,768]{1,0:T(8,128)}, f32[8,192]{1,0:T(8,128)}) custom-call(s32[2]{0:T(128)} %pad_add_fusion.where_ref.core_ref, bf16[4,3,192,256]{3,2,1,0:T(8,128)(2,1)} %pad_maximum_fusion.refs_3_.own_ref, bf16[4,3,192,256]{3,2,1,0:T(8,128)(2,1)} %collective-permute-done.46.got_ref, bf16[192,4096]{1,0:T(8,128)(2,1)} %w_ref.1), custom_call_target="tpu_custom_call" | custom-call | flops 1000000 | bytes 100000 | tf_op jit(solution)/shard_map/pallas_call | solution.py:919
  422.7 10.8 %collective-permute-done.53 = bf16[1,192,1920]{2,1,0:T(8,128)(2,1)S(1)} collective-permute-done((bf16[1,192,1920]{2,1,0:T(8,128)(2,1)S(1)}, bf16[1,192,1920]{2,1,0:T(8,128)(2,1)S(1)}, u32[]{:S(2)}, u32[]{:S(2)}) %collective-permute-start.53) | collective-permute-done | bytes 737312 | tf_op jit(solution)/shard_map/ppermute | solution.py:774
  436.5 3.6 collective-permute-done.52
  442.2 1.4 multiply_reduce_fusion
  (255 shorter events, 67.5 us)
Async XLA Ops:
  4.4 20.7 %copy-start.2 = (bf16[192,3328]{1,0:T(8,128)(2,1)}, bf16[192,3328]{1,0:T(8,128)(2,1)S(1)}, u32[]{:S(2)}) copy-start(bf16[192,3328]{1,0:T(8,128)(2,1)S(1)} %concatenate.40.refs_0_) | copy-start | bytes 3833860
  4.4 20.6 %copy-start.22 = (bf16[192,768]{1,0:T(8,128)(2,1)S(1)}, bf16[192,768]{1,0:T(8,128)(2,1)}, u32[]{:S(2)}) copy-start(bf16[192,768]{1,0:T(8,128)(2,1)} %param.26) | copy-start | bytes 884740
  4.4 20.6 %copy-start.51 = (bf16[192,768]{1,0:T(8,128)(2,1)S(1)}, bf16[192,768]{1,0:T(8,128)(2,1)}, u32[]{:S(2)}) copy-start(bf16[192,768]{1,0:T(8,128)(2,1)} %param.28) | copy-start | bytes 884740
  4.5 17.5 %collective-permute-start = (bf16[192,1664]{1,0:T(8,128)(2,1)S(1)}, bf16[192,1664]{1,0:T(8,128)(2,1)}, u32[]{:S(2)}, u32[]{:S(2)}) collective-permute-start(bf16[192,1664]{1,0:T(8,128)(2,1)S(1)} %constant_dynamic-slice_fusion.1), channel_id=1, source_target_pairs={{0,2},{1,3},{2,0},{3,1},{4,6},{5,7},{6,4},{7,5},{8,10},{9,11},{10,... | collective-permute-start | bytes 1916936 | tf_op jit(solution)/shard_map/ppermute | solution.py:774
  22.0 15.9 %collective-permute-start.3 = (bf16[192,1664]{1,0:T(8,128)(2,1)}, bf16[192,1664]{1,0:T(8,128)(2,1)}, u32[]{:S(2)}, u32[]{:S(2)}) collective-permute-start(bf16[192,1664]{1,0:T(8,128)(2,1)} %collective-permute-done.refs_2_), channel_id=1, source_target_pairs={{0,4},{4,0},{8,12},{12,8},{16,20},{20,16},{24,28},{28,24},{1,5},{5... | collective-permute-start | bytes 1916936 | tf_op jit(solution)/shard_map/ppermute | solution.py:774
  23.7 17.1 %copy-start = (bf16[192,4096]{1,0:T(8,128)(2,1)S(1)}, bf16[192,4096]{1,0:T(8,128)(2,1)}, u32[]{:S(2)}) copy-start(bf16[192,4096]{1,0:T(8,128)(2,1)} %w_ref.1) | copy-start | bytes 4718596
  23.7 17.2 %collective-permute-start.2 = (bf16[192,3328]{1,0:T(8,128)(2,1)S(1)}, bf16[192,3328]{1,0:T(8,128)(2,1)}, u32[]{:S(2)}, u32[]{:S(2)}) collective-permute-start(bf16[192,3328]{1,0:T(8,128)(2,1)S(1)} %concatenate.40.refs_0_), channel_id=1, source_target_pairs={{0,1},{1,0},{2,3},{3,2},{4,5},{5,4},{6,7},{7,6},{8,9},{9,8},{10,11... | collective-permute-start | bytes 3833864 | tf_op jit(solution)/shard_map/ppermute | solution.py:774
  25.1 15.9 %collective-permute-start.4 = (bf16[192,1664]{1,0:T(8,128)(2,1)}, bf16[192,1664]{1,0:T(8,128)(2,1)S(1)}, u32[]{:S(2)}, u32[]{:S(2)}) collective-permute-start(bf16[192,1664]{1,0:T(8,128)(2,1)} %collective-permute-done.refs_2_), channel_id=1, source_target_pairs={{0,1},{1,0},{2,3},{3,2},{4,5},{5,4},{6,7},{7,6},{8,9},{9,8},{10,11... | collective-permute-start | bytes 1916936 | tf_op jit(solution)/shard_map/ppermute | solution.py:774
  37.9 3.1 collective-permute-start.5
  38.8 16.1 %collective-permute-start.1 = (bf16[192,1536]{1,0:T(8,128)(2,1)}, bf16[192,1536]{1,0:T(8,128)(2,1)}, u32[]{:S(2)}, u32[]{:S(2)}) collective-permute-start(bf16[192,1536]{1,0:T(8,128)(2,1)} %constant_dynamic-slice_fusion.2), channel_id=1, source_target_pairs={{0,2},{1,3},{2,0},{3,1},{4,6},{5,7},{6,4},{7,5},{8,10},{9,11},{10,... | collective-permute-start | bytes 1769480 | tf_op jit(solution)/shard_map/ppermute | solution.py:774
  40.9 17.5 %copy-start.6 = (bf16[192,3072]{1,0:T(8,128)(2,1)S(1)}, bf16[192,3072]{1,0:T(8,128)(2,1)}, u32[]{:S(2)}) copy-start(bf16[192,3072]{1,0:T(8,128)(2,1)} %copy-done.5) | copy-start | bytes 3538948
  40.9 17.5 %copy-start.54 = (s32[1024]{0:T(1024)S(1)}, s32[1024]{0:T(1024)}, u32[]{:S(2)}) copy-start(s32[1024]{0:T(1024)} %param.19) | copy-start | bytes 12292
  40.9 17.5 %copy-start.58 = (s32[1024]{0:T(1024)S(1)}, s32[1024]{0:T(1024)}, u32[]{:S(2)}) copy-start(s32[1024]{0:T(1024)} %param.20) | copy-start | bytes 12292
  54.8 27.6 %collective-permute-start.9 = (bf16[192,2048]{1,0:T(8,128)(2,1)S(1)}, bf16[192,2048]{1,0:T(8,128)(2,1)S(1)}, u32[]{:S(2)}, u32[]{:S(2)}) collective-permute-start(bf16[192,2048]{1,0:T(8,128)(2,1)S(1)} %constant_dynamic-slice_fusion.refs_1_), channel_id=1, source_target_pairs={{0,2},{1,3},{2,0},{3,1},{4,6},{5,7},{6,4},{7,5},{8,10},{9,11},{10,... | collective-permute-start | bytes 2359304 | tf_op jit(solution)/shard_map/ppermute | solution.py:774
  56.3 26.2 %collective-permute-start.7 = (bf16[192,1536]{1,0:T(8,128)(2,1)}, bf16[192,1536]{1,0:T(8,128)(2,1)S(1)}, u32[]{:S(2)}, u32[]{:S(2)}) collective-permute-start(bf16[192,1536]{1,0:T(8,128)(2,1)} %collective-permute-done.1.refs_4_), channel_id=1, source_target_pairs={{0,4},{4,0},{8,12},{12,8},{16,20},{20,16},{24,28},{28,24},{1,5},{5... | collective-permute-start | bytes 1769480 | tf_op jit(solution)/shard_map/ppermute | solution.py:774
  57.9 24.6 %collective-permute-start.8 = (bf16[512,384]{1,0:T(8,128)(2,1)S(1)}, bf16[512,384]{1,0:T(8,128)(2,1)S(1)}, u32[]{:S(2)}, u32[]{:S(2)}) collective-permute-start(bf16[512,384]{1,0:T(8,128)(2,1)S(1)} %constant_dynamic-slice_fusion.3.refs_0_), channel_id=1, source_target_pairs={{0,2},{1,3},{2,0},{3,1},{4,6},{5,7},{6,4},{7,5},{8,10},{9,11},{10,... | collective-permute-start | bytes 1179656 | tf_op jit(solution)/shard_map/ppermute | solution.py:774
  58.4 28.9 %collective-permute-start.6 = (bf16[192,3072]{1,0:T(8,128)(2,1)S(1)}, bf16[192,3072]{1,0:T(8,128)(2,1)S(1)}, u32[]{:S(2)}, u32[]{:S(2)}) collective-permute-start(bf16[192,3072]{1,0:T(8,128)(2,1)S(1)} %copy-done.6), channel_id=1, source_target_pairs={{0,1},{1,0},{2,3},{3,2},{4,5},{5,4},{6,7},{7,6},{8,9},{9,8},{10,11... | collective-permute-start | bytes 3538952 | tf_op jit(solution)/shard_map/ppermute | solution.py:774
  59.6 25.7 %collective-permute-start.10 = (bf16[192,1536]{1,0:T(8,128)(2,1)}, bf16[192,1536]{1,0:T(8,128)(2,1)}, u32[]{:S(2)}, u32[]{:S(2)}) collective-permute-start(bf16[192,1536]{1,0:T(8,128)(2,1)} %collective-permute-done.1.refs_4_), channel_id=1, source_target_pairs={{0,1},{1,0},{2,3},{3,2},{4,5},{5,4},{6,7},{7,6},{8,9},{9,8},{10,11... | collective-permute-start | bytes 1769480 | tf_op jit(solution)/shard_map/ppermute | solution.py:774
  82.4 23.3 %copy-start.31 = (bf16[192,2048]{1,0:T(8,128)(2,1)}, bf16[192,2048]{1,0:T(8,128)(2,1)S(1)}, u32[]{:S(2)}) copy-start(bf16[192,2048]{1,0:T(8,128)(2,1)S(1)} %collective-permute-done.9.y_in) | copy-start | bytes 2359300
  83.4 38.0 %collective-permute-start.14 = (bf16[192,2048]{1,0:T(8,128)(2,1)S(1)}, bf16[192,2048]{1,0:T(8,128)(2,1)S(1)}, u32[]{:S(2)}, u32[]{:S(2)}) collective-permute-start(bf16[192,2048]{1,0:T(8,128)(2,1)S(1)} %collective-permute-done.9.y_in), channel_id=1, source_target_pairs={{0,4},{4,0},{8,12},{12,8},{16,20},{20,16},{24,28},{28,24},{1,5},{5... | collective-permute-start | bytes 2359304 | tf_op jit(solution)/shard_map/ppermute | solution.py:774
  84.8 40.4 %collective-permute-start.12 = (bf16[192,4096]{1,0:T(8,128)(2,1)S(1)}, bf16[192,4096]{1,0:T(8,128)(2,1)S(1)}, u32[]{:S(2)}, u32[]{:S(2)}) collective-permute-start(bf16[192,4096]{1,0:T(8,128)(2,1)S(1)} %copy-done), channel_id=1, source_target_pairs={{0,1},{1,0},{2,3},{3,2},{4,5},{5,4},{6,7},{7,6},{8,9},{9,8},{10,11... | collective-permute-start | bytes 4718600 | tf_op jit(solution)/shard_map/ppermute | solution.py:774
  84.8 4.2 collective-permute-start.11
  85.3 35.9 %collective-permute-start.13 = (bf16[512,384]{1,0:T(8,128)(2,1)}, bf16[512,384]{1,0:T(8,128)(2,1)S(1)}, u32[]{:S(2)}, u32[]{:S(2)}) collective-permute-start(bf16[512,384]{1,0:T(8,128)(2,1)} %copy-done.46), channel_id=1, source_target_pairs={{0,4},{4,0},{8,12},{12,8},{16,20},{20,16},{24,28},{28,24},{1,5},{5... | collective-permute-start | bytes 1179656 | tf_op jit(solution)/shard_map/ppermute | solution.py:774
  87.4 36.1 %collective-permute-start.15 = (bf16[192,2048]{1,0:T(8,128)(2,1)S(1)}, bf16[192,2048]{1,0:T(8,128)(2,1)S(1)}, u32[]{:S(2)}, u32[]{:S(2)}) collective-permute-start(bf16[192,2048]{1,0:T(8,128)(2,1)S(1)} %collective-permute-done.9.y_in), channel_id=1, source_target_pairs={{0,1},{1,0},{2,3},{3,2},{4,5},{5,4},{6,7},{7,6},{8,9},{9,8},{10,11... | collective-permute-start | bytes 2359304 | tf_op jit(solution)/shard_map/ppermute | solution.py:774
  89.0 32.8 %collective-permute-start.18 = (bf16[512,384]{1,0:T(8,128)(2,1)}, bf16[512,384]{1,0:T(8,128)(2,1)S(1)}, u32[]{:S(2)}, u32[]{:S(2)}) collective-permute-start(bf16[512,384]{1,0:T(8,128)(2,1)} %copy-done.46), channel_id=1, source_target_pairs={{0,1},{1,0},{2,3},{3,2},{4,5},{5,4},{6,7},{7,6},{8,9},{9,8},{10,11... | collective-permute-start | bytes 1179656 | tf_op jit(solution)/shard_map/ppermute | solution.py:774
  121.2 2.4 collective-permute-start.17
  121.4 3.8 collective-permute-start.16
  121.7 3.5 collective-permute-start.19
  173.2 8.2 %collective-permute-start.20 = (bf16[2,2,192,2048]{3,2,1,0:T(8,128)(2,1)}, bf16[2,2,192,2048]{3,2,1,0:T(8,128)(2,1)S(1)}, u32[]{:S(2)}, u32[]{:S(2)}) collective-permute-start(bf16[2,2,192,2048]{3,2,1,0:T(8,128)(2,1)} %get-tuple-element.123), channel_id=1, source_target_pairs={{0,1},{1,0},{2,3},{3,2},{4,5},{5,4},{6,7},{7,6},{8,9},{9,8},{10,11... | collective-permute-start | bytes 9437192 | tf_op jit(solution)/shard_map/ppermute | solution.py:774
  173.4 7.9 %collective-permute-start.21 = (bf16[2,512,768]{2,1,0:T(8,128)(2,1)}, bf16[2,512,768]{2,1,0:T(8,128)(2,1)}, u32[]{:S(2)}, u32[]{:S(2)}) collective-permute-start(bf16[2,512,768]{2,1,0:T(8,128)(2,1)} %get-tuple-element.124), channel_id=1, source_target_pairs={{0,1},{1,0},{2,3},{3,2},{4,5},{5,4},{6,7},{7,6},{8,9},{9,8},{10,11... | collective-permute-start | bytes 4718600 | tf_op jit(solution)/shard_map/ppermute | solution.py:774
  185.0 39.3 %collective-permute-start.22 = (bf16[1,2,192,2048]{3,2,1,0:T(8,128)(2,1)S(1)}, bf16[1,2,192,2048]{3,2,1,0:T(8,128)(2,1)}, u32[]{:S(2)}, u32[]{:S(2)}) collective-permute-start(bf16[1,2,192,2048]{3,2,1,0:T(8,128)(2,1)S(1)} %add_convert_fusion.refs_0_), channel_id=1, source_target_pairs={{0,2},{1,3},{2,0},{3,1},{4,6},{5,7},{6,4},{7,5},{8,10},{9,11},{10,... | collective-permute-start | bytes 4718600 | tf_op jit(solution)/shard_map/ppermute | solution.py:774
  188.2 23.4 %collective-permute-start.23 = (bf16[2,256,768]{2,1,0:T(8,128)(2,1)S(1)}, bf16[2,256,768]{2,1,0:T(8,128)(2,1)S(1)}, u32[]{:S(2)}, u32[]{:S(2)}) collective-permute-start(bf16[2,256,768]{2,1,0:T(8,128)(2,1)S(1)} %add_convert_fusion.3.refs_1_), channel_id=1, source_target_pairs={{0,4},{4,0},{8,12},{12,8},{16,20},{20,16},{24,28},{28,24},{1,5},{5... | collective-permute-start | bytes 2359304 | tf_op jit(solution)/shard_map/ppermute | solution.py:774
  213.3 11.1 %collective-permute-start.24 = (bf16[2,128,768]{2,1,0:T(8,128)(2,1)S(1)}, bf16[2,128,768]{2,1,0:T(8,128)(2,1)S(1)}, u32[]{:S(2)}, u32[]{:S(2)}) collective-permute-start(bf16[2,128,768]{2,1,0:T(8,128)(2,1)S(1)} %add_convert_fusion.8.refs_0_), channel_id=1, source_target_pairs={{0,8},{4,12},{8,0},{12,4},{16,24},{20,28},{24,16},{28,20},{1,9},{5... | collective-permute-start | bytes 1179656 | tf_op jit(solution)/shard_map/ppermute | solution.py:774
  224.4 27.2 %copy-start.44 = (bf16[2,128,768]{2,1,0:T(8,128)(2,1)}, bf16[2,128,768]{2,1,0:T(8,128)(2,1)S(1)}, u32[]{:S(2)}) copy-start(bf16[2,128,768]{2,1,0:T(8,128)(2,1)S(1)} %collective-permute-done.24) | copy-start | bytes 1179652
  227.0 20.6 %collective-permute-start.25 = (bf16[1,2,192,1024]{3,2,1,0:T(8,128)(2,1)S(1)}, bf16[1,2,192,1024]{3,2,1,0:T(8,128)(2,1)S(1)}, u32[]{:S(2)}, u32[]{:S(2)}) collective-permute-start(bf16[1,2,192,1024]{3,2,1,0:T(8,128)(2,1)S(1)} %add_convert_fusion.2.refs_0_), channel_id=1, source_target_pairs={{0,4},{4,0},{8,12},{12,8},{16,20},{20,16},{24,28},{28,24},{1,5},{5... | collective-permute-start | bytes 2359304 | tf_op jit(solution)/shard_map/ppermute | solution.py:774
  229.3 18.3 %collective-permute-start.26 = (bf16[2,64,768]{2,1,0:T(8,128)(2,1)S(1)}, bf16[2,64,768]{2,1,0:T(8,128)(2,1)S(1)}, u32[]{:S(2)}, u32[]{:S(2)}) collective-permute-start(bf16[2,64,768]{2,1,0:T(8,128)(2,1)S(1)} %add_convert_fusion.14.refs_1_), channel_id=1, source_target_pairs={{0,16},{4,20},{8,24},{12,28},{16,0},{20,4},{24,8},{28,12},{1,17},{... | collective-permute-start | bytes 589832 | tf_op jit(solution)/shard_map/ppermute | solution.py:774
  247.6 13.7 %collective-permute-start.27 = (bf16[2,192,3840]{2,1,0:T(8,128)(2,1)}, bf16[2,192,3840]{2,1,0:T(8,128)(2,1)}, u32[]{:S(2)}, u32[]{:S(2)}) collective-permute-start(bf16[2,192,3840]{2,1,0:T(8,128)(2,1)} %get-tuple-element.141), channel_id=1, source_target_pairs={{0,1},{1,0},{2,3},{3,2},{4,5},{5,4},{6,7},{7,6},{8,9},{9,8},{10,11... | collective-permute-start | bytes 8847368 | tf_op jit(solution)/shard_map/ppermute | solution.py:774
  249.9 11.5 %collective-permute-start.28 = (bf16[1,2,192,512]{3,2,1,0:T(8,128)(2,1)S(1)}, bf16[1,2,192,512]{3,2,1,0:T(8,128)(2,1)}, u32[]{:S(2)}, u32[]{:S(2)}) collective-permute-start(bf16[1,2,192,512]{3,2,1,0:T(8,128)(2,1)S(1)} %add_convert_fusion.7.refs_1_), channel_id=1, source_target_pairs={{0,8},{4,12},{8,0},{12,4},{16,24},{20,28},{24,16},{28,20},{1,9},{5... | collective-permute-start | bytes 1179656 | tf_op jit(solution)/shard_map/ppermute | solution.py:774
  252.7 7.9 %collective-permute-start.29 = (bf16[1,64,768]{2,1,0:T(8,128)(2,1)S(1)}, bf16[1,64,768]{2,1,0:T(8,128)(2,1)S(1)}, u32[]{:S(2)}, u32[]{:S(2)}) collective-permute-start(bf16[1,64,768]{2,1,0:T(8,128)(2,1)S(1)} %add_convert_fusion.20.refs_2_), channel_id=1, source_target_pairs={{0,2},{1,3},{2,0},{3,1},{4,6},{5,7},{6,4},{7,5},{8,10},{9,11},{10,... | collective-permute-start | bytes 294920 | tf_op jit(solution)/shard_map/ppermute | solution.py:774
  264.2 39.5 %collective-permute-start.31 = (bf16[1,192,3840]{2,1,0:T(8,128)(2,1)}, bf16[1,192,3840]{2,1,0:T(8,128)(2,1)}, u32[]{:S(2)}, u32[]{:S(2)}) collective-permute-start(bf16[1,192,3840]{2,1,0:T(8,128)(2,1)} %add_convert_fusion.1.refs_0_), channel_id=1, source_target_pairs={{0,2},{1,3},{2,0},{3,1},{4,6},{5,7},{6,4},{7,5},{8,10},{9,11},{10,... | collective-permute-start | bytes 4423688 | tf_op jit(solution)/shard_map/ppermute | solution.py:774
  266.7 17.4 %collective-permute-start.30 = (bf16[1,2,192,256]{3,2,1,0:T(8,128)(2,1)S(1)}, bf16[1,2,192,256]{3,2,1,0:T(8,128)(2,1)}, u32[]{:S(2)}, u32[]{:S(2)}) collective-permute-start(bf16[1,2,192,256]{3,2,1,0:T(8,128)(2,1)S(1)} %add_convert_fusion.13.refs_1_), channel_id=1, source_target_pairs={{0,16},{4,20},{8,24},{12,28},{16,0},{20,4},{24,8},{28,12},{1,17},{... | collective-permute-start | bytes 589832 | tf_op jit(solution)/shard_map/ppermute | solution.py:774
  286.7 17.0 %collective-permute-start.32 = (bf16[1,3,192,256]{3,2,1,0:T(8,128)(2,1)S(1)}, bf16[1,3,192,256]{3,2,1,0:T(8,128)(2,1)S(1)}, u32[]{:S(2)}, u32[]{:S(2)}) collective-permute-start(bf16[1,3,192,256]{3,2,1,0:T(8,128)(2,1)S(1)} %maximum_bitcast_fusion.1.refs_1_), channel_id=1, source_target_pairs={{0,16},{4,20},{8,24},{12,28},{16,0},{20,4},{24,8},{28,12},{1,17},{... | collective-permute-start | bytes 884744 | tf_op jit(solution)/shard_map/ppermute | solution.py:774
  306.9 18.3 %collective-permute-start.34 = (bf16[1,192,1920]{2,1,0:T(8,128)(2,1)}, bf16[1,192,1920]{2,1,0:T(8,128)(2,1)}, u32[]{:S(2)}, u32[]{:S(2)}) collective-permute-start(bf16[1,192,1920]{2,1,0:T(8,128)(2,1)} %add_convert_fusion.4.refs_1_), channel_id=1, source_target_pairs={{0,4},{4,0},{8,12},{12,8},{16,20},{20,16},{24,28},{28,24},{1,5},{5... | collective-permute-start | bytes 2211848 | tf_op jit(solution)/shard_map/ppermute | solution.py:774
  309.8 15.4 %collective-permute-start.33 = (bf16[2,3,192,256]{3,2,1,0:T(8,128)(2,1)}, bf16[2,3,192,256]{3,2,1,0:T(8,128)(2,1)}, u32[]{:S(2)}, u32[]{:S(2)}) collective-permute-start(bf16[2,3,192,256]{3,2,1,0:T(8,128)(2,1)} %pad_maximum_fusion.2.refs_0_), channel_id=1, source_target_pairs={{0,8},{4,12},{8,0},{12,4},{16,24},{20,28},{24,16},{28,20},{1,9},{5... | collective-permute-start | bytes 1769480 | tf_op jit(solution)/shard_map/ppermute | solution.py:774
  325.2 3.3 collective-permute-start.35
  325.2 8.5 %collective-permute-start.36 = (bf16[2,192,1024]{2,1,0:T(8,128)(2,1)}, bf16[2,192,1024]{2,1,0:T(8,128)(2,1)}, u32[]{:S(2)}, u32[]{:S(2)}) collective-permute-start(bf16[2,192,1024]{2,1,0:T(8,128)(2,1)} %get-tuple-element.161), channel_id=1, source_target_pairs={{0,1},{1,0},{2,3},{3,2},{4,5},{5,4},{6,7},{7,6},{8,9},{9,8},{10,11... | collective-permute-start | bytes 2359304 | tf_op jit(solution)/shard_map/ppermute | solution.py:774
  329.9 19.4 %collective-permute-start.37 = (bf16[1,192,1536]{2,1,0:T(8,128)(2,1)S(1)}, bf16[1,192,1536]{2,1,0:T(8,128)(2,1)S(1)}, u32[]{:S(2)}, u32[]{:S(2)}) collective-permute-start(bf16[1,192,1536]{2,1,0:T(8,128)(2,1)S(1)} %add_convert_fusion.5.refs_0_), channel_id=1, source_target_pairs={{0,2},{1,3},{2,0},{3,1},{4,6},{5,7},{6,4},{7,5},{8,10},{9,11},{10,... | collective-permute-start | bytes 1769480 | tf_op jit(solution)/shard_map/ppermute | solution.py:774
  333.0 16.3 %collective-permute-start.39 = (bf16[1,96,1920]{2,1,0:T(8,128)(2,1)S(1)}, bf16[1,96,1920]{2,1,0:T(8,128)(2,1)S(1)}, u32[]{:S(2)}, u32[]{:S(2)}) collective-permute-start(bf16[1,96,1920]{2,1,0:T(8,128)(2,1)S(1)} %add_convert_fusion.9.refs_2_), channel_id=1, source_target_pairs={{0,8},{4,12},{8,0},{12,4},{16,24},{20,28},{24,16},{28,20},{1,9},{5... | collective-permute-start | bytes 1105928 | tf_op jit(solution)/shard_map/ppermute | solution.py:774
  334.9 14.4 %collective-permute-start.38 = (bf16[2,192,512]{2,1,0:T(8,128)(2,1)S(1)}, bf16[2,192,512]{2,1,0:T(8,128)(2,1)S(1)}, u32[]{:S(2)}, u32[]{:S(2)}) collective-permute-start(bf16[2,192,512]{2,1,0:T(8,128)(2,1)S(1)} %add_convert_fusion.6.refs_1_), channel_id=1, source_target_pairs={{0,4},{4,0},{8,12},{12,8},{16,20},{20,16},{24,28},{28,24},{1,5},{5... | collective-permute-start | bytes 1179656 | tf_op jit(solution)/shard_map/ppermute | solution.py:774
  338.2 47.7 %collective-permute-start.46 = (bf16[4,3,192,256]{3,2,1,0:T(8,128)(2,1)}, bf16[4,3,192,256]{3,2,1,0:T(8,128)(2,1)}, u32[]{:S(2)}, u32[]{:S(2)}) collective-permute-start(bf16[4,3,192,256]{3,2,1,0:T(8,128)(2,1)} %pad_maximum_fusion.refs_3_.own_ref), channel_id=1, source_target_pairs={{0,4},{4,0},{8,12},{12,8},{16,20},{20,16},{24,28},{28,24},{1,5},{5... | collective-permute-start | bytes 3538952 | tf_op jit(solution)/shard_map/ppermute | solution.py:774
  351.5 16.7 %collective-permute-start.41 = (bf16[2,96,512]{2,1,0:T(8,128)(2,1)}, bf16[2,96,512]{2,1,0:T(8,128)(2,1)}, u32[]{:S(2)}, u32[]{:S(2)}) collective-permute-start(bf16[2,96,512]{2,1,0:T(8,128)(2,1)} %add_convert_fusion.11), channel_id=1, source_target_pairs={{0,8},{4,12},{8,0},{12,4},{16,24},{20,28},{24,16},{28,20},{1,9},{5... | collective-permute-start | bytes 589832 | tf_op jit(solution)/shard_map/ppermute | solution.py:774
  354.9 25.5 %copy-start.41 = (bf16[1,192,1536]{2,1,0:T(8,128)(2,1)S(1)}, bf16[1,192,1536]{2,1,0:T(8,128)(2,1)}, u32[]{:S(2)}) copy-start(bf16[1,192,1536]{2,1,0:T(8,128)(2,1)} %copy-done.40) | copy-start | bytes 1769476
  354.9 22.4 %collective-permute-start.40 = (bf16[1,192,768]{2,1,0:T(8,128)(2,1)}, bf16[1,192,768]{2,1,0:T(8,128)(2,1)}, u32[]{:S(2)}, u32[]{:S(2)}) collective-permute-start(bf16[1,192,768]{2,1,0:T(8,128)(2,1)} %add_convert_fusion.10), channel_id=1, source_target_pairs={{0,4},{4,0},{8,12},{12,8},{16,20},{20,16},{24,28},{28,24},{1,5},{5... | collective-permute-start | bytes 884744 | tf_op jit(solution)/shard_map/ppermute | solution.py:774
  358.3 10.0 %collective-permute-start.42 = (bf16[1,48,1920]{2,1,0:T(8,128)(2,1)}, bf16[1,48,1920]{2,1,0:T(8,128)(2,1)}, u32[]{:S(2)}, u32[]{:S(2)}) collective-permute-start(bf16[1,48,1920]{2,1,0:T(8,128)(2,1)} %add_convert_fusion.16), channel_id=1, source_target_pairs={{0,16},{4,20},{8,24},{12,28},{16,0},{20,4},{24,8},{28,12},{1,17},{... | collective-permute-start | bytes 552968 | tf_op jit(solution)/shard_map/ppermute | solution.py:774
  378.9 14.3 %collective-permute-start.45 = (bf16[1,48,1920]{2,1,0:T(8,128)(2,1)S(1)}, bf16[1,48,1920]{2,1,0:T(8,128)(2,1)S(1)}, u32[]{:S(2)}, u32[]{:S(2)}) collective-permute-start(bf16[1,48,1920]{2,1,0:T(8,128)(2,1)S(1)} %add_convert_fusion.15), channel_id=1, source_target_pairs={{0,16},{4,20},{8,24},{12,28},{16,0},{20,4},{24,8},{28,12},{1,17},{... | collective-permute-start | bytes 552968 | tf_op jit(solution)/shard_map/ppermute | solution.py:774
  381.7 11.5 %collective-permute-start.43 = (bf16[1,96,768]{2,1,0:T(8,128)(2,1)S(1)}, bf16[1,96,768]{2,1,0:T(8,128)(2,1)S(1)}, u32[]{:S(2)}, u32[]{:S(2)}) collective-permute-start(bf16[1,96,768]{2,1,0:T(8,128)(2,1)S(1)} %add_convert_fusion.17), channel_id=1, source_target_pairs={{0,8},{4,12},{8,0},{12,4},{16,24},{20,28},{24,16},{28,20},{1,9},{5... | collective-permute-start | bytes 442376 | tf_op jit(solution)/shard_map/ppermute | solution.py:774
  383.7 9.5 %collective-permute-start.44 = (bf16[2,48,512]{2,1,0:T(8,128)(2,1)S(1)}, bf16[2,48,512]{2,1,0:T(8,128)(2,1)S(1)}, u32[]{:S(2)}, u32[]{:S(2)}) collective-permute-start(bf16[2,48,512]{2,1,0:T(8,128)(2,1)S(1)} %add_convert_fusion.18), channel_id=1, source_target_pairs={{0,16},{4,20},{8,24},{12,28},{16,0},{20,4},{24,8},{28,12},{1,17},{... | collective-permute-start | bytes 294920 | tf_op jit(solution)/shard_map/ppermute | solution.py:774
  393.3 11.3 %collective-permute-start.49 = (bf16[1,96,1920]{2,1,0:T(8,128)(2,1)S(1)}, bf16[1,96,1920]{2,1,0:T(8,128)(2,1)S(1)}, u32[]{:S(2)}, u32[]{:S(2)}) collective-permute-start(bf16[1,96,1920]{2,1,0:T(8,128)(2,1)S(1)} %pad_maximum_fusion.4), channel_id=1, source_target_pairs={{0,8},{4,12},{8,0},{12,4},{16,24},{20,28},{24,16},{28,20},{1,9},{5... | collective-permute-start | bytes 1105928 | tf_op jit(solution)/shard_map/ppermute | solution.py:774
  394.5 7.9 %collective-permute-start.47 = (bf16[1,48,768]{2,1,0:T(8,128)(2,1)S(1)}, bf16[1,48,768]{2,1,0:T(8,128)(2,1)S(1)}, u32[]{:S(2)}, u32[]{:S(2)}) collective-permute-start(bf16[1,48,768]{2,1,0:T(8,128)(2,1)S(1)} %add_convert_fusion.22), channel_id=1, source_target_pairs={{0,16},{4,20},{8,24},{12,28},{16,0},{20,4},{24,8},{28,12},{1,17},{... | collective-permute-start | bytes 221192 | tf_op jit(solution)/shard_map/ppermute | solution.py:774
  397.8 4.2 collective-permute-start.48
  406.9 7.0 %collective-permute-start.50 = (bf16[1,48,1280]{2,1,0:T(8,128)(2,1)S(1)}, bf16[1,48,1280]{2,1,0:T(8,128)(2,1)S(1)}, u32[]{:S(2)}, u32[]{:S(2)}) collective-permute-start(bf16[1,48,1280]{2,1,0:T(8,128)(2,1)S(1)} %pad_maximum_fusion.6), channel_id=1, source_target_pairs={{0,16},{4,20},{8,24},{12,28},{16,0},{20,4},{24,8},{28,12},{1,17},{... | collective-permute-start | bytes 368648 | tf_op jit(solution)/shard_map/ppermute | solution.py:774
  413.9 7.5 %collective-permute-start.51 = (bf16[1,96,1280]{2,1,0:T(8,128)(2,1)S(1)}, bf16[1,96,1280]{2,1,0:T(8,128)(2,1)S(1)}, u32[]{:S(2)}, u32[]{:S(2)}) collective-permute-start(bf16[1,96,1280]{2,1,0:T(8,128)(2,1)S(1)} %pad_maximum_fusion.5), channel_id=1, source_target_pairs={{0,8},{4,12},{8,0},{12,4},{16,24},{20,28},{24,16},{28,20},{1,9},{5... | collective-permute-start | bytes 737288 | tf_op jit(solution)/shard_map/ppermute | solution.py:774
  414.1 19.5 %collective-permute-start.53 = (bf16[1,192,1920]{2,1,0:T(8,128)(2,1)S(1)}, bf16[1,192,1920]{2,1,0:T(8,128)(2,1)S(1)}, u32[]{:S(2)}, u32[]{:S(2)}) collective-permute-start(bf16[1,192,1920]{2,1,0:T(8,128)(2,1)S(1)} %pad_maximum_fusion.1), channel_id=1, source_target_pairs={{0,4},{4,0},{8,12},{12,8},{16,20},{20,16},{24,28},{28,24},{1,5},{5... | collective-permute-start | bytes 2211848 | tf_op jit(solution)/shard_map/ppermute | solution.py:774
  421.5 18.6 %collective-permute-start.52 = (bf16[1,192,1280]{2,1,0:T(8,128)(2,1)S(1)}, bf16[1,192,1280]{2,1,0:T(8,128)(2,1)S(1)}, u32[]{:S(2)}, u32[]{:S(2)}) collective-permute-start(bf16[1,192,1280]{2,1,0:T(8,128)(2,1)S(1)} %pad_maximum_fusion.3), channel_id=1, source_target_pairs={{0,4},{4,0},{8,12},{12,8},{16,20},{20,16},{24,28},{28,24},{1,5},{5... | collective-permute-start | bytes 1474568 | tf_op jit(solution)/shard_map/ppermute | solution.py:774
  (49 other events, 220.0 us)

commit v4 on v3

--- a/solution.py
+++ b/solution.py
@@ -316,7 +316,7 @@
     @pl.when(pl.program_id(0) == 0)
     def _():
         place_pieces(where_ref, full, *pieces_in)
-        small = full[:, 4 * INNER : 4 * INNER + LANES].astype(f32).T
+        small = full[:, 3 * INNER : 3 * INNER + LANES].astype(f32).T
         gains_ref[...] = small[0:8]
         table = small[16:32].astype(bf16)
         bias = jnp.where(valid_ref[...] > 0, dot_nn(table, onehot_ref[...]), masked_score)
@@ -408,7 +408,7 @@
     cq_ref[...] = dot_nn(normed, q_w_ref[...]).astype(bf16)
 
 
-def middle_step(x, attn, w_self, gain, w_cross):
+def middle_step(x, attn, gain, w_cross):
     tokens = x.shape[0]
     block = pl.BlockSpec((ROWS, D), lambda i: (i, 0))
     return pl.pallas_call(
@@ -417,7 +417,7 @@
         in_specs=[
             block,
             block,
-            pl.BlockSpec((D, D), lambda i: (0, 3)),
+            pl.BlockSpec((D, D), lambda i: (0, 4)),
             pl.BlockSpec((1, D), lambda i: (0, 0)),
             pl.BlockSpec((D, D), lambda i: (0, 2)),
         ],
@@ -429,13 +429,13 @@
         ],
         compiler_params=pltpu.CompilerParams(vmem_limit_bytes=VMEM_LIMIT),
         cost_estimate=LIGHT,
-    )(x, attn, w_self, gain, w_cross)
-
-
-def shares(core, value, keep_ref, send_ref, *at):
+    )(x, attn, w_cross, gain, w_cross)
+
+
+def shares(core, value, keep_ref, send_ref, *at, start=0):
     rows, cols = value.shape
     parts = value.astype(bf16).reshape(2, 2, rows // 4, cols)
-    columns = slice(0, cols)
+    columns = slice(start, start + cols)
     for y in range(2):
         place = (y,) + at + (slice(None), columns)
         keep_ref[place] = jnp.where(core == 0, parts[y, 0], parts[y, 1])
@@ -523,8 +523,10 @@
         acc[rows, :] += dot_nn(hid[rows, :], wo[...])
         dn[rows, :] += dot_nt(dgate[rows, :], wg[...]) + dot_nt(dup[rows, :], wu[...])
     core = shard % 2
-    shares(core, dot_nn(n3t[...], dgate[...]), gk_ref, gs_ref, 0)
-    shares(core, dot_nn(n3t[...], dup[...]), gk_ref, gs_ref, 1)
+    for part, grads in enumerate((dgate, dup)):
+        for start in range(0, FF_BLOCK, ROWS):
+            value = dot_nn(n3t[...], grads[:, start : start + ROWS])
+            shares(core, value, gk_ref, gs_ref, part, start=start)
     out_grad = dot_tn(hid[...], dout_ref[...]).astype(bf16)
 
     @pl.when(step % 2 == 0)
@@ -630,25 +632,25 @@
         def _():
             left_t[...] = left[...].T
 
-        @pl.when((step >= at) & (step < at + count))
+        def product(keep, send):
+            for start in range(0, D, ROWS):
+                columns = slice(start, start + ROWS)
+                block = right[:, columns] if len(right.shape) == 2 else right[0, :, columns]
+                shares(core, dot_nn(left_t[...], block), keep, send, start=start)
+
+        @pl.when((step >= at) & (step < (firsts if second else at + count)))
         def _():
-            block = right[...] if len(right.shape) == 2 else right[0]
-            value = dot_nn(left_t[...], block)
-            if not second:
-                shares(core, value, keep_ref, send_ref)
-            else:
-
-                @pl.when(step < firsts)
-                def _():
-                    shares(core, value, keep_ref, send_ref)
-
-                @pl.when(step >= firsts)
-                def _():
-                    shares(core, value, keep2_ref, send2_ref)
-                    tiny = tiny_ref[...]
-                    for y in range(2):
-                        keep2_ref[y, :, D:] = jnp.where(core == 0, tiny[y, 0], tiny[y, 1])
-                        send2_ref[y, :, D:] = jnp.where(core == 0, tiny[y, 1], tiny[y, 0])
+            product(keep_ref, send_ref)
+
+        if second:
+
+            @pl.when(step >= firsts)
+            def _():
+                product(keep2_ref, send2_ref)
+                tiny = tiny_ref[...]
+                for y in range(2):
+                    keep2_ref[y, :, D:] = jnp.where(core == 0, tiny[y, 0], tiny[y, 1])
+                    send2_ref[y, :, D:] = jnp.where(core == 0, tiny[y, 1], tiny[y, 0])
 
         at += count
 
@@ -813,10 +815,13 @@
 
 
 class Chain:
-    def __init__(self, keep, send, sizes, dims, order):
+    def __init__(self, keep, send, sizes, dims, order, turned=False):
         self.shards, self.reps = sizes
         self.bits = [1 << b for b in range(self.reps.bit_length() - 1)]
         self.dims = [dims[min(i, len(dims) - 1)] for i in range(len(self.bits))]
+        if turned:
+            self.bits[:2] = self.bits[1::-1]
+            self.dims[:2] = self.dims[1::-1]
         steps = []
         for name in order:
             if name == "y":
@@ -824,7 +829,7 @@
             else:
                 steps += [("rep", bit, dim) for bit, dim in zip(self.bits, self.dims)]
         self.steps = steps
-        self.kept = [keep]
+        self.kept = keep
         self.got = exchange(send, "shard", self.shards, 1)
         self.sent = send
         self.at = 0
@@ -832,23 +837,19 @@
     def own(self):
         while self.at < len(self.steps):
             self.advance()
-        total = self.got.astype(f32)
-        for part in self.kept:
-            total = total + part.astype(f32)
-        return total.astype(bf16)
+        return (self.kept.astype(f32) + self.got.astype(f32)).astype(bf16)
 
     def advance(self):
         axis, bit, dim = self.steps[self.at]
         self.at += 1
         mine = (lax.axis_index(axis) // bit) % 2
         size = self.shards if axis == "shard" else self.reps
-        parts = self.kept + [self.got]
-        total = None
-        for part in parts:
-            term = part_of(part, dim, 1 - mine).astype(f32)
-            total = term if total is None else total + term
-        self.sent = total.astype(bf16)
-        self.kept = [part_of(part, dim, mine) for part in parts]
+        def half(index):
+            kept, got = (part_of(part, dim, index).astype(f32) for part in (self.kept, self.got))
+            return lax.optimization_barrier((kept + got).astype(bf16))
+
+        self.sent = half(1 - mine)
+        self.kept = half(mine)
         self.got = exchange(self.sent, axis, size, bit)
         return self.got
 
@@ -882,13 +883,13 @@
 
 
 def unpack_kernel(where_ref, own_ref, got_ref, w_ref, in_ref, out_ref, sum_ref):
-    mine = where_ref[1]
+    mine = where_ref[2]
     half, _, rows, cols = own_ref.shape
     out_rows = out_ref.shape[0] // (2 * half)
     total = jnp.zeros((rows, LANES), f32)
-    for blocks_ref, first in ((own_ref, mine * half), (got_ref, (1 - mine) * half)):
+    for blocks_ref, bit in ((own_ref, mine), (got_ref, 1 - mine)):
         for block in range(half):
-            at = first + block
+            at = block // 2 * 4 + bit * 2 + block % 2
             for part in range(2):
                 place = pl.ds(pl.multiple_of(part * FF + at * cols, cols), cols)
                 value = blocks_ref[block, part].astype(f32)
@@ -968,7 +969,8 @@
     own_buckets = NUM_BUCKETS // shards
     width = reps.bit_length() - 1
     shard = lax.axis_index("shard")
-    where = jnp.stack([shard, lax.axis_index("rep") % 2]).astype(jnp.int32)
+    rep = lax.axis_index("rep")
+    where = jnp.stack([shard, rep % 2, rep // 2 % 2]).astype(jnp.int32)
     small = jnp.concatenate(
         [
             gains.T,
@@ -977,10 +979,10 @@
         ],
         axis=1,
     )
-    self_set = Gather(jnp.concatenate([self_qkv, self_out, small], axis=1), sizes)
+    self_set = Gather(jnp.concatenate([self_qkv, small], axis=1), sizes)
     self_set.cross()
     cross_set = Gather(
-        jnp.concatenate([cross_kv, cross_q, cross_out], axis=1), sizes, self_set.y
+        jnp.concatenate([cross_kv, cross_q, cross_out, self_out], axis=1), sizes, self_set.y
     )
     self_pieces = self_set.pieces()
 
@@ -1012,7 +1014,7 @@
     out_set.cross()
     in_set.cross()
     w_cross, ckv = encoder_step(where, enc_states, cross_pieces, [attn_one])
-    first, normed_two, cq = middle_step(hidden_in, attn_one, w_self, gains_all[1:2], w_cross)
+    first, normed_two, cq = middle_step(hidden_in, attn_one, gains_all[1:2], w_cross)
     attn_two, lows_two = attend_forward(
         cq, 0, ckv, 0, ckv, PAIRS, q_extra, cross_extra, None, CROSS_RANGES
     )
@@ -1035,7 +1037,7 @@
     meet(grad_cq, ff_out_chain)
     ff_out_chain.advance()
     grad_first, _, out_one, grad_attn_one = norm_back(
-        grad_cq, w_cross, 2, first, gains_all[1:2], grad_second, w_self, 3,
+        grad_cq, w_cross, 2, first, gains_all[1:2], grad_second, w_cross, 4,
         after=[ff_out_chain.sent],
     )
     meet(grad_attn_one, ff_in_chain, ff_out_chain)
@@ -1049,7 +1051,7 @@
     cross_send = meet(cross_send, ff_in_chain, ff_out_chain)
     ff_in_chain.advance()
     ff_out_chain.advance()
-    cross_chain = Chain(cross_keep, cross_send, sizes, [2, 1], "yr")
+    cross_chain = Chain(cross_keep, cross_send, sizes, [2, 1], "yr", turned=True)
     (enc_grad,) = norm_back(
         grad_ckv, w_cross, 0, after=[cross_keep, ff_in_chain.sent, ff_out_chain.sent]
     )
@@ -1067,7 +1069,7 @@
     rows, columns = in_own.shape[1:]
     out_rows = out_own.shape[0]
     out_own = out_own.reshape(out_rows, -1, columns).transpose(1, 0, 2).reshape(1, rows, columns)
-    bits = ff_in_chain.bits
+    bits = [2, 1, 4] if reps == 8 else ff_in_chain.bits
     blocks = Spread(
         jnp.concatenate([in_own, out_own], axis=0)[None], sizes, bits, [0] * len(bits)
     )
@@ -1106,16 +1108,10 @@
     cross_spread = None
     while last_chain.at < len(last_chain.steps):
         if last_chain.at == 3:
-            together(self_chain, last_chain, cross_spread or cross_chain, blocks)
+            together(self_chain, last_chain, cross_chain, blocks)
+            cross_spread = Spread(cross_chain.own(), sizes, cross_chain.bits, cross_chain.dims)
         else:
-            together(self_chain, last_chain, cross_spread or cross_chain)
-        if cross_spread is not None:
-            if cross_spread.left:
-                cross_spread.advance()
-        elif cross_chain.at < len(cross_chain.steps):
-            cross_chain.advance()
-        else:
-            cross_spread = Spread(cross_chain.own(), sizes, cross_chain.bits, cross_chain.dims)
+            together(self_chain, last_chain)
         self_chain.advance()
         last_chain.advance()
     together(self_chain, last_chain, cross_spread)
@@ -1137,7 +1133,7 @@
         [low[:, :self_width], high[:, :self_width], low[:, self_width:], high[:, self_width:]],
         axis=1,
     ).astype(f32)
-    cross_grad = jnp.concatenate(cross_spread.pair(), axis=2)[0].astype(f32)
+    cross_grad = jnp.concatenate(cross_spread.pair(), axis=cross_spread.now[1])[0].astype(f32)
 
     if reps == 8:
         ff_in_grad, ff_out_grad, in_sums = unpack(where, blocks.own, blocks.got, ff_in)

time: 453 us -> 427 us (0.943)
  other arithmetic: 55.2 us -> 38.3 us
  waiting for transfers between devices: 94.6 us -> 84.1 us
    convert_element_type x25, other arithmetic: 40.8 us -> 28.2 us  [the longest x20 27 us: half(): return lax.optimization_barrier((kept + got).astype(bf16))]
    ppermute x54, waiting for transfers between devices: 94.6 us -> 84.1 us  [exchange(): return lax.ppermute(array, axis, [(i, i ^ bit) for i in range(size)])]
    unnamed x121 -> x104, local copies, waits for them, and re-layouts: 10.2 us -> 8.62 us
  transfers between devices with their start and end apart: 54 -> 54, of which waited for: 21 -> 24; matrix products, arithmetic and copies ran while one was open for 11% -> 8% of each run, Pallas kernels for 40% -> 42%
where the time goes in v4:
time: 427 us; the launch traced here: 419 us
  Pallas kernels  221 us (52%)
  waiting for transfers between devices  84.1 us (20%)
  starting transfers between devices  53.8 us (13%)
  other arithmetic  38.3 us (9%)
  local copies, waits for them, and re-layouts  17.9 us (4%)
    ppermute x54, waiting for transfers between devices, exchange(): return lax.ppermute(array, axis, [(i, i ^ bit) for i in range(size)])  84.1 us
    ppermute x54, starting transfers between devices, exchange(): return lax.ppermute(array, axis, [(i, i ^ bit) for i in range(size)])  53.8 us
    pallas_call x3, Pallas kernels, attend_backward(): pl.pallas_call(partial(attend_backward_kernel, ranges, biased, len(after)...  52.1 us
    pallas_call x1, Pallas kernels, feed_forward(): pl.pallas_call(feed_forward_kernel, grid_spec=pltpu.PrefetchScalarGridSpe...  45.8 us
    pallas_call x2, Pallas kernels, attend_forward(): pl.pallas_call(partial(attend_forward_kernel, ranges, biased, len(after))...  33.8 us
    pallas_call x4, Pallas kernels, norm_back(): pl.pallas_call(partial(norm_back_kernel, x is not None, w_next is not Non...  31.3 us
    convert_element_type x20, other arithmetic, half(): return lax.optimization_barrier((kept + got).astype(bf16))  27 us
    pallas_call x2, Pallas kernels, weight_grad(): pl.pallas_call(partial(weight_grad_kernel, counts, firsts, len(after)), g...  25.1 us
  transfers between devices with their start and end apart: 54, of which 24 were waited for; matrix products, arithmetic and copies ran while one was open for 8% of the time, Pallas kernels for 42%

profile of v4, /device:TPU:0, one launch (start us, length us, event | category | flops | bytes accessed | tf_op | source)
XLA Modules:
  0.0 418.5 jit_solution(20847468400513045)
XLA Ops:
  3.6 3.0 collective-permute-start
  9.0 9.0 %collective-permute-done.refs_2_ = bf16[192,1280]{1,0:T(8,128)(2,1)} collective-permute-done((bf16[192,1280]{1,0:T(8,128)(2,1)S(1)}, bf16[192,1280]{1,0:T(8,128)(2,1)}, u32[]{:S(2)}, u32[]{:S(2)}) %collective-permute-start) | collective-permute-done | bytes 491552 | tf_op jit(solution)/shard_map/ppermute | solution.py:776
  18.0 1.7 collective-permute-start.3
  20.5 2.0 constant_dynamic-slice_fusion.2
  22.5 1.5 collective-permute-start.1
  24.0 7.9 %collective-permute-done.3.refs_3_ = bf16[192,1280]{1,0:T(8,128)(2,1)} collective-permute-done((bf16[192,1280]{1,0:T(8,128)(2,1)}, bf16[192,1280]{1,0:T(8,128)(2,1)}, u32[]{:S(2)}, u32[]{:S(2)}) %collective-permute-start.3) | collective-permute-done | bytes 491552 | tf_op jit(solution)/shard_map/ppermute | solution.py:776
  34.2 10.3 %shard_map.256 = (bf16[768,2560]{1,0:T(8,128)(2,1)}, f32[8,768]{1,0:T(8,128)}, f32[6,2,640]{2,1,0:T(2,128)}, bf16[1024,768]{1,0:T(8,128)(2,1)}, bf16[1024,2304]{1,0:T(8,128)(2,1)}) custom-call(s32[3]{0:T(128)} %pad_add_fusion.where_ref.core_ref, bf16[1024,768]{1,0:T(8,128)(2,1)} %refs_6_.1, bf16[768,640]{1,0:T(8,128)(2,1)} %constant.251.clone.onehot_ref, ...), custom_call_target="tpu_custom_call" | custom-call | flops 1000000 | bytes 100000 | tf_op jit(solution)/shard_map/pallas_call | solution.py:337
  44.5 1.8 collective-permute-start.7
  46.2 1.5 collective-permute-start.9
  50.7 18.4 %shard_map.257 = (bf16[1024,768]{1,0:T(8,128)(2,1)}, bf16[1024,768]{1,0:T(8,128)(2,1)}) custom-call(bf16[512,384]{1,0:T(8,128)(2,1)} %copy-done.17, bf16[192,2048]{1,0:T(8,128)(2,1)} %copy-done.9, bf16[1024,2304]{1,0:T(8,128)(2,1)} %get-tuple-element.104.refs_2_.refs_3_.refs_4_.refs_5_, ...), custom_call_target="tpu_custom_call" | custom-call | flops 1000000 | bytes 100000 | tf_op jit(solution)/shard_map/pallas_call | solution.py:130
  69.1 4.9 %collective-permute-done.8.y_o = bf16[512,384]{1,0:T(8,128)(2,1)S(1)} collective-permute-done((bf16[512,384]{1,0:T(8,128)(2,1)S(1)}, bf16[512,384]{1,0:T(8,128)(2,1)S(1)}, u32[]{:S(2)}, u32[]{:S(2)}) %collective-permute-start.8) | collective-permute-done | bytes 393248 | tf_op jit(solution)/shard_map/ppermute | solution.py:776
  74.9 1.7 collective-permute-start.13
  76.6 1.5 fusion.6
  79.2 9.8 %shard_map.258 = (bf16[768,3840]{1,0:T(8,128)(2,1)}, bf16[1024,1536]{1,0:T(8,128)(2,1)}) custom-call(s32[3]{0:T(128)} %pad_add_fusion.where_ref.core_ref, bf16[1024,768]{1,0:T(8,128)(2,1)} %get-tuple-element.106.refs_0_.attn_ref.refs_5_.refs_9_.refs_8_, bf16[1024,768]{1,0:T(8,128)(2,1)} %refs_2_.1, ...), custom_call_target="tpu_custom_call" | custom-call | flops 1000000 | bytes 100000 | tf_op jit(solution)/shard_map/pallas_call | solution.py:381
  89.0 7.4 %shard_map.259 = (f32[1024,768]{1,0:T(8,128)}, bf16[1024,768]{1,0:T(8,128)(2,1)}, bf16[1024,768]{1,0:T(8,128)(2,1)}) custom-call(bf16[1024,768]{1,0:T(8,128)(2,1)} %refs_6_.1, bf16[1024,768]{1,0:T(8,128)(2,1)} %get-tuple-element.106.refs_0_.attn_ref.refs_5_.refs_9_.refs_8_, ...), custom_call_target="tpu_custom_call" | custom-call | flops 1000000 | bytes 100000 | tf_op jit(solution)/shard_map/pallas_call | solution.py:414
  96.5 15.4 %shard_map.260 = (bf16[1024,768]{1,0:T(8,128)(2,1)}, bf16[1024,768]{1,0:T(8,128)(2,1)}) custom-call(bf16[1024,768]{1,0:T(8,128)(2,1)} %get-tuple-element.112.refs_0_.refs_2_, bf16[1024,1536]{1,0:T(8,128)(2,1)} %get-tuple-element.113.refs_1_.refs_2_.refs_3_.refs_4_, bf16[1024,1536]{1,0:T(8,128)(2,1)} %get-tuple-element.113.refs_1_.refs_2_.refs_3_.refs_4_, ...), custom_call_target="tpu_custom_call" | custom-call | flops 1000000 | bytes 100000 | tf_op jit(solution)/shard_map/pallas_call | solution.py:130
  112.6 1.6 collective-permute-done.17.core_o
  117.9 45.8 %shard_map.261 = (bf16[1024,768]{1,0:T(8,128)(2,1)}, f32[1024,768]{1,0:T(8,128)}, bf16[1024,768]{1,0:T(8,128)(2,1)}, bf16[2,2,192,2048]{3,2,1,0:T(8,128)(2,1)}, ...) custom-call(s32[3]{0:T(128)} %pad_add_fusion.where_ref.core_ref, ...), custom_call_target="tpu_custom_call" | custom-call | flops 1000000 | bytes 100000 | tf_op jit(solution)/shard_map/pallas_call | solution.py:576
  164.4 5.2 %shard_map.262.refs_9_ = bf16[1024,768]{1,0:T(8,128)(2,1)} custom-call(bf16[1024,768]{1,0:T(8,128)(2,1)} %get-tuple-element.86.refs_0_, bf16[1,1024,768]{2,1,0:T(8,128)(2,1)} %bitcast.33, bf16[768,3840]{1,0:T(8,128)(2,1)} %get-tuple-element.109.out_w_ref.q_w_ref.w2_ref.refs_2_.refs_6_.refs_4_), custom_call_target="tpu_custom_call" | custom-call | flops 1000000 | bytes 100000 | tf_op jit(solution)/shard_map/pallas_call | solution.py:764
  169.6 2.3 collective-permute-done.21
  172.0 1.7 copy-done.11
  173.7 3.2 add_convert_fusion.1
  176.9 1.8 collective-permute-start.22
  178.7 3.4 add_convert_fusion.7
  182.2 1.5 collective-permute-start.23
  183.7 22.7 %shard_map.263 = (bf16[1024,768]{1,0:T(8,128)(2,1)}, bf16[2,1024,768]{2,1,0:T(8,128)(2,1)}) custom-call(bf16[1,2,192,2048]{3,2,1,0:T(8,128)(2,1)} %copy-done.3, bf16[2,256,768]{2,1,0:T(8,128)(2,1)} %get-tuple-element.195.refs_1_, bf16[1024,768]{1,0:T(8,128)(2,1)} %get-tuple-element.112.refs_0_.refs_2_, ...), custom_call_target="tpu_custom_call" | custom-call | flops 1000000 | bytes 100000 | tf_op jit(solution)/shard_map/pallas_call | solution.py:257
  206.3 2.1 add_convert_fusion.16
  208.4 1.6 collective-permute-start.24
  210.0 8.9 %shard_map.264 = (f32[1024,768]{1,0:T(8,128)}, f32[1,768]{1,0:T(1,128)}, bf16[1024,768]{1,0:T(8,128)(2,1)}, bf16[1024,768]{1,0:T(8,128)(2,1)}) custom-call(bf16[2,128,768]{2,1,0:T(8,128)(2,1)} %get-tuple-element.209.refs_0_, bf16[1,1024,768]{2,1,0:T(8,128)(2,1)} %bitcast.34, ...), custom_call_target="tpu_custom_call" | custom-call | flops 1000000 | bytes 100000 | tf_op jit(solution)/shard_map/pallas_call | solution.py:764
  219.4 2.1 add_convert_fusion.5
  223.3 2.7 collective-permute-start.26
  226.0 15.7 %shard_map.265 = (bf16[2,192,3840]{2,1,0:T(8,128)(2,1)}, bf16[2,192,3840]{2,1,0:T(8,128)(2,1)}) custom-call(s32[3]{0:T(128)} %pad_add_fusion.where_ref.core_ref, bf16[1,2,192,1024]{3,2,1,0:T(8,128)(2,1)} %copy-done.8, bf16[2,64,768]{2,1,0:T(8,128)(2,1)} %copy-done.27, bf16[1024,768]{1,0:T(8,128)(2,1)} %refs_2_.1, ...), custom_call_target="tpu_custom_call" | custom-call | flops 1000000 | bytes 100000 | tf_op jit(solution)/shard_map/pallas_call | solution.py:684
  242.1 1.6 collective-permute-start.28
  244.6 7.1 %shard_map.266 = f32[1024,768]{1,0:T(8,128)} custom-call(bf16[2,192,3840]{2,1,0:T(8,128)(2,1)} %get-tuple-element.143.refs_0_, bf16[1,2,192,512]{3,2,1,0:T(8,128)(2,1)} %copy-done.19, bf16[1,64,768]{2,1,0:T(8,128)(2,1)} %copy-done.39, bf16[2,1024,768]{2,1,0:T(8,128)(2,1)} %get-tuple-element.137.refs_6_.refs_3_, ...), custom_call_target="tpu_custom_call" | custom-call | flops 1000000 | bytes 100000 | tf_op jit(solution)/shard_map/pallas_call | solution.py:764
  251.7 2.1 collective-permute-done.28
  253.8 2.5 add_convert_fusion.2
  257.1 1.9 add_convert_fusion.26
  261.6 14.7 %shard_map.267 = (bf16[3,1024,768]{2,1,0:T(8,128)(2,1)}, f32[3,2,640]{2,1,0:T(2,128)}) custom-call(bf16[1,192,3840]{2,1,0:T(8,128)(2,1)} %copy-done.6, bf16[1,2,192,256]{3,2,1,0:T(8,128)(2,1)} %get-tuple-element.223.refs_1_, bf16[64,768]{1,0:T(8,128)(2,1)} %bitcast.35, bf16[1024,2304]{1,0:T(8,128)(2,1)} %get-tuple-element.104.refs_2_.refs_3_.refs_4_.refs_5_, ...), custom_call_target="tpu_custom_call" | custom-call | flops 1000000 | bytes 100000 | tf_op jit(solution)/shard_map/pallas_call | solution.py:257
  277.4 1.9 collective-permute-start.32
  279.2 14.7 %shard_map.268 = (bf16[3,1024,768]{2,1,0:T(8,128)(2,1)}, f32[3,2,640]{2,1,0:T(2,128)}) custom-call(bf16[3,1024,768]{2,1,0:T(8,128)(2,1)} %get-tuple-element.150.refs_0_, bf16[1,3,192,256]{3,2,1,0:T(8,128)(2,1)} %copy-done.24, bf16[1024,2304]{1,0:T(8,128)(2,1)} %get-tuple-element.104.refs_2_.refs_3_.refs_4_.refs_5_, ...), custom_call_target="tpu_custom_call", output_to_operand_aliasing={{0}: (0, {})} | custom-call | flops 1000000 | bytes 100000 | tf_op jit(solution)/shard_map/pallas_call | solution.py:257
  294.0 1.7 add_convert_fusion.8
  295.7 1.6 collective-permute-start.34
  298.4 1.6 collective-permute-start.33
  302.2 9.4 %shard_map.269 = (bf16[2,192,1536]{2,1,0:T(8,128)(2,1)}, bf16[2,192,1536]{2,1,0:T(8,128)(2,1)}, bf16[2,192,1024]{2,1,0:T(8,128)(2,1)}, bf16[2,192,1024]{2,1,0:T(8,128)(2,1)}) custom-call(s32[3]{0:T(128)} %pad_add_fusion.where_ref.core_ref, bf16[2,3,192,256]{3,2,1,0:T(8,128)(2,1)} %copy-done.14, bf16[1,96,3840]{2,1,0:T(8,128)(2,1)} %copy-done.13, ...), custom_call_target="tpu_custom_call" | custom-call | flops 1000000 | bytes 100000 | tf_op jit(solution)/shard_map/pallas_call | solution.py:684
  313.6 2.1 add_convert_fusion.18
  317.3 1.6 add_convert_fusion.10
  323.0 1.7 collective-permute-start.45
  324.7 10.0 %shard_map.270 = (f32[1024,768]{1,0:T(8,128)}, f32[1,768]{1,0:T(1,128)}) custom-call(bf16[1,192,1536]{2,1,0:T(8,128)(2,1)} %copy-done.15, bf16[2,192,512]{2,1,0:T(8,128)(2,1)} %copy-done.18, bf16[1,96,1920]{2,1,0:T(8,128)(2,1)} %get-tuple-element.213.refs_2_, bf16[4,3,192,256]{3,2,1,0:T(8,128)(2,1)} %copy-done.2, ...), custom_call_target="tpu_custom_call" | custom-call | flops 1000000 | bytes 100000 | tf_op jit(solution)/shard_map/pallas_call | solution.py:764
  336.2 1.5 collective-permute-start.40
  338.8 1.7 collective-permute-start.41
  341.6 1.7 collective-permute-start.44
  343.3 15.2 %collective-permute-done.41 = bf16[2,96,512]{2,1,0:T(8,128)(2,1)S(1)} collective-permute-done((bf16[2,96,512]{2,1,0:T(8,128)(2,1)S(1)}, bf16[2,96,512]{2,1,0:T(8,128)(2,1)S(1)}, u32[]{:S(2)}, u32[]{:S(2)}) %collective-permute-start.41) | collective-permute-done | bytes 196640 | tf_op jit(solution)/shard_map/ppermute | solution.py:776
  358.8 3.3 collective-permute-start.43
  362.1 2.8 collective-permute-done.43
  365.1 2.6 collective-permute-start.48
  369.1 3.3 collective-permute-done.47
  372.4 5.3 %collective-permute-done.46 = bf16[1,48,768]{2,1,0:T(8,128)(2,1)S(1)} collective-permute-done((bf16[1,48,768]{2,1,0:T(8,128)(2,1)S(1)}, bf16[1,48,768]{2,1,0:T(8,128)(2,1)S(1)}, u32[]{:S(2)}, u32[]{:S(2)}) %collective-permute-start.46) | collective-permute-done | bytes 73760 | tf_op jit(solution)/shard_map/ppermute | solution.py:776
  378.4 6.8 %collective-permute-done.49 = bf16[1,48,1280]{2,1,0:T(8,128)(2,1)S(1)} collective-permute-done((bf16[1,48,1280]{2,1,0:T(8,128)(2,1)S(1)}, bf16[1,48,1280]{2,1,0:T(8,128)(2,1)S(1)}, u32[]{:S(2)}, u32[]{:S(2)}) %collective-permute-start.49) | collective-permute-done | bytes 122912 | tf_op jit(solution)/shard_map/ppermute | solution.py:776
  385.2 2.6 collective-permute-done.50
  387.9 5.7 %shard_map.271 = (f32[192,4096]{1,0:T(8,128)}, f32[512,768]{1,0:T(8,128)}, f32[8,192]{1,0:T(8,128)}) custom-call(s32[3]{0:T(128)} %pad_add_fusion.where_ref.core_ref, bf16[4,3,192,256]{3,2,1,0:T(8,128)(2,1)} %copy-done.2, bf16[4,3,192,256]{3,2,1,0:T(8,128)(2,1)} %collective-permute-done.45.got_ref, bf16[192,4096]{1,0:T(8,128)(2,1)} %w_ref.1), custom_call_target="tpu_custom_call" | custom-call | flops 1000000 | bytes 100000 | tf_op jit(solution)/shard_map/pallas_call | solution.py:920
  395.4 1.9 collective-permute-start.53
  397.3 8.8 %collective-permute-done.52 = bf16[1,192,1280]{2,1,0:T(8,128)(2,1)S(1)} collective-permute-done((bf16[1,192,1280]{2,1,0:T(8,128)(2,1)S(1)}, bf16[1,192,1280]{2,1,0:T(8,128)(2,1)S(1)}, u32[]{:S(2)}, u32[]{:S(2)}) %collective-permute-start.52) | collective-permute-done | bytes 491552 | tf_op jit(solution)/shard_map/ppermute | solution.py:776
  407.2 4.9 %collective-permute-done.53 = bf16[1,96,3840]{2,1,0:T(8,128)(2,1)S(1)} collective-permute-done((bf16[1,96,3840]{2,1,0:T(8,128)(2,1)S(1)}, bf16[1,96,3840]{2,1,0:T(8,128)(2,1)S(1)}, u32[]{:S(2)}, u32[]{:S(2)}) %collective-permute-start.53) | collective-permute-done | bytes 737312 | tf_op jit(solution)/shard_map/ppermute | solution.py:776
  416.0 1.5 multiply_reduce_fusion
  (238 shorter events, 50.8 us)
Async XLA Ops:
  3.5 14.5 %copy-start.5 = (bf16[192,2560]{1,0:T(8,128)(2,1)}, bf16[192,2560]{1,0:T(8,128)(2,1)S(1)}, u32[]{:S(2)}) copy-start(bf16[192,2560]{1,0:T(8,128)(2,1)S(1)} %concatenate.40.refs_0_) | copy-start | bytes 2949124
  3.6 16.1 %copy-start.43 = (bf16[192,768]{1,0:T(8,128)(2,1)S(1)}, bf16[192,768]{1,0:T(8,128)(2,1)}, u32[]{:S(2)}) copy-start(bf16[192,768]{1,0:T(8,128)(2,1)} %param.25) | copy-start | bytes 884740
  3.6 14.4 %collective-permute-start = (bf16[192,1280]{1,0:T(8,128)(2,1)S(1)}, bf16[192,1280]{1,0:T(8,128)(2,1)}, u32[]{:S(2)}, u32[]{:S(2)}) collective-permute-start(bf16[192,1280]{1,0:T(8,128)(2,1)S(1)} %constant_dynamic-slice_fusion.1), channel_id=1, source_target_pairs={{0,2},{1,3},{2,0},{3,1},{4,6},{5,7},{6,4},{7,5},{8,10},{9,11},{10,... | collective-permute-start | bytes 1474568 | tf_op jit(solution)/shard_map/ppermute | solution.py:776
  7.5 25.1 %copy-start = (bf16[192,4096]{1,0:T(8,128)(2,1)S(1)}, bf16[192,4096]{1,0:T(8,128)(2,1)}, u32[]{:S(2)}) copy-start(bf16[192,4096]{1,0:T(8,128)(2,1)} %w_ref.1) | copy-start | bytes 4718596
  18.0 14.7 %collective-permute-start.2 = (bf16[192,2560]{1,0:T(8,128)(2,1)S(1)}, bf16[192,2560]{1,0:T(8,128)(2,1)S(1)}, u32[]{:S(2)}, u32[]{:S(2)}) collective-permute-start(bf16[192,2560]{1,0:T(8,128)(2,1)S(1)} %concatenate.40.refs_0_), channel_id=1, source_target_pairs={{0,1},{1,0},{2,3},{3,2},{4,5},{5,4},{6,7},{7,6},{8,9},{9,8},{10,11... | collective-permute-start | bytes 2949128 | tf_op jit(solution)/shard_map/ppermute | solution.py:776
  18.0 14.0 %collective-permute-start.3 = (bf16[192,1280]{1,0:T(8,128)(2,1)}, bf16[192,1280]{1,0:T(8,128)(2,1)}, u32[]{:S(2)}, u32[]{:S(2)}) collective-permute-start(bf16[192,1280]{1,0:T(8,128)(2,1)} %collective-permute-done.refs_2_), channel_id=1, source_target_pairs={{0,4},{4,0},{8,12},{12,8},{16,20},{20,16},{24,28},{28,24},{1,5},{5... | collective-permute-start | bytes 1474568 | tf_op jit(solution)/shard_map/ppermute | solution.py:776
  22.5 22.0 %collective-permute-start.1 = (bf16[192,1920]{1,0:T(8,128)(2,1)}, bf16[192,1920]{1,0:T(8,128)(2,1)}, u32[]{:S(2)}, u32[]{:S(2)}) collective-permute-start(bf16[192,1920]{1,0:T(8,128)(2,1)} %constant_dynamic-slice_fusion.2), channel_id=1, source_target_pairs={{0,2},{1,3},{2,0},{3,1},{4,6},{5,7},{6,4},{7,5},{8,10},{9,11},{10,... | collective-permute-start | bytes 2211848 | tf_op jit(solution)/shard_map/ppermute | solution.py:776
  24.0 8.7 %collective-permute-start.4 = (bf16[192,1280]{1,0:T(8,128)(2,1)}, bf16[192,1280]{1,0:T(8,128)(2,1)}, u32[]{:S(2)}, u32[]{:S(2)}) collective-permute-start(bf16[192,1280]{1,0:T(8,128)(2,1)} %collective-permute-done.refs_2_), channel_id=1, source_target_pairs={{0,1},{1,0},{2,3},{3,2},{4,5},{5,4},{6,7},{7,6},{8,9},{9,8},{10,11... | collective-permute-start | bytes 1474568 | tf_op jit(solution)/shard_map/ppermute | solution.py:776
  32.0 2.2 collective-permute-start.5
  32.7 15.1 %copy-start.16 = (bf16[512,768]{1,0:T(8,128)(2,1)S(1)}, bf16[512,768]{1,0:T(8,128)(2,1)}, u32[]{:S(2)}) copy-start(bf16[512,768]{1,0:T(8,128)(2,1)} %own_o.1) | copy-start | bytes 2359300
  32.7 15.8 %copy-start.45 = (s32[1024]{0:T(1024)S(1)}, s32[1024]{0:T(1024)}, u32[]{:S(2)}) copy-start(s32[1024]{0:T(1024)} %param.19) | copy-start | bytes 12292
  32.7 16.8 %copy-start.49 = (s32[1024]{0:T(1024)S(1)}, s32[1024]{0:T(1024)}, u32[]{:S(2)}) copy-start(s32[1024]{0:T(1024)} %param.20) | copy-start | bytes 12292
  44.5 29.5 %collective-permute-start.7 = (bf16[192,1920]{1,0:T(8,128)(2,1)}, bf16[192,1920]{1,0:T(8,128)(2,1)}, u32[]{:S(2)}, u32[]{:S(2)}) collective-permute-start(bf16[192,1920]{1,0:T(8,128)(2,1)} %collective-permute-done.1.refs_4_), channel_id=1, source_target_pairs={{0,4},{4,0},{8,12},{12,8},{16,20},{20,16},{24,28},{28,24},{1,5},{5... | collective-permute-start | bytes 2211848 | tf_op jit(solution)/shard_map/ppermute | solution.py:776
  46.2 27.7 %collective-permute-start.9 = (bf16[192,2048]{1,0:T(8,128)(2,1)S(1)}, bf16[192,2048]{1,0:T(8,128)(2,1)S(1)}, u32[]{:S(2)}, u32[]{:S(2)}) collective-permute-start(bf16[192,2048]{1,0:T(8,128)(2,1)S(1)} %constant_dynamic-slice_fusion.refs_1_), channel_id=1, source_target_pairs={{0,2},{1,3},{2,0},{3,1},{4,6},{5,7},{6,4},{7,5},{8,10},{9,11},{10,... | collective-permute-start | bytes 2359304 | tf_op jit(solution)/shard_map/ppermute | solution.py:776
  47.8 30.2 %collective-permute-start.6 = (bf16[192,3840]{1,0:T(8,128)(2,1)}, bf16[192,3840]{1,0:T(8,128)(2,1)S(1)}, u32[]{:S(2)}, u32[]{:S(2)}) collective-permute-start(bf16[192,3840]{1,0:T(8,128)(2,1)} %constant_dynamic-update-slice_fusion.refs_2_), channel_id=1, source_target_pairs={{0,1},{1,0},{2,3},{3,2},{4,5},{5,4},{6,7},{7,6},{8,9},{9,8},{10,11... | collective-permute-start | bytes 4423688 | tf_op jit(solution)/shard_map/ppermute | solution.py:776
  47.9 26.1 %collective-permute-start.8 = (bf16[512,384]{1,0:T(8,128)(2,1)S(1)}, bf16[512,384]{1,0:T(8,128)(2,1)S(1)}, u32[]{:S(2)}, u32[]{:S(2)}) collective-permute-start(bf16[512,384]{1,0:T(8,128)(2,1)S(1)} %constant_dynamic-slice_fusion.3.refs_0_), channel_id=1, source_target_pairs={{0,2},{1,3},{2,0},{3,1},{4,6},{5,7},{6,4},{7,5},{8,10},{9,11},{10,... | collective-permute-start | bytes 1179656 | tf_op jit(solution)/shard_map/ppermute | solution.py:776
  49.4 25.5 %collective-permute-start.10 = (bf16[192,1920]{1,0:T(8,128)(2,1)}, bf16[192,1920]{1,0:T(8,128)(2,1)S(1)}, u32[]{:S(2)}, u32[]{:S(2)}) collective-permute-start(bf16[192,1920]{1,0:T(8,128)(2,1)} %collective-permute-done.1.refs_4_), channel_id=1, source_target_pairs={{0,1},{1,0},{2,3},{3,2},{4,5},{5,4},{6,7},{7,6},{8,9},{9,8},{10,11... | collective-permute-start | bytes 2211848 | tf_op jit(solution)/shard_map/ppermute | solution.py:776
  74.0 22.5 %copy-start.40 = (bf16[512,384]{1,0:T(8,128)(2,1)}, bf16[512,384]{1,0:T(8,128)(2,1)S(1)}, u32[]{:S(2)}) copy-start(bf16[512,384]{1,0:T(8,128)(2,1)S(1)} %collective-permute-done.8.y_o) | copy-start | bytes 1179652
  74.0 22.5 %copy-start.28 = (bf16[192,2048]{1,0:T(8,128)(2,1)}, bf16[192,2048]{1,0:T(8,128)(2,1)S(1)}, u32[]{:S(2)}) copy-start(bf16[192,2048]{1,0:T(8,128)(2,1)S(1)} %collective-permute-done.9.y_in) | copy-start | bytes 2359300
  74.0 38.1 %collective-permute-start.14 = (bf16[192,2048]{1,0:T(8,128)(2,1)S(1)}, bf16[192,2048]{1,0:T(8,128)(2,1)S(1)}, u32[]{:S(2)}, u32[]{:S(2)}) collective-permute-start(bf16[192,2048]{1,0:T(8,128)(2,1)S(1)} %collective-permute-done.9.y_in), channel_id=1, source_target_pairs={{0,4},{4,0},{8,12},{12,8},{16,20},{20,16},{24,28},{28,24},{1,5},{5... | collective-permute-start | bytes 2359304 | tf_op jit(solution)/shard_map/ppermute | solution.py:776
  74.4 41.5 %collective-permute-start.12 = (bf16[192,4096]{1,0:T(8,128)(2,1)S(1)}, bf16[192,4096]{1,0:T(8,128)(2,1)S(1)}, u32[]{:S(2)}, u32[]{:S(2)}) collective-permute-start(bf16[192,4096]{1,0:T(8,128)(2,1)S(1)} %copy-done), channel_id=1, source_target_pairs={{0,1},{1,0},{2,3},{3,2},{4,5},{5,4},{6,7},{7,6},{8,9},{9,8},{10,11... | collective-permute-start | bytes 4718600 | tf_op jit(solution)/shard_map/ppermute | solution.py:776
  74.4 4.4 %collective-permute-start.11 = (bf16[192,1920]{1,0:T(8,128)(2,1)}, bf16[192,1920]{1,0:T(8,128)(2,1)}, u32[]{:S(2)}, u32[]{:S(2)}) collective-permute-start(bf16[192,1920]{1,0:T(8,128)(2,1)} %collective-permute-done.7.refs_5_), channel_id=1, source_target_pairs={{0,1},{1,0},{2,3},{3,2},{4,5},{5,4},{6,7},{7,6},{8,9},{9,8},{10,11... | collective-permute-start | bytes 2211848 | tf_op jit(solution)/shard_map/ppermute | solution.py:776
  74.9 37.0 %collective-permute-start.13 = (bf16[512,384]{1,0:T(8,128)(2,1)S(1)}, bf16[512,384]{1,0:T(8,128)(2,1)}, u32[]{:S(2)}, u32[]{:S(2)}) collective-permute-start(bf16[512,384]{1,0:T(8,128)(2,1)S(1)} %collective-permute-done.8.y_o), channel_id=1, source_target_pairs={{0,4},{4,0},{8,12},{12,8},{16,20},{20,16},{24,28},{28,24},{1,5},{5... | collective-permute-start | bytes 1179656 | tf_op jit(solution)/shard_map/ppermute | solution.py:776
  78.1 36.2 %collective-permute-start.15 = (bf16[192,2048]{1,0:T(8,128)(2,1)S(1)}, bf16[192,2048]{1,0:T(8,128)(2,1)S(1)}, u32[]{:S(2)}, u32[]{:S(2)}) collective-permute-start(bf16[192,2048]{1,0:T(8,128)(2,1)S(1)} %collective-permute-done.9.y_in), channel_id=1, source_target_pairs={{0,1},{1,0},{2,3},{3,2},{4,5},{5,4},{6,7},{7,6},{8,9},{9,8},{10,11... | collective-permute-start | bytes 2359304 | tf_op jit(solution)/shard_map/ppermute | solution.py:776
  78.9 33.6 %collective-permute-start.18 = (bf16[512,384]{1,0:T(8,128)(2,1)S(1)}, bf16[512,384]{1,0:T(8,128)(2,1)}, u32[]{:S(2)}, u32[]{:S(2)}) collective-permute-start(bf16[512,384]{1,0:T(8,128)(2,1)S(1)} %collective-permute-done.8.y_o), channel_id=1, source_target_pairs={{0,1},{1,0},{2,3},{3,2},{4,5},{5,4},{6,7},{7,6},{8,9},{9,8},{10,11... | collective-permute-start | bytes 1179656 | tf_op jit(solution)/shard_map/ppermute | solution.py:776
  111.9 2.3 collective-permute-start.17
  112.1 3.8 collective-permute-start.16
  112.5 3.1 collective-permute-start.19
  163.8 8.2 %collective-permute-start.20 = (bf16[2,2,192,2048]{3,2,1,0:T(8,128)(2,1)}, bf16[2,2,192,2048]{3,2,1,0:T(8,128)(2,1)S(1)}, u32[]{:S(2)}, u32[]{:S(2)}) collective-permute-start(bf16[2,2,192,2048]{3,2,1,0:T(8,128)(2,1)} %get-tuple-element.123), channel_id=1, source_target_pairs={{0,1},{1,0},{2,3},{3,2},{4,5},{5,4},{6,7},{7,6},{8,9},{9,8},{10,11... | collective-permute-start | bytes 9437192 | tf_op jit(solution)/shard_map/ppermute | solution.py:776
  164.0 7.9 %collective-permute-start.21 = (bf16[2,512,768]{2,1,0:T(8,128)(2,1)}, bf16[2,512,768]{2,1,0:T(8,128)(2,1)}, u32[]{:S(2)}, u32[]{:S(2)}) collective-permute-start(bf16[2,512,768]{2,1,0:T(8,128)(2,1)} %get-tuple-element.124), channel_id=1, source_target_pairs={{0,1},{1,0},{2,3},{3,2},{4,5},{5,4},{6,7},{7,6},{8,9},{9,8},{10,11... | collective-permute-start | bytes 4718600 | tf_op jit(solution)/shard_map/ppermute | solution.py:776
  176.9 42.5 %collective-permute-start.22 = (bf16[1,2,192,2048]{3,2,1,0:T(8,128)(2,1)S(1)}, bf16[1,2,192,2048]{3,2,1,0:T(8,128)(2,1)}, u32[]{:S(2)}, u32[]{:S(2)}) collective-permute-start(bf16[1,2,192,2048]{3,2,1,0:T(8,128)(2,1)S(1)} %get-tuple-element.189.refs_0_), channel_id=1, source_target_pairs={{0,2},{1,3},{2,0},{3,1},{4,6},{5,7},{6,4},{7,5},{8,10},{9,11},{10,... | collective-permute-start | bytes 4718600 | tf_op jit(solution)/shard_map/ppermute | solution.py:776
  182.2 24.2 %collective-permute-start.23 = (bf16[2,256,768]{2,1,0:T(8,128)(2,1)}, bf16[2,256,768]{2,1,0:T(8,128)(2,1)}, u32[]{:S(2)}, u32[]{:S(2)}) collective-permute-start(bf16[2,256,768]{2,1,0:T(8,128)(2,1)} %get-tuple-element.195.refs_1_), channel_id=1, source_target_pairs={{0,4},{4,0},{8,12},{12,8},{16,20},{20,16},{24,28},{28,24},{1,5},{5... | collective-permute-start | bytes 2359304 | tf_op jit(solution)/shard_map/ppermute | solution.py:776
  183.7 22.7 %copy-start.12 = (bf16[2,256,768]{2,1,0:T(8,128)(2,1)S(1)}, bf16[2,256,768]{2,1,0:T(8,128)(2,1)}, u32[]{:S(2)}) copy-start(bf16[2,256,768]{2,1,0:T(8,128)(2,1)} %get-tuple-element.194) | copy-start | bytes 2359300
  208.4 11.1 %collective-permute-start.24 = (bf16[2,128,768]{2,1,0:T(8,128)(2,1)}, bf16[2,128,768]{2,1,0:T(8,128)(2,1)}, u32[]{:S(2)}, u32[]{:S(2)}) collective-permute-start(bf16[2,128,768]{2,1,0:T(8,128)(2,1)} %get-tuple-element.209.refs_0_), channel_id=1, source_target_pairs={{0,8},{4,12},{8,0},{12,4},{16,24},{20,28},{24,16},{28,20},{1,9},{5... | collective-permute-start | bytes 1179656 | tf_op jit(solution)/shard_map/ppermute | solution.py:776
  221.5 20.2 %collective-permute-start.25 = (bf16[1,2,192,1024]{3,2,1,0:T(8,128)(2,1)S(1)}, bf16[1,2,192,1024]{3,2,1,0:T(8,128)(2,1)S(1)}, u32[]{:S(2)}, u32[]{:S(2)}) collective-permute-start(bf16[1,2,192,1024]{3,2,1,0:T(8,128)(2,1)S(1)} %get-tuple-element.193.refs_0_), channel_id=1, source_target_pairs={{0,4},{4,0},{8,12},{12,8},{16,20},{20,16},{24,28},{28,24},{1,5},{5... | collective-permute-start | bytes 2359304 | tf_op jit(solution)/shard_map/ppermute | solution.py:776
  223.3 18.3 %collective-permute-start.26 = (bf16[2,64,768]{2,1,0:T(8,128)(2,1)S(1)}, bf16[2,64,768]{2,1,0:T(8,128)(2,1)S(1)}, u32[]{:S(2)}, u32[]{:S(2)}) collective-permute-start(bf16[2,64,768]{2,1,0:T(8,128)(2,1)S(1)} %get-tuple-element.225.refs_1_), channel_id=1, source_target_pairs={{0,16},{4,20},{8,24},{12,28},{16,0},{20,4},{24,8},{28,12},{1,17},{... | collective-permute-start | bytes 589832 | tf_op jit(solution)/shard_map/ppermute | solution.py:776
  241.7 12.1 %collective-permute-start.27 = (bf16[2,192,3840]{2,1,0:T(8,128)(2,1)}, bf16[2,192,3840]{2,1,0:T(8,128)(2,1)}, u32[]{:S(2)}, u32[]{:S(2)}) collective-permute-start(bf16[2,192,3840]{2,1,0:T(8,128)(2,1)} %get-tuple-element.141), channel_id=1, source_target_pairs={{0,1},{1,0},{2,3},{3,2},{4,5},{5,4},{6,7},{7,6},{8,9},{9,8},{10,11... | collective-permute-start | bytes 8847368 | tf_op jit(solution)/shard_map/ppermute | solution.py:776
  242.1 11.7 %collective-permute-start.28 = (bf16[1,2,192,512]{3,2,1,0:T(8,128)(2,1)S(1)}, bf16[1,2,192,512]{3,2,1,0:T(8,128)(2,1)}, u32[]{:S(2)}, u32[]{:S(2)}) collective-permute-start(bf16[1,2,192,512]{3,2,1,0:T(8,128)(2,1)S(1)} %get-tuple-element.207.refs_1_), channel_id=1, source_target_pairs={{0,8},{4,12},{8,0},{12,4},{16,24},{20,28},{24,16},{28,20},{1,9},{5... | collective-permute-start | bytes 1179656 | tf_op jit(solution)/shard_map/ppermute | solution.py:776
  243.9 7.9 %collective-permute-start.29 = (bf16[1,64,768]{2,1,0:T(8,128)(2,1)S(1)}, bf16[1,64,768]{2,1,0:T(8,128)(2,1)S(1)}, u32[]{:S(2)}, u32[]{:S(2)}) collective-permute-start(bf16[1,64,768]{2,1,0:T(8,128)(2,1)S(1)} %get-tuple-element.239.refs_2_), channel_id=1, source_target_pairs={{0,2},{1,3},{2,0},{3,1},{4,6},{5,7},{6,4},{7,5},{8,10},{9,11},{10,... | collective-permute-start | bytes 294920 | tf_op jit(solution)/shard_map/ppermute | solution.py:776
  256.3 37.6 %collective-permute-start.31 = (bf16[1,192,3840]{2,1,0:T(8,128)(2,1)S(1)}, bf16[1,192,3840]{2,1,0:T(8,128)(2,1)}, u32[]{:S(2)}, u32[]{:S(2)}) collective-permute-start(bf16[1,192,3840]{2,1,0:T(8,128)(2,1)S(1)} %get-tuple-element.191.refs_0_), channel_id=1, source_target_pairs={{0,2},{1,3},{2,0},{3,1},{4,6},{5,7},{6,4},{7,5},{8,10},{9,11},{10,... | collective-permute-start | bytes 4423688 | tf_op jit(solution)/shard_map/ppermute | solution.py:776
  258.9 17.4 %collective-permute-start.30 = (bf16[1,2,192,256]{3,2,1,0:T(8,128)(2,1)}, bf16[1,2,192,256]{3,2,1,0:T(8,128)(2,1)}, u32[]{:S(2)}, u32[]{:S(2)}) collective-permute-start(bf16[1,2,192,256]{3,2,1,0:T(8,128)(2,1)} %get-tuple-element.223.refs_1_), channel_id=1, source_target_pairs={{0,16},{4,20},{8,24},{12,28},{16,0},{20,4},{24,8},{28,12},{1,17},{... | collective-permute-start | bytes 589832 | tf_op jit(solution)/shard_map/ppermute | solution.py:776
  261.6 14.7 %copy-start.34 = (bf16[1,2,192,256]{3,2,1,0:T(8,128)(2,1)S(1)}, bf16[1,2,192,256]{3,2,1,0:T(8,128)(2,1)}, u32[]{:S(2)}) copy-start(bf16[1,2,192,256]{3,2,1,0:T(8,128)(2,1)} %get-tuple-element.222) | copy-start | bytes 589828
  277.4 16.6 %collective-permute-start.32 = (bf16[1,3,192,256]{3,2,1,0:T(8,128)(2,1)S(1)}, bf16[1,3,192,256]{3,2,1,0:T(8,128)(2,1)}, u32[]{:S(2)}, u32[]{:S(2)}) collective-permute-start(bf16[1,3,192,256]{3,2,1,0:T(8,128)(2,1)S(1)} %maximum_bitcast_fusion.1.refs_1_), channel_id=1, source_target_pairs={{0,16},{4,20},{8,24},{12,28},{16,0},{20,4},{24,8},{28,12},{1,17},{... | collective-permute-start | bytes 884744 | tf_op jit(solution)/shard_map/ppermute | solution.py:776
  295.7 17.4 %collective-permute-start.34 = (bf16[1,96,3840]{2,1,0:T(8,128)(2,1)S(1)}, bf16[1,96,3840]{2,1,0:T(8,128)(2,1)}, u32[]{:S(2)}, u32[]{:S(2)}) collective-permute-start(bf16[1,96,3840]{2,1,0:T(8,128)(2,1)S(1)} %get-tuple-element.201.refs_1_), channel_id=1, source_target_pairs={{0,8},{4,12},{8,0},{12,4},{16,24},{20,28},{24,16},{28,20},{1,9},{5... | collective-permute-start | bytes 2211848 | tf_op jit(solution)/shard_map/ppermute | solution.py:776
  298.4 13.9 %collective-permute-start.33 = (bf16[2,3,192,256]{3,2,1,0:T(8,128)(2,1)S(1)}, bf16[2,3,192,256]{3,2,1,0:T(8,128)(2,1)S(1)}, u32[]{:S(2)}, u32[]{:S(2)}) collective-permute-start(bf16[2,3,192,256]{3,2,1,0:T(8,128)(2,1)S(1)} %pad_maximum_fusion.2.refs_0_), channel_id=1, source_target_pairs={{0,4},{4,0},{8,12},{12,8},{16,20},{20,16},{24,28},{28,24},{1,5},{5... | collective-permute-start | bytes 1769480 | tf_op jit(solution)/shard_map/ppermute | solution.py:776
  313.1 4.1 collective-permute-start.35
  313.1 7.1 %collective-permute-start.36 = (bf16[2,192,1024]{2,1,0:T(8,128)(2,1)}, bf16[2,192,1024]{2,1,0:T(8,128)(2,1)}, u32[]{:S(2)}, u32[]{:S(2)}) collective-permute-start(bf16[2,192,1024]{2,1,0:T(8,128)(2,1)} %get-tuple-element.161), channel_id=1, source_target_pairs={{0,1},{1,0},{2,3},{3,2},{4,5},{5,4},{6,7},{7,6},{8,9},{9,8},{10,11... | collective-permute-start | bytes 2359304 | tf_op jit(solution)/shard_map/ppermute | solution.py:776
  315.7 19.0 %collective-permute-start.39 = (bf16[1,96,1920]{2,1,0:T(8,128)(2,1)}, bf16[1,96,1920]{2,1,0:T(8,128)(2,1)}, u32[]{:S(2)}, u32[]{:S(2)}) collective-permute-start(bf16[1,96,1920]{2,1,0:T(8,128)(2,1)} %get-tuple-element.213.refs_2_), channel_id=1, source_target_pairs={{0,4},{4,0},{8,12},{12,8},{16,20},{20,16},{24,28},{28,24},{1,5},{5... | collective-permute-start | bytes 1105928 | tf_op jit(solution)/shard_map/ppermute | solution.py:776
  318.9 16.1 %collective-permute-start.37 = (bf16[1,192,1536]{2,1,0:T(8,128)(2,1)S(1)}, bf16[1,192,1536]{2,1,0:T(8,128)(2,1)}, u32[]{:S(2)}, u32[]{:S(2)}) collective-permute-start(bf16[1,192,1536]{2,1,0:T(8,128)(2,1)S(1)} %get-tuple-element.203.refs_0_), channel_id=1, source_target_pairs={{0,2},{1,3},{2,0},{3,1},{4,6},{5,7},{6,4},{7,5},{8,10},{9,11},{10,... | collective-permute-start | bytes 1769480 | tf_op jit(solution)/shard_map/ppermute | solution.py:776
  321.6 13.3 %collective-permute-start.38 = (bf16[2,192,512]{2,1,0:T(8,128)(2,1)S(1)}, bf16[2,192,512]{2,1,0:T(8,128)(2,1)}, u32[]{:S(2)}, u32[]{:S(2)}) collective-permute-start(bf16[2,192,512]{2,1,0:T(8,128)(2,1)S(1)} %get-tuple-element.205.refs_1_), channel_id=1, source_target_pairs={{0,4},{4,0},{8,12},{12,8},{16,20},{20,16},{24,28},{28,24},{1,5},{5... | collective-permute-start | bytes 1179656 | tf_op jit(solution)/shard_map/ppermute | solution.py:776
  323.0 39.1 %collective-permute-start.45 = (bf16[4,3,192,256]{3,2,1,0:T(8,128)(2,1)S(1)}, bf16[4,3,192,256]{3,2,1,0:T(8,128)(2,1)}, u32[]{:S(2)}, u32[]{:S(2)}) collective-permute-start(bf16[4,3,192,256]{3,2,1,0:T(8,128)(2,1)S(1)} %pad_maximum_fusion.refs_3_.own_ref), channel_id=1, source_target_pairs={{0,8},{4,12},{8,0},{12,4},{16,24},{20,28},{24,16},{28,20},{1,9},{5... | collective-permute-start | bytes 3538952 | tf_op jit(solution)/shard_map/ppermute | solution.py:776
  336.2 22.4 %collective-permute-start.40 = (bf16[1,192,768]{2,1,0:T(8,128)(2,1)S(1)}, bf16[1,192,768]{2,1,0:T(8,128)(2,1)S(1)}, u32[]{:S(2)}, u32[]{:S(2)}) collective-permute-start(bf16[1,192,768]{2,1,0:T(8,128)(2,1)S(1)} %get-tuple-element.215), channel_id=1, source_target_pairs={{0,4},{4,0},{8,12},{12,8},{16,20},{20,16},{24,28},{28,24},{1,5},{5... | collective-permute-start | bytes 884744 | tf_op jit(solution)/shard_map/ppermute | solution.py:776
  338.8 19.7 %collective-permute-start.41 = (bf16[2,96,512]{2,1,0:T(8,128)(2,1)S(1)}, bf16[2,96,512]{2,1,0:T(8,128)(2,1)S(1)}, u32[]{:S(2)}, u32[]{:S(2)}) collective-permute-start(bf16[2,96,512]{2,1,0:T(8,128)(2,1)S(1)} %get-tuple-element.221), channel_id=1, source_target_pairs={{0,8},{4,12},{8,0},{12,4},{16,24},{20,28},{24,16},{28,20},{1,9},{5... | collective-permute-start | bytes 589832 | tf_op jit(solution)/shard_map/ppermute | solution.py:776
  341.6 20.5 %collective-permute-start.44 = (bf16[1,48,1920]{2,1,0:T(8,128)(2,1)S(1)}, bf16[1,48,1920]{2,1,0:T(8,128)(2,1)S(1)}, u32[]{:S(2)}, u32[]{:S(2)}) collective-permute-start(bf16[1,48,1920]{2,1,0:T(8,128)(2,1)S(1)} %get-tuple-element.229), channel_id=1, source_target_pairs={{0,16},{4,20},{8,24},{12,28},{16,0},{20,4},{24,8},{28,12},{1,17},{... | collective-permute-start | bytes 552968 | tf_op jit(solution)/shard_map/ppermute | solution.py:776
  358.6 6.4 %collective-permute-start.42 = (bf16[1,96,768]{2,1,0:T(8,128)(2,1)S(1)}, bf16[1,96,768]{2,1,0:T(8,128)(2,1)S(1)}, u32[]{:S(2)}, u32[]{:S(2)}) collective-permute-start(bf16[1,96,768]{2,1,0:T(8,128)(2,1)S(1)} %get-tuple-element.231), channel_id=1, source_target_pairs={{0,8},{4,12},{8,0},{12,4},{16,24},{20,28},{24,16},{28,20},{1,9},{5... | collective-permute-start | bytes 442376 | tf_op jit(solution)/shard_map/ppermute | solution.py:776
  358.8 6.1 %collective-permute-start.43 = (bf16[2,48,512]{2,1,0:T(8,128)(2,1)S(1)}, bf16[2,48,512]{2,1,0:T(8,128)(2,1)S(1)}, u32[]{:S(2)}, u32[]{:S(2)}) collective-permute-start(bf16[2,48,512]{2,1,0:T(8,128)(2,1)S(1)} %get-tuple-element.237), channel_id=1, source_target_pairs={{0,16},{4,20},{8,24},{12,28},{16,0},{20,4},{24,8},{28,12},{1,17},{... | collective-permute-start | bytes 294920 | tf_op jit(solution)/shard_map/ppermute | solution.py:776
  365.1 12.6 %collective-permute-start.48 = (bf16[1,48,1920]{2,1,0:T(8,128)(2,1)S(1)}, bf16[1,48,1920]{2,1,0:T(8,128)(2,1)S(1)}, u32[]{:S(2)}, u32[]{:S(2)}) collective-permute-start(bf16[1,48,1920]{2,1,0:T(8,128)(2,1)S(1)} %add_convert_fusion.29), channel_id=1, source_target_pairs={{0,16},{4,20},{8,24},{12,28},{16,0},{20,4},{24,8},{28,12},{1,17},{... | collective-permute-start | bytes 552968 | tf_op jit(solution)/shard_map/ppermute | solution.py:776
  367.7 10.0 %collective-permute-start.46 = (bf16[1,48,768]{2,1,0:T(8,128)(2,1)S(1)}, bf16[1,48,768]{2,1,0:T(8,128)(2,1)S(1)}, u32[]{:S(2)}, u32[]{:S(2)}) collective-permute-start(bf16[1,48,768]{2,1,0:T(8,128)(2,1)S(1)} %get-tuple-element.243), channel_id=1, source_target_pairs={{0,16},{4,20},{8,24},{12,28},{16,0},{20,4},{24,8},{28,12},{1,17},{... | collective-permute-start | bytes 221192 | tf_op jit(solution)/shard_map/ppermute | solution.py:776
  368.2 4.2 collective-permute-start.47
  377.8 10.0 %collective-permute-start.50 = (bf16[1,96,1920]{2,1,0:T(8,128)(2,1)S(1)}, bf16[1,96,1920]{2,1,0:T(8,128)(2,1)S(1)}, u32[]{:S(2)}, u32[]{:S(2)}) collective-permute-start(bf16[1,96,1920]{2,1,0:T(8,128)(2,1)S(1)} %pad_maximum_fusion.4), channel_id=1, source_target_pairs={{0,4},{4,0},{8,12},{12,8},{16,20},{20,16},{24,28},{28,24},{1,5},{5... | collective-permute-start | bytes 1105928 | tf_op jit(solution)/shard_map/ppermute | solution.py:776
  378.3 6.9 %collective-permute-start.49 = (bf16[1,48,1280]{2,1,0:T(8,128)(2,1)S(1)}, bf16[1,48,1280]{2,1,0:T(8,128)(2,1)S(1)}, u32[]{:S(2)}, u32[]{:S(2)}) collective-permute-start(bf16[1,48,1280]{2,1,0:T(8,128)(2,1)S(1)} %pad_maximum_fusion.6), channel_id=1, source_target_pairs={{0,16},{4,20},{8,24},{12,28},{16,0},{20,4},{24,8},{28,12},{1,17},{... | collective-permute-start | bytes 368648 | tf_op jit(solution)/shard_map/ppermute | solution.py:776
  387.9 6.5 %collective-permute-start.51 = (bf16[1,96,1280]{2,1,0:T(8,128)(2,1)S(1)}, bf16[1,96,1280]{2,1,0:T(8,128)(2,1)S(1)}, u32[]{:S(2)}, u32[]{:S(2)}) collective-permute-start(bf16[1,96,1280]{2,1,0:T(8,128)(2,1)S(1)} %pad_maximum_fusion.5), channel_id=1, source_target_pairs={{0,8},{4,12},{8,0},{12,4},{16,24},{20,28},{24,16},{28,20},{1,9},{5... | collective-permute-start | bytes 737288 | tf_op jit(solution)/shard_map/ppermute | solution.py:776
  394.4 11.7 %collective-permute-start.52 = (bf16[1,192,1280]{2,1,0:T(8,128)(2,1)S(1)}, bf16[1,192,1280]{2,1,0:T(8,128)(2,1)S(1)}, u32[]{:S(2)}, u32[]{:S(2)}) collective-permute-start(bf16[1,192,1280]{2,1,0:T(8,128)(2,1)S(1)} %pad_maximum_fusion.3), channel_id=1, source_target_pairs={{0,4},{4,0},{8,12},{12,8},{16,20},{20,16},{24,28},{28,24},{1,5},{5... | collective-permute-start | bytes 1474568 | tf_op jit(solution)/shard_map/ppermute | solution.py:776
  395.4 16.7 %collective-permute-start.53 = (bf16[1,96,3840]{2,1,0:T(8,128)(2,1)S(1)}, bf16[1,96,3840]{2,1,0:T(8,128)(2,1)S(1)}, u32[]{:S(2)}, u32[]{:S(2)}) collective-permute-start(bf16[1,96,3840]{2,1,0:T(8,128)(2,1)S(1)} %pad_maximum_fusion.1), channel_id=1, source_target_pairs={{0,8},{4,12},{8,0},{12,4},{16,24},{20,28},{24,16},{28,20},{1,9},{5... | collective-permute-start | bytes 2211848 | tf_op jit(solution)/shard_map/ppermute | solution.py:776
  (40 other events, 134.6 us)
